TPU v7x, 256 devices: a whole 4x4x8 slice. The times are simulated.
256 devices in a mesh: row: 8 (over y, core), col: 32 (over x, z).
Axes of the slice: x: 4, y: 4, z: 8, core: 2. Of those that a mesh axis runs over, the one named last changes fastest.
Arguments:
- charges: float32 [262144], P(('row', 'col')), may hold values from -6 to 6
- anchors: int32 [3, 262144], P(None, ('row', 'col')), may hold values from 0 to 255, as said below
- stencil_weights: float32 [64, 262144], P(None, ('row', 'col')), may hold values from -0.75 to 0.75
- kernel_spectrum: float32 [256, 256, 256], P('row', 'col'), may hold values from 1 to 200, as said below
- near_count: int32 [256], P(('row', 'col')), may hold values from 1 to 32, 4096 in all
- near_target: int32 [8192], P(('row', 'col')), may hold values from 0 to 7
- near_source: int32 [8192], P(('row', 'col')), may hold values from 0 to 71
- near_tiles: float32 [8192, 128, 128], P(('row', 'col')), may hold values from -0.5 to 0.5
Outputs:
- potential: float32 [262144], P(('row', 'col'))
Inputs may be any that keep to these rules, and one draw needn't show every extreme that they name: With p = t // 1024, r = p // 32, c = p % 32: anchors[0, t] = (r * 32 - 1 + i) mod 256 for some i in 0..30, anchors[1, t] = (c * 8 - 1 + j) mod 256 for some j in 0..6, anchors[2, t] any cell. kernel_spectrum[b, c, a] is unchanged when any one index n is replaced by (256 - n) mod 256, and positive.
All inputs are finite; a program needn't handle non-finite values. No bound on the sum of `near_count` on one device may be relied on, other than what follows from the above.
Results may differ from a plain program's by a relative error of at most 0.00005.
Values sent between devices are 32-bit elements; how exact they have to be, the bound alone decides.
No kernel may reach another device: no remote copies, remote signals or barrier semaphores. Data moves between devices by JAX's collectives and lax.ppermute only.
A program may use at most 64 MiB of HBM per device.

v0:
```python
import jax
import jax.numpy as jnp
import ml_dtypes
import numpy as np
from jax import lax
from jax.experimental import pallas as pl
from jax.experimental.pallas import tpu as pltpu
from jax.sharding import PartitionSpec as P

G = 256
ROWS = 8
COLS = 32
CELLS_A = 32
CELLS_B = 8
TRI = 1024
LINES_B = 10
MAIN = LINES_B * CELLS_A
LINES = 384
SPREAD = MAIN + 8 * LINES_B
LANES = 128
TILES = TRI // LANES
F32 = jnp.float32
BF16 = jnp.bfloat16
BOTH = ("row", "col")
PARAMS = pltpu.CompilerParams(vmem_limit_bytes=48 * 1024 * 1024)


def split_table(table):
    high = table.astype(np.float32).astype(ml_dtypes.bfloat16)
    low = (table - high.astype(np.float64)).astype(np.float32).astype(ml_dtypes.bfloat16)
    return np.stack([high, low])


def cas(first, second):
    angle = (np.outer(first, second) % G) * (2.0 * np.pi / G)
    return np.cos(angle) + np.sin(angle)


def tables():
    steps = np.arange(G)
    device = np.arange(ROWS * COLS)
    plane = CELLS_B * (device % COLS) + device // COLS
    along_a = (np.arange(G) - 1) % G
    order = np.arange(LINES_B * COLS)
    along_b = (CELLS_B * (order % COLS) - 1 + order // COLS) % G
    lines = cas(plane, steps)
    first = cas(along_a, steps)
    second = cas(steps, along_b)
    return split_table(lines), split_table(first), split_table(second), split_table(second.T)


def halves(value):
    high = value.astype(BF16)
    low = (value - high.astype(F32)).astype(BF16)
    return high, low


def dot(left, right, dims=((1,), (0,))):
    return lax.dot_general(left, right, (dims, ((), ())), preferred_element_type=F32)


def dot_split(left, right, dims=((1,), (0,))):
    left_high, left_low = left
    right_high, right_low = right
    cross = dot(left_high, right_low, dims) + dot(left_low, right_high, dims)
    return dot(left_high, right_high, dims) + cross


def extra_row(line):
    return MAIN + 2 * (line // 2) + 32 * (line % 2)


def onehot(anchors_ref):
    cells = lax.broadcasted_iota(jnp.int32, (G, TRI), 0)
    matched = cells == anchors_ref[2:3, :]
    return jnp.where(matched, 1.0, 0.0).astype(BF16)


def local_place(anchors_ref, at):
    first = (anchors_ref[0:1, at] - (lax.axis_index("row") * CELLS_A - 1)) & (G - 1)
    second = (anchors_ref[1:2, at] - (lax.axis_index("col") * CELLS_B - 1)) & (G - 1)
    first = jnp.broadcast_to(first, (8, LANES))
    second = jnp.broadcast_to(second, (8, LANES))
    relative = lax.broadcasted_iota(jnp.int32, (8, LANES), 0) - (first & 7)
    near_masks = [relative == i for i in range(4)]
    next_masks = [relative == i - 8 for i in range(1, 4)]
    group = first >> 3
    groups = [group == g for g in range(4)]
    bits = [(second & bit) != 0 for bit in (1, 2, 4)]
    return near_masks, next_masks, groups, bits


def two_rows(rows, near_masks, next_masks):
    near = jnp.zeros((8, LANES), F32)
    after = jnp.zeros((8, LANES), F32)
    for i in range(4):
        near = jnp.where(near_masks[i], rows[i], near)
    for i in range(1, 4):
        after = jnp.where(next_masks[i - 1], rows[i], after)
    return near, after


def deposit_kernel(charges_ref, anchors_ref, weights_ref, table_ref, out_ref, scaled, spread, lines):
    scaled[...] = weights_ref[...] * charges_ref[...]
    zero = jnp.zeros((8, LANES), F32)

    def tile(step, carry):
        at = pl.ds(pl.multiple_of(step * LANES, LANES), LANES)
        near_masks, next_masks, groups, bits = local_place(anchors_ref, at)
        for k in range(4):
            blocks = []
            for j in range(4):
                rows = [
                    jnp.broadcast_to(scaled[16 * i + 4 * j + k, at][None, :], (8, LANES))
                    for i in range(4)
                ]
                blocks.append(two_rows(rows, near_masks, next_masks))
            for mask, shift, count in zip(bits, (1, 2, 4), (5, 7, 10)):
                wider = []
                for line in range(count):
                    low = blocks[line] if line < len(blocks) else (zero, zero)
                    high = blocks[line - shift] if line >= shift else (zero, zero)
                    wider.append(tuple(jnp.where(mask, h, l) for h, l in zip(high, low)))
                blocks = wider
            extras = []
            for line in range(LINES_B):
                near, after = blocks[line]
                pieces = []
                for v in range(5):
                    piece = jnp.where(groups[v], near, zero) if v < 4 else zero
                    if v > 0:
                        piece = jnp.where(groups[v - 1], after, piece)
                    pieces.append(piece)
                high, low = halves(jnp.concatenate(pieces[:4], axis=0))
                spread[0, k, pl.ds(line * 32, 32), at] = high
                spread[1, k, pl.ds(line * 32, 32), at] = low
                extras.append(pieces[4])
            high, low = halves(jnp.concatenate(extras, axis=0))
            spread[0, k, pl.ds(MAIN, 8 * LINES_B), at] = high
            spread[1, k, pl.ds(MAIN, 8 * LINES_B), at] = low
        return carry

    lax.fori_loop(0, TILES, tile, 0)
    hot = onehot(anchors_ref)
    total = None
    for k in range(4):
        placed = dot(spread[0, k], hot, ((1,), (1,))) + dot(spread[1, k], hot, ((1,), (1,)))
        placed = pltpu.roll(placed, k, 1) if k else placed
        total = placed if total is None else total + placed
    lines[pl.ds(0, MAIN), :] = total[:MAIN]
    lines[pl.ds(MAIN, LINES - MAIN), :] = jnp.zeros((LINES - MAIN, G), F32)
    for line in range(LINES_B):
        lines[pl.ds(extra_row(line), 2), :] = total[MAIN + 8 * line : MAIN + 8 * line + 2]
    out_ref[...] = dot_split((table_ref[0], table_ref[1]), halves(lines[...]), ((1,), (1,)))


def lane_roll(value, shift):
    shift = shift % LANES
    return pltpu.roll(value, shift, 1) if shift else value


def plane_kernel(tiles_ref, spectrum_ref, first_ref, second_ref, flipped_ref, out_ref, whole):
    lane = lax.broadcasted_iota(jnp.int32, (32, LANES), 1)
    slots = [(lane >> 5) == s for s in range(4)]
    rim = (lane & 31) < 2
    sides = [rim & (lane < 64), rim & (lane >= 64)]
    pieces = []
    for r in range(ROWS):
        main = [tiles_ref[pl.ds(32 * r, 32), pl.ds(LANES * v, LANES)] for v in range(3)]
        extra = tiles_ref[pl.ds(32 * ((r - 1) % ROWS), 32), pl.ds(2 * LANES, LANES)]
        for p in range(5):
            side = p % 2
            moved = lane_roll(extra, 64 * side - 64 - 2 * p)
            main[p // 2] = main[p // 2] + jnp.where(sides[side], moved, 0.0)
        pieces.append(main)
    for line in range(LINES_B):
        for w in range(2):
            joined = None
            for s in range(4):
                moved = lane_roll(pieces[4 * w + s][line // 4], 32 * (s - line % 4))
                joined = moved if joined is None else jnp.where(slots[s], moved, joined)
            whole[pl.ds(32 * line, 32), pl.ds(LANES * w, LANES)] = joined
    first = (first_ref[0], first_ref[1])
    half = dot_split(halves(whole[...]), first)
    image = dot_split((second_ref[0], second_ref[1]), halves(half))
    image = image * (spectrum_ref[...] * (1.0 / (G * G * G)))
    half = dot_split((flipped_ref[0], flipped_ref[1]), halves(image))
    whole[...] = dot_split(halves(half), first, ((1,), (1,)))
    results = []
    for r in range(ROWS):
        main = []
        for v in range(3):
            joined = None
            for s in range(4 if v < 2 else 2):
                line = 4 * v + s
                block = whole[pl.ds(32 * line, 32), pl.ds(LANES * (r // 4), LANES)]
                moved = lane_roll(block, 32 * (s - r % 4))
                joined = moved if joined is None else jnp.where(slots[s], moved, joined)
            main.append(joined)
        results.append(main)
    for r in range(ROWS):
        source = results[(r + 1) % ROWS]
        last = jnp.where(lane < 64, results[r][2], 0.0)
        for p in range(5):
            side = p % 2
            moved = lane_roll(source[p // 2], 64 + 2 * p - 64 * side)
            here = ((lane & 31) >> 1 == p) & (lane >= 64)
            last = jnp.where(here, moved, last)
        out_ref[pl.ds(32 * r, 32), pl.ds(0, LANES)] = results[r][0]
        out_ref[pl.ds(32 * r, 32), pl.ds(LANES, LANES)] = results[r][1]
        out_ref[pl.ds(32 * r, 32), pl.ds(2 * LANES, LANES)] = last


def gather_kernel(field_ref, anchors_ref, weights_ref, table_ref, near_ref, out_ref, lines, picked):
    turned = halves(field_ref[...].T)
    field = dot_split(turned, (table_ref[0], table_ref[1]))
    lines[pl.ds(0, MAIN), :] = field[:MAIN]
    lines[pl.ds(MAIN, 8 * LINES_B), :] = jnp.zeros((8 * LINES_B, G), F32)
    for line in range(LINES_B):
        row = extra_row(line)
        lines[pl.ds(MAIN + 8 * line, 2), :] = field[row : row + 2]
    hot = onehot(anchors_ref)
    for k in range(4):
        moved = lines[...]
        moved = pltpu.roll(moved, G - k, 1) if k else moved
        high, low = halves(moved)
        picked[k] = dot(high, hot) + dot(low, hot)

    def tile(step, carry):
        at = pl.ds(pl.multiple_of(step * LANES, LANES), LANES)
        near_masks, next_masks, groups, bits = local_place(anchors_ref, at)
        total = jnp.zeros((8, LANES), F32)
        for k in range(4):
            blocks = []
            for line in range(LINES_B):
                rows = [picked[k, pl.ds(32 * line + 8 * v, 8), at] for v in range(4)]
                rows.append(picked[k, pl.ds(MAIN + 8 * line, 8), at])
                pair = []
                for skip in range(2):
                    chosen = rows[skip]
                    for g in range(1, 4):
                        chosen = jnp.where(groups[g], rows[g + skip], chosen)
                    pair.append(chosen)
                blocks.append(pair)
            for mask, shift, count in zip(bits[::-1], (4, 2, 1), (7, 5, 4)):
                fewer = []
                for line in range(count):
                    low = blocks[line]
                    if line + shift < len(blocks):
                        high = blocks[line + shift]
                        fewer.append([jnp.where(mask, h, l) for h, l in zip(high, low)])
                    else:
                        fewer.append(low)
                blocks = fewer
            for j in range(4):
                rows = [
                    jnp.broadcast_to(weights_ref[16 * i + 4 * j + k, at][None, :], (8, LANES))
                    for i in range(4)
                ]
                near, after = two_rows(rows, near_masks, next_masks)
                total = total + (near * blocks[j][0] + after * blocks[j][1])
        out_ref[:, at] = jnp.sum(total, axis=0, keepdims=True) + near_ref[:, at]
        return carry

    lax.fori_loop(0, TILES, tile, 0)


def near_kernel(count_ref, target_ref, source_ref, charges_ref, tiles_ref, out_ref, beside, total, sem):
    step = pl.program_id(0)
    per_step, size = tiles_ref.shape[0], tiles_ref.shape[1]

    @pl.when(step == 0)
    def _():
        row, col = lax.axis_index("row"), lax.axis_index("col")
        copies = []
        for n in range(9):
            patch = ((row + n // 3 + ROWS - 1) % ROWS) * COLS + (col + n % 3 + COLS - 1) % COLS
            copies.append(
                pltpu.make_async_copy(
                    charges_ref.at[pl.ds(patch * 8, 8)], beside.at[pl.ds(8 * n, 8)], sem.at[n]
                )
            )
        for copy in copies:
            copy.start()
        total[...] = jnp.zeros_like(total)
        for copy in copies:
            copy.wait()

    def slot(u, carry):
        place = step * per_step + u
        rows = pl.ds(pl.multiple_of(target_ref[place] * size, size), size)
        source = beside[pl.ds(source_ref[place], 1), :]
        total[rows, :] = total[rows, :] + tiles_ref[u] * source
        return carry

    lax.fori_loop(0, jnp.clip(count_ref[0] - step * per_step, 0, per_step), slot, 0)

    @pl.when(step == pl.num_programs(0) - 1)
    def _():
        ones = jnp.ones((8, size), BF16)
        rest = total[...]
        result = jnp.zeros((8, TRI), F32)
        for _ in range(3):
            part = rest.astype(BF16)
            result = result + dot(ones, part, ((1,), (1,)))
            rest = rest - part.astype(F32)
        out_ref[...] = result[0:1]


def near_field(charges, near_count, near_target, near_source, near_tiles):
    slots, size, _ = near_tiles.shape
    everyone = lax.all_gather(charges.reshape(8, size), BOTH, axis=0, tiled=True)
    per_step = 8
    return pl.pallas_call(
        near_kernel,
        grid=(slots // per_step,),
        in_specs=[
            pl.BlockSpec(memory_space=pltpu.SMEM),
            pl.BlockSpec(memory_space=pltpu.SMEM),
            pl.BlockSpec(memory_space=pltpu.SMEM),
            pl.BlockSpec(memory_space=pl.ANY),
            pl.BlockSpec((per_step, size, size), lambda step: (step, 0, 0)),
        ],
        out_specs=pl.BlockSpec((1, TRI), lambda step: (0, 0)),
        out_shape=jax.ShapeDtypeStruct((1, TRI), F32),
        scratch_shapes=[
            pltpu.VMEM((72, size), F32),
            pltpu.VMEM((TRI, size), F32),
            pltpu.SemaphoreType.DMA((9,)),
        ],
        compiler_params=PARAMS,
        name="near",
    )(near_count, near_target, near_source, everyone, near_tiles)


def exchange(values):
    return lax.all_to_all(values, BOTH, split_axis=0, concat_axis=0, tiled=True)


def local(
    charges,
    anchors,
    stencil_weights,
    kernel_spectrum,
    near_count,
    near_target,
    near_source,
    near_tiles,
):
    lines_table, first, second, flipped = [jnp.asarray(table) for table in tables()]
    spectrum = lax.all_gather(kernel_spectrum, "row", axis=0, tiled=True)
    spectrum = lax.dynamic_index_in_dim(spectrum, lax.axis_index("row"), axis=1, keepdims=False)
    deposited = pl.pallas_call(
        deposit_kernel,
        out_shape=jax.ShapeDtypeStruct((G, LINES), F32),
        scratch_shapes=[
            pltpu.VMEM((64, TRI), F32),
            pltpu.VMEM((2, 4, SPREAD, TRI), BF16),
            pltpu.VMEM((LINES, G), F32),
        ],
        compiler_params=PARAMS,
        name="deposit",
    )(charges.reshape(1, TRI), anchors, stencil_weights, lines_table)
    received = exchange(deposited)
    near = near_field(charges, near_count, near_target, near_source, near_tiles)
    handed = pl.pallas_call(
        plane_kernel,
        out_shape=jax.ShapeDtypeStruct((G, LINES), F32),
        scratch_shapes=[pltpu.VMEM((MAIN, G), F32)],
        compiler_params=PARAMS,
        name="plane",
    )(received, spectrum, first, second, flipped)
    field = exchange(handed)
    result = pl.pallas_call(
        gather_kernel,
        out_shape=jax.ShapeDtypeStruct((1, TRI), F32),
        scratch_shapes=[
            pltpu.VMEM((SPREAD, G), F32),
            pltpu.VMEM((4, SPREAD, TRI), F32),
        ],
        compiler_params=PARAMS,
        name="gather",
    )(field, anchors, stencil_weights, lines_table, near)
    return result.reshape(TRI)


def solution(mesh):
    return jax.shard_map(
        local,
        mesh=mesh,
        in_specs=(
            P(("row", "col")),
            P(None, ("row", "col")),
            P(None, ("row", "col")),
            P("row", "col", None),
            P(("row", "col")),
            P(("row", "col")),
            P(("row", "col")),
            P(("row", "col"), None, None),
        ),
        out_specs=P(("row", "col")),
        check_vma=False,
    )
```

profile of v0, /device:TPU:1, one launch (start us, length us, event | category | flops | bytes accessed | tf_op | source)
XLA Modules:
  0.0 163.2 jit_solution(17503177397303912329)
XLA Ops:
  6.5 0.0 all-gather.3.cloned.1.call-start
  6.5 0.0 copy-start.6
  6.5 0.0 copy-start.7
  6.5 1.8 %copy.15 = f32[32,8,256]{2,0,1:T(8,128)} copy(f32[32,8,256]{2,1,0:T(8,128)} %param.15) | data formatting | bytes 524288 | tf_op args[3]
  8.4 0.0 all-gather.3.cloned.1.call-update
  8.4 0.0 all-gather.5.cloned.1.call-start
  8.4 0.7 all-gather.5.cloned.1.call-update
  9.1 0.0 copy-start.2
  9.1 0.9 copy-done.2
  10.1 0.0 copy-start.4
  10.1 0.9 copy-done.4
  11.0 0.0 copy-start.9
  11.0 0.7 copy-done.9
  11.8 0.0 copy-start.11
  11.8 0.7 copy-done.11
  12.4 0.0 copy-start.8
  12.4 4.6 %deposit.1 = f32[256,384]{1,0:T(8,128)S(1)} custom-call(f32[1,1024]{1,0:T(1,128)S(1)} %bitcast.18, s32[3,1024]{1,0:T(4,128)S(1)} %copy-done.9, f32[64,1024]{1,0:T(8,128)S(1)} %copy-done.2, bf16[2,256,256]{2,1,0:T(8,128)(2,1)S(1)} %copy-done.4), custom_call_target="tpu_custom_call" | custom-call | tf_op jit(solution)/shard_map/deposit/pallas_call | solution.py:353
  17.0 1.1 copy.14
  18.2 15.7 %all-to-all-start = ((f32[256,1,384]{2,1,0:T(1,128)}), f32[256,1,384]{2,1,0:T(1,128)S(1)}, u32[]{:S(2)}, u32[]{:S(2)}) async-start(f32[256,1,384]{2,1,0:T(1,128)} %copy.14), calls=%async_computation | async-start | bytes 786432 | tf_op jit(solution)/shard_map/all_to_all | solution.py:337
  33.9 18.4 %all-to-all-done = f32[256,1,384]{2,1,0:T(1,128)S(1)} async-done(((f32[256,1,384]{2,1,0:T(1,128)}), f32[256,1,384]{2,1,0:T(1,128)S(1)}, u32[]{:S(2)}, u32[]{:S(2)}) %all-to-all-start) | async-done | bytes 393248 | tf_op jit(solution)/shard_map/all_to_all | solution.py:337
  52.3 0.0 copy-start
  52.3 0.0 copy-start.12
  52.3 0.0 copy-start.13
  52.3 0.0 all-gather.3.cloned.1.call-done
  52.3 1.1 dynamic-slice_bitcast_fusion.spectrum_ref
  53.5 0.0 copy-done.6
  53.5 0.0 copy-done.7
  53.5 0.0 copy-done.8
  53.5 2.3 %plane.1 = f32[256,384]{1,0:T(8,128)S(1)} custom-call(f32[256,384]{1,0:T(8,128)S(1)} %bitcast.15, f32[256,256]{1,0:T(8,128)S(1)} %dynamic-slice_bitcast_fusion.spectrum_ref, bf16[2,256,256]{2,1,0:T(8,128)(2,1)S(1)} %copy-done.8, bf16[2,256,320]{2,1,0:T(8,128)(2,1)S(1)} %copy-done.6, bf16[2,320,256]{2,1,0:T(8,128)(2,1)S(1)} %copy-done.7), custom_call_target="tpu_custom_call" | custom-call | tf_op jit(solution)/shard_map/plane/pallas_call | solution.py:366
  55.8 1.2 copy.16
  57.0 0.0 copy-start.3
  57.0 0.0 copy-start.5
  57.0 0.0 copy-start.10
  57.0 5.6 %all-to-all-start.1 = ((f32[256,1,384]{2,1,0:T(1,128)}), f32[256,1,384]{2,1,0:T(1,128)S(1)}, u32[]{:S(2)}, u32[]{:S(2)}) async-start(f32[256,1,384]{2,1,0:T(1,128)} %copy.16), calls=%async_computation.1 | async-start | bytes 786432 | tf_op jit(solution)/shard_map/all_to_all | solution.py:337
  63.2 86.5 %all-gather.5.cloned.1.call-done.charges_ref = f32[2048,128]{1,0:T(8,128)} async-done(((f32[8,128]{1,0:T(8,128)}), f32[2048,128]{1,0:T(8,128)}) %all-gather.5.cloned.1.call-update) | async-done | bytes 1048592 | tf_op jit(solution)/shard_map/all_gather | solution.py:312
  149.7 0.0 copy-done
  149.7 0.0 copy-done.12
  149.7 0.0 copy-done.13
  149.7 0.0 copy-start.1
  149.7 1.2 copy-done.1
  151.0 1.3 near.1.near_ref
  152.3 0.0 all-to-all-done.1
  152.3 0.0 copy-done.3
  152.3 0.0 copy-done.5
  152.3 0.0 copy-done.10
  152.4 4.0 %gather.1 = f32[1,1024]{1,0:T(1,128)} custom-call(f32[256,384]{1,0:T(8,128)S(1)} %bitcast.13, s32[3,1024]{1,0:T(4,128)S(1)} %copy-done.10, f32[64,1024]{1,0:T(8,128)S(1)} %copy-done.3, bf16[2,256,256]{2,1,0:T(8,128)(2,1)S(1)} %copy-done.5, f32[1,1024]{1,0:T(1,128)S(1)} %near.1.near_ref), custom_call_target="tpu_custom_call" | custom-call | tf_op jit(solution)/shard_map/gather/pallas_call | solution.py:374
  (2 shorter events, 0.1 us)
Async XLA Ops:
  6.5 45.8 %all-gather.3.cloned.1.call-start = ((), (), s32[]{:S(2)}) async-start(), calls=%async_computation.2 | async-start | bytes 2359296 | tf_op jit(solution)/shard_map/all_gather | solution.py:351
  6.5 46.9 %copy-start.6 = (bf16[2,256,320]{2,1,0:T(8,128)(2,1)S(1)}, bf16[2,256,320]{2,1,0:T(8,128)(2,1)}, u32[]{:S(2)}) copy-start(bf16[2,256,320]{2,1,0:T(8,128)(2,1)} %constant.22.clone.second_ref) | copy-start | bytes 983044
  6.5 46.9 %copy-start.7 = (bf16[2,320,256]{2,1,0:T(8,128)(2,1)S(1)}, bf16[2,320,256]{2,1,0:T(8,128)(2,1)}, u32[]{:S(2)}) copy-start(bf16[2,320,256]{2,1,0:T(8,128)(2,1)} %constant.23.clone.flipped_ref) | copy-start | bytes 983044
  8.4 141.3 %all-gather.5.cloned.1.call-start = ((), (), s32[]{:S(2)}) async-start(), calls=%async_computation.3 | async-start | bytes 1052672 | tf_op jit(solution)/shard_map/all_gather | solution.py:312
  9.1 1.0 copy-start.2
  10.1 0.9 copy-start.4
  11.0 0.7 copy-start.9
  11.8 0.7 copy-start.11
  12.4 41.0 %copy-start.8 = (bf16[2,256,256]{2,1,0:T(8,128)(2,1)S(1)}, bf16[2,256,256]{2,1,0:T(8,128)(2,1)}, u32[]{:S(2)}) copy-start(bf16[2,256,256]{2,1,0:T(8,128)(2,1)} %constant.21.clone.first_ref) | copy-start | bytes 786436
  18.2 34.1 %all-to-all-start = ((f32[256,1,384]{2,1,0:T(1,128)}), f32[256,1,384]{2,1,0:T(1,128)S(1)}, u32[]{:S(2)}, u32[]{:S(2)}) async-start(f32[256,1,384]{2,1,0:T(1,128)} %copy.14), calls=%async_computation | async-start | bytes 786432 | tf_op jit(solution)/shard_map/all_to_all | solution.py:337
  52.3 97.4 %copy-start = (f32[32,128,128]{2,1,0:T(8,128)S(1)}, f32[32,128,128]{2,1,0:T(8,128)}, u32[]{:S(2)}) copy-start(f32[32,128,128]{2,1,0:T(8,128)} %tiles_ref.1) | copy-start | bytes 6291460
  52.3 97.4 %copy-start.12 = (s32[32]{0:T(128)S(1)}, s32[32]{0:T(128)}, u32[]{:S(2)}) copy-start(s32[32]{0:T(128)} %target_ref.1) | copy-start | bytes 388
  52.3 97.4 %copy-start.13 = (s32[32]{0:T(128)S(1)}, s32[32]{0:T(128)}, u32[]{:S(2)}) copy-start(s32[32]{0:T(128)} %source_ref.1) | copy-start | bytes 388
  57.0 95.4 %copy-start.3 = (f32[64,1024]{1,0:T(8,128)S(1)}, f32[64,1024]{1,0:T(8,128)}, u32[]{:S(2)}) copy-start(f32[64,1024]{1,0:T(8,128)} %weights_ref.3) | copy-start | bytes 786436
  57.0 95.4 %copy-start.5 = (bf16[2,256,256]{2,1,0:T(8,128)(2,1)S(1)}, bf16[2,256,256]{2,1,0:T(8,128)(2,1)}, u32[]{:S(2)}) copy-start(bf16[2,256,256]{2,1,0:T(8,128)(2,1)} %constant.20.clone.table_ref) | copy-start | bytes 786436
  57.0 95.4 %copy-start.10 = (s32[3,1024]{1,0:T(4,128)S(1)}, s32[3,1024]{1,0:T(4,128)}, u32[]{:S(2)}) copy-start(s32[3,1024]{1,0:T(4,128)} %anchors_ref.3) | copy-start | bytes 36868
  57.0 95.3 %all-to-all-start.1 = ((f32[256,1,384]{2,1,0:T(1,128)}), f32[256,1,384]{2,1,0:T(1,128)S(1)}, u32[]{:S(2)}, u32[]{:S(2)}) async-start(f32[256,1,384]{2,1,0:T(1,128)} %copy.16), calls=%async_computation.1 | async-start | bytes 786432 | tf_op jit(solution)/shard_map/all_to_all | solution.py:337
  149.7 1.2 copy-start.1
Sparse Core Ops, SparseCore 0:
  9.2 32.0 all-gather.2
  45.1 104.6 all-gather.4
where the time goes:
time: 164 us; the launch traced here: 163 us
  waiting for transfers between devices  106 us (65%)
  starting transfers between devices  21.3 us (13%)
  between operations  14.2 us (9%)
  Pallas kernels  12.3 us (8%)
  local copies, waits for them, and re-layouts  9.84 us (6%)
    all_gather x1, waiting for transfers between devices, near_field(): lax.all_gather(charges.reshape(8, size), BOTH, axis=0, tiled=True)  86.5 us
    all_to_all x2, starting transfers between devices, exchange(): return lax.all_to_all(values, BOTH, split_axis=0, concat_axis=0, tiled=True)  21.2 us
    all_to_all x2, waiting for transfers between devices, exchange(): return lax.all_to_all(values, BOTH, split_axis=0, concat_axis=0, tiled=True)  18.4 us
    unnamed x31, local copies, waits for them, and re-layouts  6.43 us
    pallas_call x1, Pallas kernels, local(): pl.pallas_call(deposit_kernel, out_shape=jax.ShapeDtypeStruct((G, LINES),...  4.59 us
    pallas_call x1, Pallas kernels, local(): pl.pallas_call(gather_kernel, out_shape=jax.ShapeDtypeStruct((1, TRI), F3...  4.05 us
  transfers between devices with their start and end apart: 4, of which 2 were waited for; matrix products, arithmetic and copies ran while one was open for 2% of the time, Pallas kernels for 5%

commit v1 on v0

--- a/solution.py
+++ b/solution.py
@@ -22,6 +22,8 @@
 F32 = jnp.float32
 BF16 = jnp.bfloat16
 BOTH = ("row", "col")
+KEPT = CELLS_A // 2 + 1
+SENT = 2 * KEPT
 PARAMS = pltpu.CompilerParams(vmem_limit_bytes=48 * 1024 * 1024)
 
 
@@ -43,16 +45,32 @@
     along_a = (np.arange(G) - 1) % G
     order = np.arange(LINES_B * COLS)
     along_b = (CELLS_B * (order % COLS) - 1 + order // COLS) % G
+    folded = np.minimum(steps, G - steps)
+    block, inside = folded // CELLS_A, folded % CELLS_A
+    mirrored = inside >= KEPT
+    owner = np.where(mirrored, ROWS - 1 - block, block)
+    inside = np.where(mirrored, CELLS_A - inside, inside)
+    chosen = np.zeros((2, G, ROWS * SENT), ml_dtypes.bfloat16)
+    for half in range(2):
+        chosen[half, steps, owner * SENT + half * KEPT + inside] = 1.0
     lines = cas(plane, steps)
     first = cas(along_a, steps)
     second = cas(steps, along_b)
-    return split_table(lines), split_table(first), split_table(second), split_table(second.T)
+    return split_table(lines), split_table(first), split_table(second), split_table(second.T), chosen
 
 
 def halves(value):
     high = value.astype(BF16)
     low = (value - high.astype(F32)).astype(BF16)
     return high, low
+
+
+def thirds(value):
+    parts = []
+    for _ in range(3):
+        parts.append(value.astype(BF16))
+        value = value - parts[-1].astype(F32)
+    return parts
 
 
 def dot(left, right, dims=((1,), (0,))):
@@ -100,7 +118,23 @@
     return near, after
 
 
-def deposit_kernel(charges_ref, anchors_ref, weights_ref, table_ref, out_ref, scaled, spread, lines):
+def deposit_kernel(
+    charges_hbm, anchors_hbm, weights_hbm, table_hbm, spectrum_hbm, out_ref, sent_ref,
+    charges_ref, anchors_ref, weights_ref, table_ref, spectrum_ref, scaled, spread, lines, sem,
+):
+    pairs = (
+        (weights_hbm, weights_ref),
+        (anchors_hbm, anchors_ref),
+        (charges_hbm, charges_ref),
+        (spectrum_hbm.at[pl.ds(0, CELLS_B * KEPT), pl.ds(0, LANES)], spectrum_ref.at[0]),
+        (spectrum_hbm.at[pl.ds(0, CELLS_B * KEPT), pl.ds(LANES, LANES)], spectrum_ref.at[1]),
+        (table_hbm, table_ref),
+    )
+    copies = [pltpu.make_async_copy(a, b, sem.at[n]) for n, (a, b) in enumerate(pairs)]
+    for copy in copies:
+        copy.start()
+    for copy in copies[:3]:
+        copy.wait()
     scaled[...] = weights_ref[...] * charges_ref[...]
     zero = jnp.zeros((8, LANES), F32)
 
@@ -141,6 +175,12 @@
         return carry
 
     lax.fori_loop(0, TILES, tile, 0)
+    for copy in copies[3:]:
+        copy.wait()
+    for c in range(CELLS_B):
+        for half in range(2):
+            rows = spectrum_ref[half, pl.ds(c, KEPT, stride=CELLS_B), :]
+            sent_ref[pl.ds(c * SENT + half * KEPT, KEPT), :] = rows
     hot = onehot(anchors_ref)
     total = None
     for k in range(4):
@@ -151,7 +191,9 @@
     lines[pl.ds(MAIN, LINES - MAIN), :] = jnp.zeros((LINES - MAIN, G), F32)
     for line in range(LINES_B):
         lines[pl.ds(extra_row(line), 2), :] = total[MAIN + 8 * line : MAIN + 8 * line + 2]
-    out_ref[...] = dot_split((table_ref[0], table_ref[1]), halves(lines[...]), ((1,), (1,)))
+    result = dot_split((table_ref[0], table_ref[1]), halves(lines[...]), ((1,), (1,)))
+    for v in range(3):
+        out_ref[pl.ds(v, G, stride=3), :] = result[:, LANES * v : LANES * (v + 1)]
 
 
 def lane_roll(value, shift):
@@ -159,15 +201,15 @@
     return pltpu.roll(value, shift, 1) if shift else value
 
 
-def plane_kernel(tiles_ref, spectrum_ref, first_ref, second_ref, flipped_ref, out_ref, whole):
+def plane_kernel(tiles_ref, spectrum_ref, chosen_ref, first_ref, second_ref, flipped_ref, out_ref, whole):
     lane = lax.broadcasted_iota(jnp.int32, (32, LANES), 1)
     slots = [(lane >> 5) == s for s in range(4)]
     rim = (lane & 31) < 2
     sides = [rim & (lane < 64), rim & (lane >= 64)]
     pieces = []
     for r in range(ROWS):
-        main = [tiles_ref[pl.ds(32 * r, 32), pl.ds(LANES * v, LANES)] for v in range(3)]
-        extra = tiles_ref[pl.ds(32 * ((r - 1) % ROWS), 32), pl.ds(2 * LANES, LANES)]
+        main = [tiles_ref[pl.ds(96 * r + v, 32, stride=3), :] for v in range(3)]
+        extra = tiles_ref[pl.ds(96 * ((r - 1) % ROWS) + 2, 32, stride=3), :]
         for p in range(5):
             side = p % 2
             moved = lane_roll(extra, 64 * side - 64 - 2 * p)
@@ -180,10 +222,15 @@
                 moved = lane_roll(pieces[4 * w + s][line // 4], 32 * (s - line % 4))
                 joined = moved if joined is None else jnp.where(slots[s], moved, joined)
             whole[pl.ds(32 * line, 32), pl.ds(LANES * w, LANES)] = joined
+    scale = 1.0 / (G * G * G)
+    parts = thirds(spectrum_ref[...])
+    spectrum = jnp.concatenate(
+        [sum(dot(chosen_ref[half], part) for part in parts) * scale for half in range(2)], axis=1
+    )
     first = (first_ref[0], first_ref[1])
     half = dot_split(halves(whole[...]), first)
     image = dot_split((second_ref[0], second_ref[1]), halves(half))
-    image = image * (spectrum_ref[...] * (1.0 / (G * G * G)))
+    image = image * spectrum
     half = dot_split((flipped_ref[0], flipped_ref[1]), halves(image))
     whole[...] = dot_split(halves(half), first, ((1,), (1,)))
     results = []
@@ -206,13 +253,13 @@
             moved = lane_roll(source[p // 2], 64 + 2 * p - 64 * side)
             here = ((lane & 31) >> 1 == p) & (lane >= 64)
             last = jnp.where(here, moved, last)
-        out_ref[pl.ds(32 * r, 32), pl.ds(0, LANES)] = results[r][0]
-        out_ref[pl.ds(32 * r, 32), pl.ds(LANES, LANES)] = results[r][1]
-        out_ref[pl.ds(32 * r, 32), pl.ds(2 * LANES, LANES)] = last
+        for v, value in enumerate((results[r][0], results[r][1], last)):
+            out_ref[pl.ds(96 * r + v, 32, stride=3), :] = value
 
 
 def gather_kernel(field_ref, anchors_ref, weights_ref, table_ref, near_ref, out_ref, lines, picked):
-    turned = halves(field_ref[...].T)
+    turned = [field_ref[pl.ds(v, G, stride=3), :].T for v in range(3)]
+    turned = halves(jnp.concatenate(turned, axis=0))
     field = dot_split(turned, (table_ref[0], table_ref[1]))
     lines[pl.ds(0, MAIN), :] = field[:MAIN]
     lines[pl.ds(MAIN, 8 * LINES_B), :] = jnp.zeros((8 * LINES_B, G), F32)
@@ -265,31 +312,18 @@
     lax.fori_loop(0, TILES, tile, 0)
 
 
-def near_kernel(count_ref, target_ref, source_ref, charges_ref, tiles_ref, out_ref, beside, total, sem):
+def near_kernel(count_ref, target_ref, source_ref, charges_ref, tiles_ref, out_ref, total):
     step = pl.program_id(0)
     per_step, size = tiles_ref.shape[0], tiles_ref.shape[1]
 
     @pl.when(step == 0)
     def _():
-        row, col = lax.axis_index("row"), lax.axis_index("col")
-        copies = []
-        for n in range(9):
-            patch = ((row + n // 3 + ROWS - 1) % ROWS) * COLS + (col + n % 3 + COLS - 1) % COLS
-            copies.append(
-                pltpu.make_async_copy(
-                    charges_ref.at[pl.ds(patch * 8, 8)], beside.at[pl.ds(8 * n, 8)], sem.at[n]
-                )
-            )
-        for copy in copies:
-            copy.start()
         total[...] = jnp.zeros_like(total)
-        for copy in copies:
-            copy.wait()
 
     def slot(u, carry):
         place = step * per_step + u
         rows = pl.ds(pl.multiple_of(target_ref[place] * size, size), size)
-        source = beside[pl.ds(source_ref[place], 1), :]
+        source = charges_ref[pl.ds(source_ref[place], 1), :]
         total[rows, :] = total[rows, :] + tiles_ref[u] * source
         return carry
 
@@ -298,43 +332,47 @@
     @pl.when(step == pl.num_programs(0) - 1)
     def _():
         ones = jnp.ones((8, size), BF16)
-        rest = total[...]
-        result = jnp.zeros((8, TRI), F32)
-        for _ in range(3):
-            part = rest.astype(BF16)
-            result = result + dot(ones, part, ((1,), (1,)))
-            rest = rest - part.astype(F32)
+        result = sum(dot(ones, part, ((1,), (1,))) for part in thirds(total[...]))
         out_ref[...] = result[0:1]
+
+
+def with_sides(value, axis):
+    size = lax.axis_size(axis)
+    up = [(i, (i + 1) % size) for i in range(size)]
+    down = [(j, i) for i, j in up]
+    before = lax.ppermute(value, axis, up)
+    after = lax.ppermute(value, axis, down)
+    return jnp.stack([before, value, after])
 
 
 def near_field(charges, near_count, near_target, near_source, near_tiles):
     slots, size, _ = near_tiles.shape
-    everyone = lax.all_gather(charges.reshape(8, size), BOTH, axis=0, tiled=True)
+    beside = with_sides(charges.reshape(8, size), "col")
+    beside = with_sides(beside.reshape(24, size), "row").reshape(72, size)
     per_step = 8
+    smem = pl.BlockSpec(memory_space=pltpu.SMEM)
     return pl.pallas_call(
         near_kernel,
         grid=(slots // per_step,),
         in_specs=[
-            pl.BlockSpec(memory_space=pltpu.SMEM),
-            pl.BlockSpec(memory_space=pltpu.SMEM),
-            pl.BlockSpec(memory_space=pltpu.SMEM),
-            pl.BlockSpec(memory_space=pl.ANY),
+            smem,
+            smem,
+            smem,
+            pl.BlockSpec((72, size), lambda step: (0, 0)),
             pl.BlockSpec((per_step, size, size), lambda step: (step, 0, 0)),
         ],
         out_specs=pl.BlockSpec((1, TRI), lambda step: (0, 0)),
         out_shape=jax.ShapeDtypeStruct((1, TRI), F32),
-        scratch_shapes=[
-            pltpu.VMEM((72, size), F32),
-            pltpu.VMEM((TRI, size), F32),
-            pltpu.SemaphoreType.DMA((9,)),
-        ],
+        scratch_shapes=[pltpu.VMEM((TRI, size), F32)],
         compiler_params=PARAMS,
         name="near",
-    )(near_count, near_target, near_source, everyone, near_tiles)
-
-
-def exchange(values):
-    return lax.all_to_all(values, BOTH, split_axis=0, concat_axis=0, tiled=True)
+    )(near_count, near_target, near_source, beside, near_tiles)
+
+
+def exchange(values, axes, pieces):
+    shaped = values.reshape(pieces, 1, values.size // pieces)
+    moved = lax.all_to_all(shaped, axes, split_axis=0, concat_axis=0, tiled=True)
+    return moved.reshape(values.shape)
 
 
 def local(
@@ -347,30 +385,46 @@
     near_source,
     near_tiles,
 ):
-    lines_table, first, second, flipped = [jnp.asarray(table) for table in tables()]
-    spectrum = lax.all_gather(kernel_spectrum, "row", axis=0, tiled=True)
-    spectrum = lax.dynamic_index_in_dim(spectrum, lax.axis_index("row"), axis=1, keepdims=False)
-    deposited = pl.pallas_call(
+    lines_table, first, second, flipped, chosen = [jnp.asarray(table) for table in tables()]
+    devices = ROWS * COLS
+    packed = jax.ShapeDtypeStruct((devices * LINES // LANES, LANES), F32)
+    hbm = pl.BlockSpec(memory_space=pltpu.HBM)
+    deposited, sent = pl.pallas_call(
         deposit_kernel,
-        out_shape=jax.ShapeDtypeStruct((G, LINES), F32),
+        out_shape=(packed, jax.ShapeDtypeStruct((CELLS_B * SENT, LANES), F32)),
+        in_specs=[hbm] * 5,
         scratch_shapes=[
+            pltpu.VMEM((1, TRI), F32),
+            pltpu.VMEM((3, TRI), jnp.int32),
+            pltpu.VMEM((64, TRI), F32),
+            pltpu.VMEM((2, G, G), BF16),
+            pltpu.VMEM((2, CELLS_B * KEPT, LANES), F32),
             pltpu.VMEM((64, TRI), F32),
             pltpu.VMEM((2, 4, SPREAD, TRI), BF16),
             pltpu.VMEM((LINES, G), F32),
+            pltpu.SemaphoreType.DMA((6,)),
         ],
         compiler_params=PARAMS,
         name="deposit",
-    )(charges.reshape(1, TRI), anchors, stencil_weights, lines_table)
-    received = exchange(deposited)
-    near = near_field(charges, near_count, near_target, near_source, near_tiles)
+    )(
+        charges.reshape(1, TRI),
+        anchors,
+        stencil_weights,
+        lines_table,
+        kernel_spectrum.reshape(CELLS_A * CELLS_B, G),
+    )
+    received = exchange(deposited, BOTH, devices)
+    spectrum = exchange(sent, "row", ROWS)
     handed = pl.pallas_call(
         plane_kernel,
-        out_shape=jax.ShapeDtypeStruct((G, LINES), F32),
+        out_shape=packed,
         scratch_shapes=[pltpu.VMEM((MAIN, G), F32)],
         compiler_params=PARAMS,
         name="plane",
-    )(received, spectrum, first, second, flipped)
-    field = exchange(handed)
+    )(received, spectrum, chosen, first, second, flipped)
+    field = exchange(handed, BOTH, devices)
+    charges, _ = lax.optimization_barrier((charges, handed))
+    near = near_field(charges, near_count, near_target, near_source, near_tiles)
     result = pl.pallas_call(
         gather_kernel,
         out_shape=jax.ShapeDtypeStruct((1, TRI), F32),

time: 164 us -> 85.6 us (0.52)
  waiting for transfers between devices: 106 us -> 8.88 us
  blocking collectives: 0 us -> 42.5 us
  between operations: 14.2 us -> 0.76 us
  starting transfers between devices: 21.3 us -> 14.7 us
  local copies, waits for them, and re-layouts: 9.84 us -> 5.26 us
    all_gather x2 -> x0, waiting for transfers between devices: 86.6 us -> none  [the longest x1 86.5 us: near_field(): lax.all_gather(charges.reshape(8, size), BOTH, axis=0, tiled=True)]
    all_to_all x0 -> x2, blocking collectives: none -> 42.5 us  [exchange(): lax.all_to_all(shaped, axes, split_axis=0, concat_axis=0, tiled=True)]
    all_to_all x2 -> x1, waiting for transfers between devices: 18.4 us -> 0.01 us  [exchange(): lax.all_to_all(shaped, axes, split_axis=0, concat_axis=0, tiled=True)]
    all_to_all x2 -> x1, starting transfers between devices: 21.2 us -> 5.52 us  [exchange(): lax.all_to_all(shaped, axes, split_axis=0, concat_axis=0, tiled=True)]
    ppermute x0 -> x4, starting transfers between devices: none -> 9.19 us  [the longest x2 6.71 us: with_sides(): after = lax.ppermute(value, axis, down)]
    ppermute x0 -> x4, waiting for transfers between devices: none -> 8.88 us  [the longest x2 4.55 us: with_sides(): before = lax.ppermute(value, axis, up)]
    all_to_all x2 -> x0, local copies, waits for them, and re-layouts: 2.3 us -> none  [exchange(): return lax.all_to_all(values, BOTH, split_axis=0, concat_axis=0, tiled=True)]
    unnamed x31 -> x32, local copies, waits for them, and re-layouts: 6.43 us -> 5.26 us
  transfers between devices with their start and end apart: 4 -> 5, of which waited for: 2 -> 4; matrix products, arithmetic and copies ran while one was open for 2% -> 0% of each run, Pallas kernels for 5% -> 1%
where the time goes in v1:
time: 85.6 us; the launch traced here: 85 us
  blocking collectives  42.5 us (50%)
  starting transfers between devices  14.7 us (17%)
  Pallas kernels  12.9 us (15%)
  waiting for transfers between devices  8.88 us (10%)
  local copies, waits for them, and re-layouts  5.26 us (6%)
    all_to_all x2, blocking collectives, exchange(): lax.all_to_all(shaped, axes, split_axis=0, concat_axis=0, tiled=True)  42.5 us
    ppermute x2, starting transfers between devices, with_sides(): after = lax.ppermute(value, axis, down)  6.71 us
    all_to_all x1, starting transfers between devices, exchange(): lax.all_to_all(shaped, axes, split_axis=0, concat_axis=0, tiled=True)  5.52 us
    unnamed x32, local copies, waits for them, and re-layouts  5.26 us
    pallas_call x1, Pallas kernels, local(): pl.pallas_call(deposit_kernel, out_shape=(packed, jax.ShapeDtypeStruct((C...  4.76 us
    ppermute x2, waiting for transfers between devices, with_sides(): before = lax.ppermute(value, axis, up)  4.55 us
    ppermute x2, waiting for transfers between devices, with_sides(): after = lax.ppermute(value, axis, down)  4.32 us
    pallas_call x1, Pallas kernels, local(): pl.pallas_call(gather_kernel, out_shape=jax.ShapeDtypeStruct((1, TRI), F3...  4.04 us
  transfers between devices with their start and end apart: 5, of which 4 were waited for; matrix products, arithmetic and copies ran while one was open for 0% of the time, Pallas kernels for 1%

profile of v1, /device:TPU:1, one launch (start us, length us, event | category | flops | bytes accessed | tf_op | source)
XLA Modules:
  0.0 85.0 jit_solution(8903522713267382688)
XLA Ops:
  0.0 0.0 copy-start.14
  0.0 0.0 copy-start.15
  0.0 0.0 copy-start.1
  0.0 1.0 %copy-done.1 = f32[64,1024]{1,0:T(8,128)S(1)} copy-done((f32[64,1024]{1,0:T(8,128)S(1)}, f32[64,1024]{1,0:T(8,128)}, u32[]{:S(2)}) %copy-start.1) | copy-done | bytes 262168
  1.0 0.0 copy-start.3
  1.0 0.9 %copy-done.3 = bf16[2,256,256]{2,1,0:T(8,128)(2,1)S(1)} copy-done((bf16[2,256,256]{2,1,0:T(8,128)(2,1)S(1)}, bf16[2,256,256]{2,1,0:T(8,128)(2,1)}, u32[]{:S(2)}) %copy-start.3) | copy-done | bytes 262168
  1.9 0.0 copy-start.8
  1.9 0.9 %copy-done.8 = f32[32,8,256]{2,1,0:T(8,128)S(1)} copy-done((f32[32,8,256]{2,1,0:T(8,128)S(1)}, f32[32,8,256]{2,1,0:T(8,128)}, u32[]{:S(2)}) %copy-start.8) | copy-done | bytes 262168
  2.9 0.0 copy-start.10
  2.9 0.7 copy-done.10
  3.6 0.0 copy-start.12
  3.6 0.7 copy-done.12
  4.3 0.0 copy-start.5
  4.3 0.0 copy-start.6
  4.3 0.0 copy-start.7
  4.3 4.8 %deposit.1 = (f32[768,128]{1,0:T(8,128)S(1)}, f32[272,128]{1,0:T(8,128)S(1)}) custom-call(f32[1,1024]{1,0:T(1,128)S(1)} %bitcast.27, s32[3,1024]{1,0:T(4,128)S(1)} %copy-done.10, f32[64,1024]{1,0:T(8,128)S(1)} %copy-done.1, bf16[2,256,256]{2,1,0:T(8,128)(2,1)S(1)} %copy-done.3, f32[256,256]{1,0:T(8,128)S(1)} %bitcast.24), custom_call_target="tpu_custom_call" | custom-call | tf_op jit(solution)/shard_map/deposit/pallas_call | solution.py:392
  9.1 0.0 copy-start
  9.1 11.3 %all_to_all.15 = f32[8,1,4352]{2,1,0:T(1,128)S(1)} all-to-all(f32[8,1,4352]{2,1,0:T(1,128)S(1)} %bitcast.26), channel_id=1, replica_groups=mesh['row'=8,'col'=32] {'row'}, dimensions={0} | all-to-all | bytes 278528 | tf_op jit(solution)/shard_map/all_to_all | solution.py:374
  20.3 31.2 %all_to_all.16 = f32[256,1,384]{2,1,0:T(1,128)S(1)} all-to-all(f32[256,1,384]{2,1,0:T(1,128)S(1)} %bitcast.23), channel_id=1, replica_groups=mesh['row'=8,'col'=32] {'row','col'}, dimensions={0} | all-to-all | bytes 786432 | tf_op jit(solution)/shard_map/all_to_all | solution.py:374
  51.6 0.0 copy-done.5
  51.6 0.0 copy-done.6
  51.6 0.0 copy-done.7
  51.6 0.0 copy-start.9
  51.6 0.9 %copy-done.9 = bf16[2,256,256]{2,1,0:T(8,128)(2,1)S(1)} copy-done((bf16[2,256,256]{2,1,0:T(8,128)(2,1)S(1)}, bf16[2,256,256]{2,1,0:T(8,128)(2,1)}, u32[]{:S(2)}) %copy-start.9) | copy-done | bytes 262168
  52.5 0.0 copy-start.13
  52.5 3.1 %plane.1 = f32[768,128]{1,0:T(8,128)} custom-call(f32[768,128]{1,0:T(8,128)S(1)} %bitcast.21, f32[272,128]{1,0:T(8,128)S(1)} %bitcast.22, bf16[2,256,272]{2,1,0:T(8,128)(2,1)S(1)} %copy-done.6, bf16[2,256,256]{2,1,0:T(8,128)(2,1)S(1)} %copy-done.9, bf16[2,256,320]{2,1,0:T(8,128)(2,1)S(1)} %copy-done.5, bf16[2,320,256]{2,1,0:T(8,128)(2,1)S(1)} %copy-done.7), custom_call_target="tpu_custom_call" | custom-call | tf_op jit(solution)/shard_map/plane/pallas_call | solution.py:418
  55.6 0.0 copy-start.2
  55.6 0.0 copy-start.4
  55.6 0.0 copy-start.11
  55.6 5.5 %all-to-all-start.2 = ((f32[256,1,384]{2,1,0:T(1,128)}), f32[256,1,384]{2,1,0:T(1,128)S(1)}, u32[]{:S(2)}, u32[]{:S(2)}) async-start(f32[256,1,384]{2,1,0:T(1,128)} %bitcast.6), calls=%async_computation.2 | async-start | bytes 786432 | tf_op jit(solution)/shard_map/all_to_all | solution.py:374
  61.1 0.0 copy-done.13
  61.1 6.7 %collective-permute-start.1 = (f32[8,128]{1,0:T(8,128)S(1)}, f32[8,128]{1,0:T(8,128)S(1)}, u32[]{:S(2)}, u32[]{:S(2)}) collective-permute-start(f32[8,128]{1,0:T(8,128)S(1)} %bitcast.28), channel_id=1, source_target_pairs={{1,0},{2,1},{3,2},{4,3},{5,4},{6,5},{7,6},{8,7},{9,8},{10,9},{11,1... | collective-permute-start | bytes 12296 | tf_op jit(solution)/shard_map/ppermute | solution.py:344
  67.9 0.0 collective-permute-start
  67.9 2.0 %collective-permute-done.1 = f32[8,128]{1,0:T(8,128)S(1)} collective-permute-done((f32[8,128]{1,0:T(8,128)S(1)}, f32[8,128]{1,0:T(8,128)S(1)}, u32[]{:S(2)}, u32[]{:S(2)}) %collective-permute-start.1) | collective-permute-done | bytes 4128 | tf_op jit(solution)/shard_map/ppermute | solution.py:344
  69.9 4.4 %collective-permute-done = f32[8,128]{1,0:T(8,128)S(1)} collective-permute-done((f32[8,128]{1,0:T(8,128)S(1)}, f32[8,128]{1,0:T(8,128)S(1)}, u32[]{:S(2)}, u32[]{:S(2)}) %collective-permute-start) | collective-permute-done | bytes 4128 | tf_op jit(solution)/shard_map/ppermute | solution.py:343
  74.3 2.5 %collective-permute-start.2 = (f32[24,128]{1,0:T(8,128)S(1)}, f32[24,128]{1,0:T(8,128)S(1)}, u32[]{:S(2)}, u32[]{:S(2)}) collective-permute-start(f32[24,128]{1,0:T(8,128)S(1)} %get-tuple-element.12), channel_id=1, source_target_pairs={{0,32},{32,64},{64,96},{96,128},{128,160},{160,192},{192,224},{224... | collective-permute-start | bytes 36872 | tf_op jit(solution)/shard_map/ppermute | solution.py:343
  76.7 0.0 collective-permute-start.3
  77.4 0.2 collective-permute-done.2
  77.6 2.3 %collective-permute-done.3 = f32[24,128]{1,0:T(8,128)S(1)} collective-permute-done((f32[24,128]{1,0:T(8,128)S(1)}, f32[24,128]{1,0:T(8,128)S(1)}, u32[]{:S(2)}, u32[]{:S(2)}) %collective-permute-start.3) | collective-permute-done | bytes 12320 | tf_op jit(solution)/shard_map/ppermute | solution.py:344
  79.9 0.0 copy-done.14
  79.9 0.0 copy-done.15
  79.9 0.0 copy-done
  79.9 1.1 %near.1.near_ref = f32[1,1024]{1,0:T(1,128)S(1)} custom-call(s32[1]{0:T(128)S(6)} %copy.17.count_ref, s32[32]{0:T(128)S(1)} %copy-done.14, s32[32]{0:T(128)S(1)} %copy-done.15, f32[72,128]{1,0:T(8,128)S(1)} %bitcast.25, f32[32,128,128]{2,1,0:T(8,128)S(1)} %copy-done), custom_call_target="tpu_custom_call" | custom-call | tf_op jit(solution)/shard_map/near/pallas_call | solution.py:354
  81.0 0.0 all-to-all-done.2
  81.0 0.0 copy-done.2
  81.0 0.0 copy-done.4
  81.0 0.0 copy-done.11
  81.0 4.0 %gather.1 = f32[1,1024]{1,0:T(1,128)} custom-call(f32[768,128]{1,0:T(8,128)S(1)} %bitcast.20, s32[3,1024]{1,0:T(4,128)S(1)} %copy-done.11, f32[64,1024]{1,0:T(8,128)S(1)} %copy-done.2, bf16[2,256,256]{2,1,0:T(8,128)(2,1)S(1)} %copy-done.4, f32[1,1024]{1,0:T(1,128)S(1)} %near.1.near_ref), custom_call_target="tpu_custom_call" | custom-call | tf_op jit(solution)/shard_map/gather/pallas_call | solution.py:428
  (2 shorter events, 0.0 us)
Async XLA Ops:
  0.0 79.9 %copy-start.14 = (s32[32]{0:T(128)S(1)}, s32[32]{0:T(128)}, u32[]{:S(2)}) copy-start(s32[32]{0:T(128)} %target_ref.1) | copy-start | bytes 388
  0.0 79.9 %copy-start.15 = (s32[32]{0:T(128)S(1)}, s32[32]{0:T(128)}, u32[]{:S(2)}) copy-start(s32[32]{0:T(128)} %source_ref.1) | copy-start | bytes 388
  0.0 1.0 %copy-start.1 = (f32[64,1024]{1,0:T(8,128)S(1)}, f32[64,1024]{1,0:T(8,128)}, u32[]{:S(2)}) copy-start(f32[64,1024]{1,0:T(8,128)} %weights_ref.1) | copy-start | bytes 786436
  1.0 0.9 %copy-start.3 = (bf16[2,256,256]{2,1,0:T(8,128)(2,1)S(1)}, bf16[2,256,256]{2,1,0:T(8,128)(2,1)}, u32[]{:S(2)}) copy-start(bf16[2,256,256]{2,1,0:T(8,128)(2,1)} %constant.10.clone.table_hbm.table_ref) | copy-start | bytes 786436
  1.9 0.9 %copy-start.8 = (f32[32,8,256]{2,1,0:T(8,128)S(1)}, f32[32,8,256]{2,1,0:T(8,128)}, u32[]{:S(2)}) copy-start(f32[32,8,256]{2,1,0:T(8,128)} %param.16) | copy-start | bytes 786436
  2.9 0.7 copy-start.10
  3.6 0.7 copy-start.12
  4.3 47.3 %copy-start.5 = (bf16[2,256,320]{2,1,0:T(8,128)(2,1)S(1)}, bf16[2,256,320]{2,1,0:T(8,128)(2,1)}, u32[]{:S(2)}) copy-start(bf16[2,256,320]{2,1,0:T(8,128)(2,1)} %constant.12.clone.second_ref) | copy-start | bytes 983044
  4.3 47.3 %copy-start.6 = (bf16[2,256,272]{2,1,0:T(8,128)(2,1)S(1)}, bf16[2,256,272]{2,1,0:T(8,128)(2,1)}, u32[]{:S(2)}) copy-start(bf16[2,256,272]{2,1,0:T(8,128)(2,1)} %constant.14.clone.chosen_ref) | copy-start | bytes 835588
  4.3 47.3 %copy-start.7 = (bf16[2,320,256]{2,1,0:T(8,128)(2,1)S(1)}, bf16[2,320,256]{2,1,0:T(8,128)(2,1)}, u32[]{:S(2)}) copy-start(bf16[2,320,256]{2,1,0:T(8,128)(2,1)} %constant.13.clone.flipped_ref) | copy-start | bytes 983044
  9.1 70.8 %copy-start = (f32[32,128,128]{2,1,0:T(8,128)S(1)}, f32[32,128,128]{2,1,0:T(8,128)}, u32[]{:S(2)}) copy-start(f32[32,128,128]{2,1,0:T(8,128)} %tiles_ref.1) | copy-start | bytes 6291460
  51.6 1.0 %copy-start.9 = (bf16[2,256,256]{2,1,0:T(8,128)(2,1)S(1)}, bf16[2,256,256]{2,1,0:T(8,128)(2,1)}, u32[]{:S(2)}) copy-start(bf16[2,256,256]{2,1,0:T(8,128)(2,1)} %constant.11.clone.first_ref) | copy-start | bytes 786436
  52.5 8.6 %copy-start.13 = (f32[1024]{0:T(1024)S(1)}, f32[1024]{0:T(1024)}, u32[]{:S(2)}) copy-start(f32[1024]{0:T(1024)} %param.13) | copy-start | bytes 12292
  55.6 25.4 %copy-start.2 = (f32[64,1024]{1,0:T(8,128)S(1)}, f32[64,1024]{1,0:T(8,128)}, u32[]{:S(2)}) copy-start(f32[64,1024]{1,0:T(8,128)} %weights_ref.1) | copy-start | bytes 786436
  55.6 25.4 %copy-start.4 = (bf16[2,256,256]{2,1,0:T(8,128)(2,1)S(1)}, bf16[2,256,256]{2,1,0:T(8,128)(2,1)}, u32[]{:S(2)}) copy-start(bf16[2,256,256]{2,1,0:T(8,128)(2,1)} %constant.10.clone.table_hbm.table_ref) | copy-start | bytes 786436
  55.6 25.4 %copy-start.11 = (s32[3,1024]{1,0:T(4,128)S(1)}, s32[3,1024]{1,0:T(4,128)}, u32[]{:S(2)}) copy-start(s32[3,1024]{1,0:T(4,128)} %anchors_ref.1) | copy-start | bytes 36868
  55.6 25.4 %all-to-all-start.2 = ((f32[256,1,384]{2,1,0:T(1,128)}), f32[256,1,384]{2,1,0:T(1,128)S(1)}, u32[]{:S(2)}, u32[]{:S(2)}) async-start(f32[256,1,384]{2,1,0:T(1,128)} %bitcast.6), calls=%async_computation.2 | async-start | bytes 786432 | tf_op jit(solution)/shard_map/all_to_all | solution.py:374
  61.1 8.7 %collective-permute-start.1 = (f32[8,128]{1,0:T(8,128)S(1)}, f32[8,128]{1,0:T(8,128)S(1)}, u32[]{:S(2)}, u32[]{:S(2)}) collective-permute-start(f32[8,128]{1,0:T(8,128)S(1)} %bitcast.28), channel_id=1, source_target_pairs={{1,0},{2,1},{3,2},{4,3},{5,4},{6,5},{7,6},{8,7},{9,8},{10,9},{11,1... | collective-permute-start | bytes 12296 | tf_op jit(solution)/shard_map/ppermute | solution.py:344
  67.9 6.4 %collective-permute-start = (f32[8,128]{1,0:T(8,128)S(1)}, f32[8,128]{1,0:T(8,128)S(1)}, u32[]{:S(2)}, u32[]{:S(2)}) collective-permute-start(f32[8,128]{1,0:T(8,128)S(1)} %bitcast.29), channel_id=1, source_target_pairs={{0,1},{1,2},{2,3},{3,4},{4,5},{5,6},{6,7},{7,8},{8,9},{9,10},{10,1... | collective-permute-start | bytes 12296 | tf_op jit(solution)/shard_map/ppermute | solution.py:343
  74.3 3.3 %collective-permute-start.2 = (f32[24,128]{1,0:T(8,128)S(1)}, f32[24,128]{1,0:T(8,128)S(1)}, u32[]{:S(2)}, u32[]{:S(2)}) collective-permute-start(f32[24,128]{1,0:T(8,128)S(1)} %get-tuple-element.12), channel_id=1, source_target_pairs={{0,32},{32,64},{64,96},{96,128},{128,160},{160,192},{192,224},{224... | collective-permute-start | bytes 36872 | tf_op jit(solution)/shard_map/ppermute | solution.py:343
  76.7 3.1 %collective-permute-start.3 = (f32[24,128]{1,0:T(8,128)S(1)}, f32[24,128]{1,0:T(8,128)S(1)}, u32[]{:S(2)}, u32[]{:S(2)}) collective-permute-start(f32[24,128]{1,0:T(8,128)S(1)} %get-tuple-element.12), channel_id=1, source_target_pairs={{32,0},{64,32},{96,64},{128,96},{160,128},{192,160},{224,192},{0,2... | collective-permute-start | bytes 36872 | tf_op jit(solution)/shard_map/ppermute | solution.py:344

commit v2 on v1

--- a/solution.py
+++ b/solution.py
@@ -23,7 +23,7 @@
 BF16 = jnp.bfloat16
 BOTH = ("row", "col")
 KEPT = CELLS_A // 2 + 1
-SENT = 2 * KEPT
+SENT = 40
 PARAMS = pltpu.CompilerParams(vmem_limit_bytes=48 * 1024 * 1024)
 
 
@@ -119,9 +119,11 @@
 
 
 def deposit_kernel(
-    charges_hbm, anchors_hbm, weights_hbm, table_hbm, spectrum_hbm, out_ref, sent_ref,
-    charges_ref, anchors_ref, weights_ref, table_ref, spectrum_ref, scaled, spread, lines, sem,
+    charges_hbm, anchors_hbm, weights_hbm, table_hbm, spectrum_hbm, out_ref, *rest
 ):
+    sent_refs = rest[:ROWS]
+    charges_ref, anchors_ref, weights_ref, table_ref, spectrum_ref = rest[ROWS : ROWS + 5]
+    scaled, spread, lines, sem = rest[ROWS + 5 :]
     pairs = (
         (weights_hbm, weights_ref),
         (anchors_hbm, anchors_ref),
@@ -177,10 +179,16 @@
     lax.fori_loop(0, TILES, tile, 0)
     for copy in copies[3:]:
         copy.wait()
-    for c in range(CELLS_B):
+    for shift, sent in enumerate(sent_refs):
+        c = (lax.axis_index("row") + shift) & (ROWS - 1)
+        sent[pl.ds(SENT - 8, 8), :] = jnp.zeros((8, LANES), F32)
         for half in range(2):
             rows = spectrum_ref[half, pl.ds(c, KEPT, stride=CELLS_B), :]
-            sent_ref[pl.ds(c * SENT + half * KEPT, KEPT), :] = rows
+            sent[pl.ds(half * KEPT, KEPT), :] = rows
+    for shift in (1, ROWS - 1):
+        for block in range(8):
+            at = pl.ds(block * LANES, LANES)
+            sent_refs[shift][pl.ds(SENT + block, 1), :] = charges_ref[:, at]
     hot = onehot(anchors_ref)
     total = None
     for k in range(4):
@@ -201,7 +209,17 @@
     return pltpu.roll(value, shift, 1) if shift else value
 
 
-def plane_kernel(tiles_ref, spectrum_ref, chosen_ref, first_ref, second_ref, flipped_ref, out_ref, whole):
+def plane_kernel(
+    tiles_ref, charges_ref, chosen_ref, first_ref, second_ref, flipped_ref, *rest
+):
+    sent_refs, (out_ref, beside_ref, whole, spectrum_ref) = rest[:ROWS], rest[ROWS:]
+    for shift, sent in enumerate(sent_refs):
+        owner = (lax.axis_index("row") - shift) & (ROWS - 1)
+        at = pl.ds(pl.multiple_of(owner * SENT, 8), SENT)
+        spectrum_ref[at, :] = sent[pl.ds(0, SENT), :]
+    beside_ref[pl.ds(0, 8), :] = sent_refs[1][pl.ds(SENT, 8), :]
+    beside_ref[pl.ds(8, 8), :] = charges_ref[...]
+    beside_ref[pl.ds(16, 8), :] = sent_refs[ROWS - 1][pl.ds(SENT, 8), :]
     lane = lax.broadcasted_iota(jnp.int32, (32, LANES), 1)
     slots = [(lane >> 5) == s for s in range(4)]
     rim = (lane & 31) < 2
@@ -312,18 +330,27 @@
     lax.fori_loop(0, TILES, tile, 0)
 
 
-def near_kernel(count_ref, target_ref, source_ref, charges_ref, tiles_ref, out_ref, total):
+def near_kernel(
+    count_ref, target_ref, source_ref, before_ref, own_ref, after_ref, tiles_ref, out_ref,
+    charges_ref, total,
+):
     step = pl.program_id(0)
     per_step, size = tiles_ref.shape[0], tiles_ref.shape[1]
 
     @pl.when(step == 0)
     def _():
         total[...] = jnp.zeros_like(total)
+        for place, ref in enumerate((before_ref, own_ref, after_ref)):
+            charges_ref[pl.ds(24 * place, 24), :] = ref[...]
 
     def slot(u, carry):
         place = step * per_step + u
         rows = pl.ds(pl.multiple_of(target_ref[place] * size, size), size)
-        source = charges_ref[pl.ds(source_ref[place], 1), :]
+        code = source_ref[place]
+        neighbour = code >> 3
+        row = neighbour // 3
+        line = 24 * (neighbour - 3 * row) + 8 * row + (code & 7)
+        source = charges_ref[pl.ds(line, 1), :]
         total[rows, :] = total[rows, :] + tiles_ref[u] * source
         return carry
 
@@ -336,19 +363,14 @@
         out_ref[...] = result[0:1]
 
 
-def with_sides(value, axis):
+def shifted(value, axis, by):
     size = lax.axis_size(axis)
-    up = [(i, (i + 1) % size) for i in range(size)]
-    down = [(j, i) for i, j in up]
-    before = lax.ppermute(value, axis, up)
-    after = lax.ppermute(value, axis, down)
-    return jnp.stack([before, value, after])
-
-
-def near_field(charges, near_count, near_target, near_source, near_tiles):
+    return lax.ppermute(value, axis, [(i, (i + by) % size) for i in range(size)])
+
+
+def near_field(beside, near_count, near_target, near_source, near_tiles):
     slots, size, _ = near_tiles.shape
-    beside = with_sides(charges.reshape(8, size), "col")
-    beside = with_sides(beside.reshape(24, size), "row").reshape(72, size)
+    before, after = shifted(beside, "col", 1), shifted(beside, "col", -1)
     per_step = 8
     smem = pl.BlockSpec(memory_space=pltpu.SMEM)
     return pl.pallas_call(
@@ -358,15 +380,15 @@
             smem,
             smem,
             smem,
-            pl.BlockSpec((72, size), lambda step: (0, 0)),
+            *[pl.BlockSpec((24, size), lambda step: (0, 0))] * 3,
             pl.BlockSpec((per_step, size, size), lambda step: (step, 0, 0)),
         ],
         out_specs=pl.BlockSpec((1, TRI), lambda step: (0, 0)),
         out_shape=jax.ShapeDtypeStruct((1, TRI), F32),
-        scratch_shapes=[pltpu.VMEM((TRI, size), F32)],
+        scratch_shapes=[pltpu.VMEM((72, size), F32), pltpu.VMEM((TRI, size), F32)],
         compiler_params=PARAMS,
         name="near",
-    )(near_count, near_target, near_source, beside, near_tiles)
+    )(near_count, near_target, near_source, before, beside, after, near_tiles)
 
 
 def exchange(values, axes, pieces):
@@ -389,9 +411,10 @@
     devices = ROWS * COLS
     packed = jax.ShapeDtypeStruct((devices * LINES // LANES, LANES), F32)
     hbm = pl.BlockSpec(memory_space=pltpu.HBM)
-    deposited, sent = pl.pallas_call(
+    sizes = [SENT + 8 if shift in (1, ROWS - 1) else SENT for shift in range(ROWS)]
+    deposited, *sent = pl.pallas_call(
         deposit_kernel,
-        out_shape=(packed, jax.ShapeDtypeStruct((CELLS_B * SENT, LANES), F32)),
+        out_shape=(packed, *[jax.ShapeDtypeStruct((size, LANES), F32) for size in sizes]),
         in_specs=[hbm] * 5,
         scratch_shapes=[
             pltpu.VMEM((1, TRI), F32),
@@ -407,24 +430,28 @@
         compiler_params=PARAMS,
         name="deposit",
     )(
-        charges.reshape(1, TRI),
-        anchors,
-        stencil_weights,
-        lines_table,
-        kernel_spectrum.reshape(CELLS_A * CELLS_B, G),
+        *[
+            pltpu.with_memory_space_constraint(value, pltpu.HBM)
+            for value in (
+                charges.reshape(1, TRI),
+                anchors,
+                stencil_weights,
+                lines_table,
+                kernel_spectrum.reshape(CELLS_A * CELLS_B, G),
+            )
+        ]
     )
     received = exchange(deposited, BOTH, devices)
-    spectrum = exchange(sent, "row", ROWS)
-    handed = pl.pallas_call(
+    sent = [shifted(value, "row", shift) if shift else value for shift, value in enumerate(sent)]
+    handed, beside = pl.pallas_call(
         plane_kernel,
-        out_shape=packed,
-        scratch_shapes=[pltpu.VMEM((MAIN, G), F32)],
+        out_shape=(packed, jax.ShapeDtypeStruct((24, LANES), F32)),
+        scratch_shapes=[pltpu.VMEM((MAIN, G), F32), pltpu.VMEM((ROWS * SENT, LANES), F32)],
         compiler_params=PARAMS,
         name="plane",
-    )(received, spectrum, chosen, first, second, flipped)
+    )(received, charges.reshape(8, LANES), chosen, first, second, flipped, *sent)
     field = exchange(handed, BOTH, devices)
-    charges, _ = lax.optimization_barrier((charges, handed))
-    near = near_field(charges, near_count, near_target, near_source, near_tiles)
+    near = near_field(beside, near_count, near_target, near_source, near_tiles)
     result = pl.pallas_call(
         gather_kernel,
         out_shape=jax.ShapeDtypeStruct((1, TRI), F32),

time: 85.6 us -> 77.8 us (0.909)
  blocking collectives: 42.5 us -> 0 us
  starting transfers between devices: 14.7 us -> 38.5 us
  waiting for transfers between devices: 8.88 us -> 18.3 us
  Pallas kernels: 12.9 us -> 15.3 us
    all_to_all x2 -> x0, blocking collectives: 42.5 us -> none  [exchange(): lax.all_to_all(shaped, axes, split_axis=0, concat_axis=0, tiled=True)]
    all_to_all x1 -> x2, starting transfers between devices: 5.52 us -> 22.2 us  [exchange(): lax.all_to_all(shaped, axes, split_axis=0, concat_axis=0, tiled=True)]
    all_to_all x1 -> x2, waiting for transfers between devices: 0.01 us -> 10.2 us  [exchange(): lax.all_to_all(shaped, axes, split_axis=0, concat_axis=0, tiled=True)]
    ppermute x4 -> x9, starting transfers between devices: 9.19 us -> 16.3 us  [shifted(): lax.ppermute(value, axis, [(i, (i + by) % size) for i in range(size)])]
    pallas_call x2, Pallas kernels: 7.83 us -> 9.61 us  [the longest x1 6.52 us: local(): pl.pallas_call(deposit_kernel, out_shape=(packed, *[jax.ShapeDtypeStruct(...]
    ppermute x4 -> x9, waiting for transfers between devices: 8.88 us -> 8.12 us  [shifted(): lax.ppermute(value, axis, [(i, (i + by) % size) for i in range(size)])]
    unnamed x32 -> x22, local copies, waits for them, and re-layouts: 5.26 us -> 4.62 us
  transfers between devices with their start and end apart: 5 -> 11, of which waited for: 4 -> 6; matrix products, arithmetic and copies ran while one was open for 0% -> 0% of each run, Pallas kernels for 1% -> 2%
where the time goes in v2:
time: 77.8 us; the launch traced here: 77.4 us
  starting transfers between devices  38.5 us (49%)
  waiting for transfers between devices  18.3 us (24%)
  Pallas kernels  15.3 us (20%)
  local copies, waits for them, and re-layouts  4.62 us (6%)
    all_to_all x2, starting transfers between devices, exchange(): lax.all_to_all(shaped, axes, split_axis=0, concat_axis=0, tiled=True)  22.2 us
    ppermute x9, starting transfers between devices, shifted(): lax.ppermute(value, axis, [(i, (i + by) % size) for i in range(size)])  16.3 us
    all_to_all x2, waiting for transfers between devices, exchange(): lax.all_to_all(shaped, axes, split_axis=0, concat_axis=0, tiled=True)  10.2 us
    ppermute x9, waiting for transfers between devices, shifted(): lax.ppermute(value, axis, [(i, (i + by) % size) for i in range(size)])  8.12 us
    pallas_call x1, Pallas kernels, local(): pl.pallas_call(deposit_kernel, out_shape=(packed, *[jax.ShapeDtypeStruct(...  6.52 us
    unnamed x22, local copies, waits for them, and re-layouts  4.62 us
    pallas_call x1, Pallas kernels, local(): pl.pallas_call(gather_kernel, out_shape=jax.ShapeDtypeStruct((1, TRI), F3...  4.05 us
    pallas_call x1, Pallas kernels, local(): pl.pallas_call(plane_kernel, out_shape=(packed, jax.ShapeDtypeStruct((24,...  3.09 us
  transfers between devices with their start and end apart: 11, of which 6 were waited for; matrix products, arithmetic and copies ran while one was open for 0% of the time, Pallas kernels for 2%

profile of v2, /device:TPU:1, one launch (start us, length us, event | category | flops | bytes accessed | tf_op | source)
XLA Modules:
  0.0 77.4 jit_solution(4484690581202754662)
XLA Ops:
  0.0 0.0 copy-start.9
  0.0 0.0 copy-start.10
  0.0 0.0 copy-start
  0.0 6.5 %deposit.1 = (f32[768,128]{1,0:T(8,128)}, f32[40,128]{1,0:T(8,128)S(1)}, f32[48,128]{1,0:T(8,128)S(1)}, f32[40,128]{1,0:T(8,128)S(1)}, f32[40,128]{1,0:T(8,128)S...) custom-call(f32[1,1024]{1,0:T(1,128)} %bitcast.10, ...), custom_call_target="tpu_custom_call" | custom-call | tf_op jit(solution)/shard_map/deposit/pallas_call | solution.py:415
  6.5 15.7 %all-to-all-start = ((f32[256,1,384]{2,1,0:T(1,128)}), f32[256,1,384]{2,1,0:T(1,128)S(1)}, u32[]{:S(2)}, u32[]{:S(2)}) async-start(f32[256,1,384]{2,1,0:T(1,128)} %bitcast.2), calls=%async_computation | async-start | bytes 786432 | tf_op jit(solution)/shard_map/all_to_all | solution.py:396
  22.2 1.5 %collective-permute-start.1 = (f32[40,128]{1,0:T(8,128)S(1)}, f32[40,128]{1,0:T(8,128)S(1)}, u32[]{:S(2)}, u32[]{:S(2)}) collective-permute-start(f32[40,128]{1,0:T(8,128)S(1)} %get-tuple-element.19), channel_id=1, source_target_pairs={{0,64},{32,96},{64,128},{96,160},{128,192},{160,224},{192,0},{224,... | collective-permute-start | bytes 61448 | tf_op jit(solution)/shard_map/ppermute | solution.py:368
  23.7 3.0 %collective-permute-start.2 = (f32[40,128]{1,0:T(8,128)S(1)}, f32[40,128]{1,0:T(8,128)S(1)}, u32[]{:S(2)}, u32[]{:S(2)}) collective-permute-start(f32[40,128]{1,0:T(8,128)S(1)} %get-tuple-element.20), channel_id=1, source_target_pairs={{0,96},{32,128},{64,160},{96,192},{128,224},{160,0},{192,32},{224,... | collective-permute-start | bytes 61448 | tf_op jit(solution)/shard_map/ppermute | solution.py:368
  26.7 0.0 collective-permute-start
  26.7 0.5 collective-permute-start.6
  27.2 1.3 %collective-permute-start.3 = (f32[40,128]{1,0:T(8,128)S(1)}, f32[40,128]{1,0:T(8,128)S(1)}, u32[]{:S(2)}, u32[]{:S(2)}) collective-permute-start(f32[40,128]{1,0:T(8,128)S(1)} %get-tuple-element.21), channel_id=1, source_target_pairs={{0,128},{32,160},{64,192},{96,224},{128,0},{160,32},{192,64},{224,... | collective-permute-start | bytes 61448 | tf_op jit(solution)/shard_map/ppermute | solution.py:368
  28.5 0.0 collective-permute-done.1.rest_2_
  28.5 2.6 %collective-permute-start.4 = (f32[40,128]{1,0:T(8,128)S(1)}, f32[40,128]{1,0:T(8,128)S(1)}, u32[]{:S(2)}, u32[]{:S(2)}) collective-permute-start(f32[40,128]{1,0:T(8,128)S(1)} %get-tuple-element.22), channel_id=1, source_target_pairs={{0,160},{32,192},{64,224},{96,0},{128,32},{160,64},{192,96},{224,1... | collective-permute-start | bytes 61448 | tf_op jit(solution)/shard_map/ppermute | solution.py:368
  31.1 0.0 collective-permute-done.2.rest_3_
  31.1 0.6 collective-permute-start.5
  31.7 0.1 collective-permute-done.3.rest_4_
  31.7 2.0 %collective-permute-done.4.rest_5_ = f32[40,128]{1,0:T(8,128)S(1)} collective-permute-done((f32[40,128]{1,0:T(8,128)S(1)}, f32[40,128]{1,0:T(8,128)S(1)}, u32[]{:S(2)}, u32[]{:S(2)}) %collective-permute-start.4) | collective-permute-done | bytes 20512 | tf_op jit(solution)/shard_map/ppermute | solution.py:368
  33.7 0.7 collective-permute-done.5.rest_6_
  34.4 0.0 collective-permute-done.rest_1_
  34.4 0.0 collective-permute-done.6.rest_7_
  34.4 6.2 %all-to-all-done = f32[256,1,384]{2,1,0:T(1,128)S(1)} async-done(((f32[256,1,384]{2,1,0:T(1,128)}), f32[256,1,384]{2,1,0:T(1,128)S(1)}, u32[]{:S(2)}, u32[]{:S(2)}) %all-to-all-start) | async-done | bytes 393248 | tf_op jit(solution)/shard_map/all_to_all | solution.py:396
  40.6 0.0 copy-start.3
  40.6 1.0 %copy-done.3 = bf16[2,256,320]{2,1,0:T(8,128)(2,1)S(1)} copy-done((bf16[2,256,320]{2,1,0:T(8,128)(2,1)S(1)}, bf16[2,256,320]{2,1,0:T(8,128)(2,1)}, u32[]{:S(2)}) %copy-start.3) | copy-done | bytes 327704
  41.6 0.0 copy-start.4
  41.6 1.0 %copy-done.4 = bf16[2,256,320]{2,1,0:T(8,128)(2,1)S(1)} copy-done((bf16[2,256,320]{2,1,0:T(8,128)(2,1)S(1)}, bf16[2,256,320]{2,1,0:T(8,128)(2,1)}, u32[]{:S(2)}) %copy-start.4) | copy-done | bytes 327704
  42.6 0.0 copy-start.5
  42.6 1.0 %copy-done.5 = bf16[2,320,256]{2,1,0:T(8,128)(2,1)S(1)} copy-done((bf16[2,320,256]{2,1,0:T(8,128)(2,1)S(1)}, bf16[2,320,256]{2,1,0:T(8,128)(2,1)}, u32[]{:S(2)}) %copy-start.5) | copy-done | bytes 327704
  43.6 0.0 copy-start.6
  43.6 0.9 %copy-done.6 = bf16[2,256,256]{2,1,0:T(8,128)(2,1)S(1)} copy-done((bf16[2,256,256]{2,1,0:T(8,128)(2,1)S(1)}, bf16[2,256,256]{2,1,0:T(8,128)(2,1)}, u32[]{:S(2)}) %copy-start.6) | copy-done | bytes 262168
  44.5 0.0 copy-start.8
  44.5 0.7 copy-done.8
  45.2 0.0 copy-start.1
  45.2 0.0 copy-start.2
  45.2 0.0 copy-start.7
  45.2 3.1 %plane.1 = (f32[768,128]{1,0:T(8,128)}, f32[24,128]{1,0:T(8,128)S(1)}) custom-call(f32[768,128]{1,0:T(8,128)S(1)} %bitcast.9, f32[8,128]{1,0:T(8,128)S(1)} %bitcast.11, bf16[2,256,320]{2,1,0:T(8,128)(2,1)S(1)} %copy-done.4, bf16[2,256,256]{2,1,0:T(8,128)(2,1)S(1)} %copy-done.6, bf16[2,256,320]{2,1,0:T(8,128)(2,1)S(1)} %copy-done.3, ...), custom_call_target="tpu_custom_call" | custom-call | tf_op jit(solution)/shard_map/plane/pallas_call | solution.py:446
  48.3 6.5 %all-to-all-start.1 = ((f32[256,1,384]{2,1,0:T(1,128)}), f32[256,1,384]{2,1,0:T(1,128)S(1)}, u32[]{:S(2)}, u32[]{:S(2)}) async-start(f32[256,1,384]{2,1,0:T(1,128)} %bitcast.5), calls=%async_computation.1 | async-start | bytes 786432 | tf_op jit(solution)/shard_map/all_to_all | solution.py:396
  54.9 1.6 %collective-permute-start.7 = (f32[24,128]{1,0:T(8,128)S(1)}, f32[24,128]{1,0:T(8,128)S(1)}, u32[]{:S(2)}, u32[]{:S(2)}) collective-permute-start(f32[24,128]{1,0:T(8,128)S(1)} %get-tuple-element.26.own_ref), channel_id=1, source_target_pairs={{0,1},{1,2},{2,3},{3,4},{4,5},{5,6},{6,7},{7,8},{8,9},{9,10},{10,1... | collective-permute-start | bytes 36872 | tf_op jit(solution)/shard_map/ppermute | solution.py:368
  56.4 5.3 %collective-permute-start.8 = (f32[24,128]{1,0:T(8,128)S(1)}, f32[24,128]{1,0:T(8,128)S(1)}, u32[]{:S(2)}, u32[]{:S(2)}) collective-permute-start(f32[24,128]{1,0:T(8,128)S(1)} %get-tuple-element.26.own_ref), channel_id=1, source_target_pairs={{0,31},{1,0},{2,1},{3,2},{4,3},{5,4},{6,5},{7,6},{8,7},{9,8},{10,9... | collective-permute-start | bytes 36872 | tf_op jit(solution)/shard_map/ppermute | solution.py:368
  62.3 5.4 %collective-permute-done.7.before_ref = f32[24,128]{1,0:T(8,128)S(1)} collective-permute-done((f32[24,128]{1,0:T(8,128)S(1)}, f32[24,128]{1,0:T(8,128)S(1)}, u32[]{:S(2)}, u32[]{:S(2)}) %collective-permute-start.7) | collective-permute-done | bytes 12320 | tf_op jit(solution)/shard_map/ppermute | solution.py:368
  67.7 0.0 collective-permute-done.8.after_ref
  67.7 0.0 copy-done.9
  67.7 0.0 copy-done.10
  67.7 0.0 copy-done
  67.8 1.7 %near.1.near_ref = f32[1,1024]{1,0:T(1,128)S(1)} custom-call(s32[1]{0:T(128)S(6)} %copy.16.count_ref, s32[32]{0:T(128)S(1)} %copy-done.9, s32[32]{0:T(128)S(1)} %copy-done.10, f32[24,128]{1,0:T(8,128)S(1)} %collective-permute-done.7.before_ref, f32[24,128]{1,0:T(8,128)S(1)} %get-tuple-element.26.own_ref, f32[24,128]{1,0:T(8,128)S(1)} %collective-permute-done.8.after_ref, ...), custom_call_target="tpu_custom_call" | custom-call | tf_op jit(solution)/shard_map/near/pallas_call | solution.py:376
  69.4 3.9 %all-to-all-done.1 = f32[256,1,384]{2,1,0:T(1,128)S(1)} async-done(((f32[256,1,384]{2,1,0:T(1,128)}), f32[256,1,384]{2,1,0:T(1,128)S(1)}, u32[]{:S(2)}, u32[]{:S(2)}) %all-to-all-start.1) | async-done | bytes 393248 | tf_op jit(solution)/shard_map/all_to_all | solution.py:396
  73.4 0.0 copy-done.1
  73.4 0.0 copy-done.2
  73.4 0.0 copy-done.7
  73.4 4.0 %gather.1 = f32[1,1024]{1,0:T(1,128)} custom-call(f32[768,128]{1,0:T(8,128)S(1)} %bitcast.8, s32[3,1024]{1,0:T(4,128)S(1)} %copy-done.7, f32[64,1024]{1,0:T(8,128)S(1)} %copy-done.1, bf16[2,256,256]{2,1,0:T(8,128)(2,1)S(1)} %copy-done.2, f32[1,1024]{1,0:T(1,128)S(1)} %near.1.near_ref), custom_call_target="tpu_custom_call" | custom-call | tf_op jit(solution)/shard_map/gather/pallas_call | solution.py:455
Async XLA Ops:
  0.0 67.7 %copy-start.9 = (s32[32]{0:T(128)S(1)}, s32[32]{0:T(128)}, u32[]{:S(2)}) copy-start(s32[32]{0:T(128)} %target_ref.1) | copy-start | bytes 388
  0.0 67.7 %copy-start.10 = (s32[32]{0:T(128)S(1)}, s32[32]{0:T(128)}, u32[]{:S(2)}) copy-start(s32[32]{0:T(128)} %source_ref.1) | copy-start | bytes 388
  0.0 67.7 %copy-start = (f32[32,128,128]{2,1,0:T(8,128)S(1)}, f32[32,128,128]{2,1,0:T(8,128)}, u32[]{:S(2)}) copy-start(f32[32,128,128]{2,1,0:T(8,128)} %tiles_ref.1) | copy-start | bytes 6291460
  6.5 34.1 %all-to-all-start = ((f32[256,1,384]{2,1,0:T(1,128)}), f32[256,1,384]{2,1,0:T(1,128)S(1)}, u32[]{:S(2)}, u32[]{:S(2)}) async-start(f32[256,1,384]{2,1,0:T(1,128)} %bitcast.2), calls=%async_computation | async-start | bytes 786432 | tf_op jit(solution)/shard_map/all_to_all | solution.py:396
  22.2 6.3 %collective-permute-start.1 = (f32[40,128]{1,0:T(8,128)S(1)}, f32[40,128]{1,0:T(8,128)S(1)}, u32[]{:S(2)}, u32[]{:S(2)}) collective-permute-start(f32[40,128]{1,0:T(8,128)S(1)} %get-tuple-element.19), channel_id=1, source_target_pairs={{0,64},{32,96},{64,128},{96,160},{128,192},{160,224},{192,0},{224,... | collective-permute-start | bytes 61448 | tf_op jit(solution)/shard_map/ppermute | solution.py:368
  23.7 7.4 %collective-permute-start.2 = (f32[40,128]{1,0:T(8,128)S(1)}, f32[40,128]{1,0:T(8,128)S(1)}, u32[]{:S(2)}, u32[]{:S(2)}) collective-permute-start(f32[40,128]{1,0:T(8,128)S(1)} %get-tuple-element.20), channel_id=1, source_target_pairs={{0,96},{32,128},{64,160},{96,192},{128,224},{160,0},{192,32},{224,... | collective-permute-start | bytes 61448 | tf_op jit(solution)/shard_map/ppermute | solution.py:368
  26.7 7.7 %collective-permute-start = (f32[48,128]{1,0:T(8,128)S(1)}, f32[48,128]{1,0:T(8,128)S(1)}, u32[]{:S(2)}, u32[]{:S(2)}) collective-permute-start(f32[48,128]{1,0:T(8,128)S(1)} %get-tuple-element.18), channel_id=1, source_target_pairs={{0,32},{32,64},{64,96},{96,128},{128,160},{160,192},{192,224},{224... | collective-permute-start | bytes 73736 | tf_op jit(solution)/shard_map/ppermute | solution.py:368
  26.7 7.7 %collective-permute-start.6 = (f32[48,128]{1,0:T(8,128)S(1)}, f32[48,128]{1,0:T(8,128)S(1)}, u32[]{:S(2)}, u32[]{:S(2)}) collective-permute-start(f32[48,128]{1,0:T(8,128)S(1)} %get-tuple-element.24), channel_id=1, source_target_pairs={{0,224},{32,0},{64,32},{96,64},{128,96},{160,128},{192,160},{224,1... | collective-permute-start | bytes 73736 | tf_op jit(solution)/shard_map/ppermute | solution.py:368
  27.2 4.5 %collective-permute-start.3 = (f32[40,128]{1,0:T(8,128)S(1)}, f32[40,128]{1,0:T(8,128)S(1)}, u32[]{:S(2)}, u32[]{:S(2)}) collective-permute-start(f32[40,128]{1,0:T(8,128)S(1)} %get-tuple-element.21), channel_id=1, source_target_pairs={{0,128},{32,160},{64,192},{96,224},{128,0},{160,32},{192,64},{224,... | collective-permute-start | bytes 61448 | tf_op jit(solution)/shard_map/ppermute | solution.py:368
  28.5 5.2 %collective-permute-start.4 = (f32[40,128]{1,0:T(8,128)S(1)}, f32[40,128]{1,0:T(8,128)S(1)}, u32[]{:S(2)}, u32[]{:S(2)}) collective-permute-start(f32[40,128]{1,0:T(8,128)S(1)} %get-tuple-element.22), channel_id=1, source_target_pairs={{0,160},{32,192},{64,224},{96,0},{128,32},{160,64},{192,96},{224,1... | collective-permute-start | bytes 61448 | tf_op jit(solution)/shard_map/ppermute | solution.py:368
  31.1 3.3 %collective-permute-start.5 = (f32[40,128]{1,0:T(8,128)S(1)}, f32[40,128]{1,0:T(8,128)S(1)}, u32[]{:S(2)}, u32[]{:S(2)}) collective-permute-start(f32[40,128]{1,0:T(8,128)S(1)} %get-tuple-element.23), channel_id=1, source_target_pairs={{0,192},{32,224},{64,0},{96,32},{128,64},{160,96},{192,128},{224,1... | collective-permute-start | bytes 61448 | tf_op jit(solution)/shard_map/ppermute | solution.py:368
  40.6 1.0 %copy-start.3 = (bf16[2,256,320]{2,1,0:T(8,128)(2,1)S(1)}, bf16[2,256,320]{2,1,0:T(8,128)(2,1)}, u32[]{:S(2)}) copy-start(bf16[2,256,320]{2,1,0:T(8,128)(2,1)} %constant.12.clone.second_ref) | copy-start | bytes 983044
  41.6 1.0 %copy-start.4 = (bf16[2,256,320]{2,1,0:T(8,128)(2,1)S(1)}, bf16[2,256,320]{2,1,0:T(8,128)(2,1)}, u32[]{:S(2)}) copy-start(bf16[2,256,320]{2,1,0:T(8,128)(2,1)} %constant.14.clone.chosen_ref) | copy-start | bytes 983044
  42.6 1.0 %copy-start.5 = (bf16[2,320,256]{2,1,0:T(8,128)(2,1)S(1)}, bf16[2,320,256]{2,1,0:T(8,128)(2,1)}, u32[]{:S(2)}) copy-start(bf16[2,320,256]{2,1,0:T(8,128)(2,1)} %constant.13.clone.flipped_ref) | copy-start | bytes 983044
  43.6 0.9 %copy-start.6 = (bf16[2,256,256]{2,1,0:T(8,128)(2,1)S(1)}, bf16[2,256,256]{2,1,0:T(8,128)(2,1)}, u32[]{:S(2)}) copy-start(bf16[2,256,256]{2,1,0:T(8,128)(2,1)} %constant.11.clone.first_ref) | copy-start | bytes 786436
  44.5 0.7 copy-start.8
  45.2 28.2 %copy-start.1 = (f32[64,1024]{1,0:T(8,128)S(1)}, f32[64,1024]{1,0:T(8,128)}, u32[]{:S(2)}) copy-start(f32[64,1024]{1,0:T(8,128)} %weights_ref.1) | copy-start | bytes 786436
  45.2 28.2 %copy-start.2 = (bf16[2,256,256]{2,1,0:T(8,128)(2,1)S(1)}, bf16[2,256,256]{2,1,0:T(8,128)(2,1)}, u32[]{:S(2)}) copy-start(bf16[2,256,256]{2,1,0:T(8,128)(2,1)} %constant.10.clone.table_hbm.table_ref) | copy-start | bytes 786436
  45.2 28.2 %copy-start.7 = (s32[3,1024]{1,0:T(4,128)S(1)}, s32[3,1024]{1,0:T(4,128)}, u32[]{:S(2)}) copy-start(s32[3,1024]{1,0:T(4,128)} %anchors_ref.1) | copy-start | bytes 36868
  48.3 25.1 %all-to-all-start.1 = ((f32[256,1,384]{2,1,0:T(1,128)}), f32[256,1,384]{2,1,0:T(1,128)S(1)}, u32[]{:S(2)}, u32[]{:S(2)}) async-start(f32[256,1,384]{2,1,0:T(1,128)} %bitcast.5), calls=%async_computation.1 | async-start | bytes 786432 | tf_op jit(solution)/shard_map/all_to_all | solution.py:396
  54.9 12.9 %collective-permute-start.7 = (f32[24,128]{1,0:T(8,128)S(1)}, f32[24,128]{1,0:T(8,128)S(1)}, u32[]{:S(2)}, u32[]{:S(2)}) collective-permute-start(f32[24,128]{1,0:T(8,128)S(1)} %get-tuple-element.26.own_ref), channel_id=1, source_target_pairs={{0,1},{1,2},{2,3},{3,4},{4,5},{5,6},{6,7},{7,8},{8,9},{9,10},{10,1... | collective-permute-start | bytes 36872 | tf_op jit(solution)/shard_map/ppermute | solution.py:368
  56.4 11.3 %collective-permute-start.8 = (f32[24,128]{1,0:T(8,128)S(1)}, f32[24,128]{1,0:T(8,128)S(1)}, u32[]{:S(2)}, u32[]{:S(2)}) collective-permute-start(f32[24,128]{1,0:T(8,128)S(1)} %get-tuple-element.26.own_ref), channel_id=1, source_target_pairs={{0,31},{1,0},{2,1},{3,2},{4,3},{5,4},{6,5},{7,6},{8,7},{9,8},{10,9... | collective-permute-start | bytes 36872 | tf_op jit(solution)/shard_map/ppermute | solution.py:368

commit v3 on v2

v3 whole, which is shorter than its diff:
```python
import jax
import jax.numpy as jnp
import ml_dtypes
import numpy as np
from jax import lax
from jax.experimental import pallas as pl
from jax.experimental.pallas import tpu as pltpu
from jax.sharding import PartitionSpec as P

G = 256
ROWS = 8
COLS = 32
CELLS_A = 32
CELLS_B = 8
TRI = 1024
LINES_B = 10
MAIN = LINES_B * CELLS_A
BLOCKS = 12
LINES = BLOCKS * CELLS_A
SPREAD = MAIN + CELLS_A
LANES = 128
TILES = TRI // LANES
KEPT = CELLS_A // 2 + 1
SENT = 40
CHUNK = 256
GROUPS = ((0, 4, 8), (1, 5, 9), (2, 6), (3, 7))
F32 = jnp.float32
BF16 = jnp.bfloat16
BOTH = ("row", "col")
PARAMS = pltpu.CompilerParams(vmem_limit_bytes=48 * 1024 * 1024)


def split_table(table):
    high = table.astype(np.float32).astype(ml_dtypes.bfloat16)
    low = (table - high.astype(np.float64)).astype(np.float32).astype(ml_dtypes.bfloat16)
    return np.stack([high, low])


def cas(first, second):
    angle = (np.outer(first, second) % G) * (2.0 * np.pi / G)
    return np.cos(angle) + np.sin(angle)


def row_at(slot, block):
    return 4 * (slot // 4) + (slot - block) % 4


def tables():
    steps = np.arange(G)
    device = np.arange(ROWS * COLS)
    plane = CELLS_B * (device % COLS) + device // COLS
    along_a = (np.arange(G) - 1) % G
    order = np.concatenate([
        (CELLS_B * np.arange(COLS) - 1 + line) % G for group in GROUPS for line in group
    ])
    outer = np.zeros((G, G))
    for slot in range(ROWS):
        row = row_at(slot, LINES_B)
        for extra in range(2):
            cell = (CELLS_A * (row + 1) - 1 + extra) % G
            for line in range(LINES_B):
                outer[CELLS_A * slot + 2 * line + extra] = cas(np.array([cell]), steps)[0]
    folded = np.minimum(steps, G - steps)
    block, inside = folded // CELLS_A, folded % CELLS_A
    mirrored = inside >= KEPT
    owner = np.where(mirrored, ROWS - 1 - block, block)
    inside = np.where(mirrored, CELLS_A - inside, inside)
    chosen = np.zeros((2, G, ROWS * SENT), ml_dtypes.bfloat16)
    for half in range(2):
        chosen[half, steps, owner * SENT + half * KEPT + inside] = 1.0
    second = cas(steps, order)
    return {
        "lines": split_table(cas(plane, steps)),
        "chosen": chosen,
        "first": split_table(cas(along_a, steps)),
        "outer": split_table(outer),
        "second": split_table(second),
        "flipped": split_table(second.T),
    }


def halves(value):
    high = value.astype(BF16)
    low = (value - high.astype(F32)).astype(BF16)
    return high, low


def thirds(value):
    parts = []
    for _ in range(3):
        parts.append(value.astype(BF16))
        value = value - parts[-1].astype(F32)
    return parts


def dot(left, right, dims=((1,), (0,))):
    return lax.dot_general(left, right, (dims, ((), ())), preferred_element_type=F32)


def dot_split(left, right, dims=((1,), (0,))):
    left_high, left_low = left
    right_high, right_low = right
    cross = dot(left_high, right_low, dims) + dot(left_low, right_high, dims)
    return dot(left_high, right_high, dims) + cross


def block_place(block):
    slot = (lax.axis_index("row") + block) & 3
    return pl.ds(pl.multiple_of(LANES * (block // 4) + CELLS_A * slot, CELLS_A), CELLS_A)


def onehot(anchors_ref):
    cells = lax.broadcasted_iota(jnp.int32, (G, TRI), 0)
    matched = cells == anchors_ref[2:3, :]
    return jnp.where(matched, 1.0, 0.0).astype(BF16)


def local_place(anchors_ref, at):
    first = (anchors_ref[0:1, at] - (lax.axis_index("row") * CELLS_A - 1)) & (G - 1)
    second = (anchors_ref[1:2, at] - (lax.axis_index("col") * CELLS_B - 1)) & (G - 1)
    first = jnp.broadcast_to(first, (8, LANES))
    second = jnp.broadcast_to(second, (8, LANES))
    return lax.broadcasted_iota(jnp.int32, (8, LANES), 0) - (first & 7), first >> 3, second


def masks_of(place):
    relative, group, second = place
    near_masks = [relative == i for i in range(4)]
    next_masks = [relative == i - 8 for i in range(1, 4)]
    groups = [group == g for g in range(4)]
    bits = [(second & bit) != 0 for bit in (1, 2, 4)]
    return near_masks, next_masks, groups, bits


def two_rows(rows, near_masks, next_masks):
    near = jnp.zeros((8, LANES), F32)
    after = jnp.zeros((8, LANES), F32)
    for i in range(4):
        near = jnp.where(near_masks[i], rows[i], near)
    for i in range(1, 4):
        after = jnp.where(next_masks[i - 1], rows[i], after)
    return near, after


def stencil_rows(ref, j, k, at):
    return [
        jnp.broadcast_to(ref[16 * i + 4 * j + k, at][None, :], (8, LANES)) for i in range(4)
    ]


def spread_tile(scaled, place, spread, k, tile):
    at = pl.ds(tile * LANES, LANES)
    low_at = pl.ds(TRI + tile * LANES, LANES)
    zero = jnp.zeros((8, LANES), F32)
    near_masks, next_masks, groups, bits = masks_of(place)
    blocks = [two_rows(stencil_rows(scaled, j, k, at), near_masks, next_masks) for j in range(4)]
    for mask, shift, count in zip(bits, (1, 2, 4), (5, 7, 10)):
        wider = []
        for line in range(count):
            if line < shift:
                wider.append([jnp.where(mask, zero, low) for low in blocks[line]])
            elif line >= len(blocks):
                wider.append([jnp.where(mask, high, zero) for high in blocks[line - shift]])
            else:
                pairs = zip(blocks[line - shift], blocks[line])
                wider.append([jnp.where(mask, high, low) for high, low in pairs])
        blocks = wider
    extras = [zero] * 4
    for line in range(LINES_B):
        near, after = blocks[line]
        pieces = []
        for v in range(4):
            piece = jnp.where(groups[v], near, zero)
            pieces.append(jnp.where(groups[v - 1], after, piece) if v else piece)
        high, low = halves(jnp.concatenate(pieces, axis=0))
        rows = pl.ds(CELLS_A * line, CELLS_A)
        spread[k, rows, at] = high
        spread[k, rows, low_at] = low
        last = jnp.where(groups[3], after, zero)
        if line % 4:
            last = extras[line // 4] + pltpu.roll(last, 2 * (line % 4), 0)
        extras[line // 4] = last
    high, low = halves(jnp.concatenate(extras, axis=0))
    spread[k, pl.ds(MAIN, CELLS_A), at] = high
    spread[k, pl.ds(MAIN, CELLS_A), low_at] = low


def deposit_kernel(
    charges_hbm, anchors_hbm, weights_hbm, table_hbm, spectrum_hbm, out_ref, *rest
):
    sent_refs = rest[:ROWS]
    charges_ref, anchors_ref, weights_ref, table_ref, spectrum_ref = rest[ROWS : ROWS + 5]
    scaled, spread, lines, sem = rest[ROWS + 5 :]
    pairs = (
        (weights_hbm, weights_ref),
        (anchors_hbm, anchors_ref),
        (charges_hbm, charges_ref),
        (spectrum_hbm.at[pl.ds(0, CELLS_B * KEPT), pl.ds(0, LANES)], spectrum_ref.at[0]),
        (spectrum_hbm.at[pl.ds(0, CELLS_B * KEPT), pl.ds(LANES, LANES)], spectrum_ref.at[1]),
        (table_hbm, table_ref),
    )
    copies = [pltpu.make_async_copy(a, b, sem.at[n]) for n, (a, b) in enumerate(pairs)]
    for copy in copies:
        copy.start()
    for copy in copies:
        copy.wait()
    scaled[...] = weights_ref[...] * charges_ref[...]
    places = [local_place(anchors_ref, pl.ds(tile * LANES, LANES)) for tile in range(TILES)]
    hot = onehot(anchors_ref)
    hot = jnp.concatenate([hot, hot], axis=1)
    total = None
    for k in (1, 2, 3, 0):
        for tile in range(TILES):
            spread_tile(scaled, places[tile], spread, k, tile)
        placed = dot(spread[k], hot, ((1,), (1,)))
        placed = pltpu.roll(placed, k, 1) if k else placed
        total = placed if total is None else total + placed
    for block in range(LINES_B + 1):
        lines[block_place(block), :] = total[CELLS_A * block : CELLS_A * (block + 1)]
    lines[block_place(LINES_B + 1), :] = jnp.zeros((CELLS_A, G), F32)
    result = dot_split((table_ref[0], table_ref[1]), halves(lines[...]), ((1,), (1,)))
    for v in range(3):
        out_ref[pl.ds(v, G, stride=3), :] = result[:, LANES * v : LANES * (v + 1)]
    for shift, sent in enumerate(sent_refs):
        c = (lax.axis_index("row") + shift) & (ROWS - 1)
        sent[pl.ds(SENT - 8, 8), :] = jnp.zeros((8, LANES), F32)
        for half in range(2):
            rows = spectrum_ref[half, pl.ds(c, KEPT, stride=CELLS_B), :]
            sent[pl.ds(half * KEPT, KEPT), :] = rows
    for shift in (1, ROWS - 1):
        for block in range(8):
            at = pl.ds(block * LANES, LANES)
            sent_refs[shift][pl.ds(SENT + block, 1), :] = charges_ref[:, at]


def spectrum_kernel(charges_ref, chosen_hbm, *rest):
    tables_hbm, sent_refs = rest[:4], rest[4 : 4 + ROWS]
    out_ref, beside_ref = rest[4 + ROWS : 6 + ROWS]
    staged, (chosen_ref, joined, sem) = rest[6 + ROWS : 10 + ROWS], rest[10 + ROWS :]
    pairs = [(chosen_hbm, chosen_ref), *zip(tables_hbm, staged)]
    copies = [pltpu.make_async_copy(a, b, sem.at[n]) for n, (a, b) in enumerate(pairs)]
    for copy in copies:
        copy.start()
    for shift, sent in enumerate(sent_refs):
        owner = (lax.axis_index("row") - shift) & (ROWS - 1)
        at = pl.ds(pl.multiple_of(owner * SENT, 8), SENT)
        joined[at, :] = sent[pl.ds(0, SENT), :]
    beside_ref[pl.ds(0, 8), :] = sent_refs[1][pl.ds(SENT, 8), :]
    beside_ref[pl.ds(8, 8), :] = charges_ref[...]
    beside_ref[pl.ds(16, 8), :] = sent_refs[ROWS - 1][pl.ds(SENT, 8), :]
    for copy in copies:
        copy.wait()
    parts = thirds(joined[...])
    for half in range(2):
        value = sum(dot(chosen_ref[half], part) for part in parts)
        out_ref[:, pl.ds(LANES * half, LANES)] = value * (1.0 / (G * G * G))


def plane_kernel(tiles_ref, spectrum_ref, first_ref, outer_ref, second_ref, flipped_ref, out_ref):
    lane = lax.broadcasted_iota(jnp.int32, (CELLS_A, LANES), 1)
    slots = [(lane >> 5) == s for s in range(4)]
    wide = lax.broadcasted_iota(jnp.int32, (CELLS_A, G), 1)
    pairs = [((wide & 31) >> 1) == line for line in range(LINES_B)]
    pieces = [
        [tiles_ref[pl.ds(96 * r + v, CELLS_A, stride=3), :] for v in range(3)] for r in range(ROWS)
    ]

    def joined(block):
        parts = []
        for w in range(2):
            value = None
            for s in range(4):
                piece = pieces[4 * w + s][block // 4]
                value = piece if value is None else jnp.where(slots[(block + s) & 3], piece, value)
            parts.append(value)
        return jnp.concatenate(parts, axis=1)

    def table(m):
        order = [row_at(slot, m) for slot in range(ROWS)]
        both = []
        for part in range(2):
            rows = [first_ref[part, pl.ds(CELLS_A * r, CELLS_A), :] for r in order]
            both.append(jnp.concatenate([*rows, outer_ref[part]], axis=0))
        return both

    rim = joined(LINES_B)
    half = []
    for m, group in enumerate(GROUPS):
        rows = [
            jnp.concatenate([joined(line), jnp.where(pairs[line], rim, 0.0)], axis=1)
            for line in group
        ]
        half.append(dot_split(halves(jnp.concatenate(rows, axis=0)), table(m)))
    half = jnp.concatenate(half, axis=0)
    image = dot_split((second_ref[0], second_ref[1]), halves(half)) * spectrum_ref[...]
    half = dot_split((flipped_ref[0], flipped_ref[1]), halves(image))
    blocks, at = {}, 0
    for m, group in enumerate(GROUPS):
        size = CELLS_A * len(group)
        value = dot_split(halves(half[at : at + size]), table(m), ((1,), (1,)))
        for place, line in enumerate(group):
            blocks[line] = value[CELLS_A * place : CELLS_A * (place + 1)]
        at += size
    zero = jnp.zeros((CELLS_A, G), F32)
    rim = zero
    for line in range(LINES_B):
        rim = jnp.where(pairs[line], blocks[line][:, G:], rim)
    blocks[LINES_B], blocks[LINES_B + 1] = rim, zero
    for r in range(ROWS):
        lanes = slice(LANES * (r // 4), LANES * (r // 4 + 1))
        for v in range(3):
            value = None
            for block in range(4 * v, 4 * v + 4):
                piece = blocks[block][:, lanes]
                value = piece if value is None else jnp.where(slots[(block + r) & 3], piece, value)
            out_ref[pl.ds(96 * r + v, CELLS_A, stride=3), :] = value


def gather_tile(weights_ref, place, picked, tile, base, at):
    near_masks, next_masks, groups, bits = masks_of(place)
    weights_at = pl.ds(tile * LANES, LANES)
    total = jnp.zeros((8, LANES), F32)
    for k in range(4):
        blocks = []
        for line in range(LINES_B):
            start = SPREAD * k + CELLS_A * line
            rows = [picked[base, pl.ds(start + 8 * v, 8), at] for v in range(4)]
            last = picked[base, pl.ds(SPREAD * k + MAIN + 8 * (line // 4), 8), at]
            rows.append(pltpu.roll(last, 8 - 2 * (line % 4), 0) if line % 4 else last)
            pair = []
            for skip in range(2):
                chosen = rows[skip]
                for g in range(1, 4):
                    chosen = jnp.where(groups[g], rows[g + skip], chosen)
                pair.append(chosen)
            blocks.append(pair)
        for mask, shift, count in zip(bits[::-1], (4, 2, 1), (7, 5, 4)):
            fewer = []
            for line in range(count):
                low = blocks[line]
                if line + shift < len(blocks):
                    high = blocks[line + shift]
                    low = [jnp.where(mask, h, l) for h, l in zip(high, low)]
                fewer.append(low)
            blocks = fewer
        for j in range(4):
            rows = stencil_rows(weights_ref, j, k, weights_at)
            near, after = two_rows(rows, near_masks, next_masks)
            total = total + (near * blocks[j][0] + after * blocks[j][1])
    return jnp.sum(total, axis=0, keepdims=True)


def gather_kernel(
    field_ref, anchors_ref, weights_ref, table_ref, near_ref, out_ref, lines, parts, picked
):
    turned = [field_ref[pl.ds(v, G, stride=3), :].T for v in range(3)]
    turned = halves(jnp.concatenate(turned, axis=0))
    lines[...] = dot_split(turned, (table_ref[0], table_ref[1]))
    field = jnp.concatenate([lines[block_place(b), :] for b in range(LINES_B + 1)], axis=0)
    for k in range(4):
        high, low = halves(pltpu.roll(field, G - k, 1) if k else field)
        parts[pl.ds(SPREAD * k, SPREAD), pl.ds(0, G)] = high
        parts[pl.ds(SPREAD * k, SPREAD), pl.ds(G, G)] = low
    hot = onehot(anchors_ref)
    hot = jnp.concatenate([hot, hot], axis=0)
    for chunk in range(TRI // CHUNK):
        picked[chunk] = dot(parts[...], hot[:, CHUNK * chunk : CHUNK * (chunk + 1)])
        for step in range(CHUNK // LANES):
            tile = chunk * (CHUNK // LANES) + step
            at = pl.ds(tile * LANES, LANES)
            place = local_place(anchors_ref, at)
            value = gather_tile(
                weights_ref, place, picked, tile, chunk, pl.ds(step * LANES, LANES)
            )
            out_ref[:, at] = value + near_ref[:, at]


def near_kernel(
    count_ref, target_ref, source_ref, before_ref, own_ref, after_ref, tiles_ref, out_ref,
    charges_ref, total,
):
    step = pl.program_id(0)
    per_step, size = tiles_ref.shape[0], tiles_ref.shape[1]

    @pl.when(step == 0)
    def _():
        total[...] = jnp.zeros_like(total)
        for place, ref in enumerate((before_ref, own_ref, after_ref)):
            charges_ref[pl.ds(24 * place, 24), :] = ref[...]

    def slot(u, carry):
        place = step * per_step + u
        rows = pl.ds(pl.multiple_of(target_ref[place] * size, size), size)
        code = source_ref[place]
        neighbour = code >> 3
        row = neighbour // 3
        line = 24 * (neighbour - 3 * row) + 8 * row + (code & 7)
        source = charges_ref[pl.ds(line, 1), :]
        total[rows, :] = total[rows, :] + tiles_ref[u] * source
        return carry

    lax.fori_loop(0, jnp.clip(count_ref[0] - step * per_step, 0, per_step), slot, 0)

    @pl.when(step == pl.num_programs(0) - 1)
    def _():
        ones = jnp.ones((8, size), BF16)
        result = sum(dot(ones, part, ((1,), (1,))) for part in thirds(total[...]))
        out_ref[...] = result[0:1]


def shifted(value, axis, by):
    size = lax.axis_size(axis)
    return lax.ppermute(value, axis, [(i, (i + by) % size) for i in range(size)])


def near_field(beside, near_count, near_target, near_source, near_tiles):
    slots, size, _ = near_tiles.shape
    before, after = shifted(beside, "col", 1), shifted(beside, "col", -1)
    per_step = 8
    smem = pl.BlockSpec(memory_space=pltpu.SMEM)
    return pl.pallas_call(
        near_kernel,
        grid=(slots // per_step,),
        in_specs=[
            smem,
            smem,
            smem,
            *[pl.BlockSpec((24, size), lambda step: (0, 0))] * 3,
            pl.BlockSpec((per_step, size, size), lambda step: (step, 0, 0)),
        ],
        out_specs=pl.BlockSpec((1, TRI), lambda step: (0, 0)),
        out_shape=jax.ShapeDtypeStruct((1, TRI), F32),
        scratch_shapes=[pltpu.VMEM((72, size), F32), pltpu.VMEM((TRI, size), F32)],
        compiler_params=PARAMS,
        name="near",
    )(near_count, near_target, near_source, before, beside, after, near_tiles)


def exchange(values, axes, pieces):
    shaped = values.reshape(pieces, 1, values.size // pieces)
    moved = lax.all_to_all(shaped, axes, split_axis=0, concat_axis=0, tiled=True)
    return moved.reshape(values.shape)


def local(
    charges,
    anchors,
    stencil_weights,
    kernel_spectrum,
    near_count,
    near_target,
    near_source,
    near_tiles,
):
    table = {name: jnp.asarray(value) for name, value in tables().items()}
    devices = ROWS * COLS
    packed = jax.ShapeDtypeStruct((devices * LINES // LANES, LANES), F32)
    hbm = pl.BlockSpec(memory_space=pltpu.HBM)
    sizes = [SENT + 8 if shift in (1, ROWS - 1) else SENT for shift in range(ROWS)]
    deposited, *sent = pl.pallas_call(
        deposit_kernel,
        out_shape=(packed, *[jax.ShapeDtypeStruct((size, LANES), F32) for size in sizes]),
        in_specs=[hbm] * 5,
        scratch_shapes=[
            pltpu.VMEM((1, TRI), F32),
            pltpu.VMEM((3, TRI), jnp.int32),
            pltpu.VMEM((64, TRI), F32),
            pltpu.VMEM((2, G, G), BF16),
            pltpu.VMEM((2, CELLS_B * KEPT, LANES), F32),
            pltpu.VMEM((64, TRI), F32),
            pltpu.VMEM((4, SPREAD, 2 * TRI), BF16),
            pltpu.VMEM((LINES, G), F32),
            pltpu.SemaphoreType.DMA((6,)),
        ],
        compiler_params=PARAMS,
        name="deposit",
    )(
        *[
            pltpu.with_memory_space_constraint(value, pltpu.HBM)
            for value in (
                charges.reshape(1, TRI),
                anchors,
                stencil_weights,
                table["lines"],
                kernel_spectrum.reshape(CELLS_A * CELLS_B, G),
            )
        ]
    )
    received = exchange(deposited, BOTH, devices)
    sent = [shifted(value, "row", shift) if shift else value for shift, value in enumerate(sent)]
    vmem = pl.BlockSpec(memory_space=pltpu.VMEM)
    names = ("first", "outer", "second", "flipped")
    spectrum, beside, *staged = pl.pallas_call(
        spectrum_kernel,
        out_shape=(
            jax.ShapeDtypeStruct((G, G), F32),
            jax.ShapeDtypeStruct((24, LANES), F32),
            *[jax.ShapeDtypeStruct(table[name].shape, BF16) for name in names],
        ),
        in_specs=[vmem, *[hbm] * 5, *[vmem] * ROWS],
        scratch_shapes=[
            pltpu.VMEM(table["chosen"].shape, BF16),
            pltpu.VMEM((ROWS * SENT, LANES), F32),
            pltpu.SemaphoreType.DMA((5,)),
        ],
        compiler_params=PARAMS,
        name="spectrum",
    )(
        charges.reshape(8, LANES),
        *[
            pltpu.with_memory_space_constraint(table[name], pltpu.HBM)
            for name in ("chosen", *names)
        ],
        *sent,
    )
    handed = pl.pallas_call(
        plane_kernel, out_shape=packed, compiler_params=PARAMS, name="plane"
    )(received, spectrum, *staged)
    field = exchange(handed, BOTH, devices)
    beside, _ = lax.optimization_barrier((beside, handed))
    near = near_field(beside, near_count, near_target, near_source, near_tiles)
    result = pl.pallas_call(
        gather_kernel,
        out_shape=jax.ShapeDtypeStruct((1, TRI), F32),
        scratch_shapes=[
            pltpu.VMEM((LINES, G), F32),
            pltpu.VMEM((4 * SPREAD, 2 * G), BF16),
            pltpu.VMEM((TRI // CHUNK, 4 * SPREAD, CHUNK), F32),
        ],
        compiler_params=PARAMS,
        name="gather",
    )(field, anchors, stencil_weights, table["lines"], near)
    return result.reshape(TRI)


def solution(mesh):
    return jax.shard_map(
        local,
        mesh=mesh,
        in_specs=(
            P(("row", "col")),
            P(None, ("row", "col")),
            P(None, ("row", "col")),
            P("row", "col", None),
            P(("row", "col")),
            P(("row", "col")),
            P(("row", "col")),
            P(("row", "col"), None, None),
        ),
        out_specs=P(("row", "col")),
        check_vma=False,
    )
```

time: 77.8 us -> 80.7 us (1.037)
  waiting for transfers between devices: 18.3 us -> 12.6 us
  starting transfers between devices: 38.5 us -> 44 us
  local copies, waits for them, and re-layouts: 4.62 us -> 7.34 us
    all_to_all x2, waiting for transfers between devices: 10.2 us -> 4.53 us  [exchange(): lax.all_to_all(shaped, axes, split_axis=0, concat_axis=0, tiled=True)]
    all_to_all x2, starting transfers between devices: 22.2 us -> 27.7 us  [exchange(): lax.all_to_all(shaped, axes, split_axis=0, concat_axis=0, tiled=True)]
    unnamed x22 -> x30, local copies, waits for them, and re-layouts: 4.62 us -> 7.34 us
    pallas_call x1 -> x2, Pallas kernels: 3.09 us -> 5.12 us  [the longest x1 3.09 us: local(): pl.pallas_call(plane_kernel, out_shape=packed, compiler_params=PARAMS, na...]
    pallas_call x1, Pallas kernels: 4.05 us -> 3.05 us  [local(): pl.pallas_call(gather_kernel, out_shape=jax.ShapeDtypeStruct((1, TRI), F3...]
    pallas_call x1, Pallas kernels: 6.52 us -> 5.64 us  [local(): pl.pallas_call(deposit_kernel, out_shape=(packed, *[jax.ShapeDtypeStruct(...]
  transfers between devices with their start and end apart: 11 -> 11, of which waited for: 6 -> 6; matrix products, arithmetic and copies ran while one was open for 0% -> 0% of each run, Pallas kernels for 2% -> 5%
where the time goes in v3:
time: 80.7 us; the launch traced here: 80.4 us
  starting transfers between devices  44 us (55%)
  Pallas kernels  15.7 us (19%)
  waiting for transfers between devices  12.6 us (16%)
  local copies, waits for them, and re-layouts  7.34 us (9%)
    all_to_all x2, starting transfers between devices, exchange(): lax.all_to_all(shaped, axes, split_axis=0, concat_axis=0, tiled=True)  27.7 us
    ppermute x9, starting transfers between devices, shifted(): lax.ppermute(value, axis, [(i, (i + by) % size) for i in range(size)])  16.3 us
    ppermute x9, waiting for transfers between devices, shifted(): lax.ppermute(value, axis, [(i, (i + by) % size) for i in range(size)])  8.08 us
    unnamed x30, local copies, waits for them, and re-layouts  7.34 us
    pallas_call x1, Pallas kernels, local(): pl.pallas_call(deposit_kernel, out_shape=(packed, *[jax.ShapeDtypeStruct(...  5.64 us
    all_to_all x2, waiting for transfers between devices, exchange(): lax.all_to_all(shaped, axes, split_axis=0, concat_axis=0, tiled=True)  4.53 us
    pallas_call x1, Pallas kernels, local(): pl.pallas_call(plane_kernel, out_shape=packed, compiler_params=PARAMS, na...  3.09 us
    pallas_call x1, Pallas kernels, local(): pl.pallas_call(gather_kernel, out_shape=jax.ShapeDtypeStruct((1, TRI), F3...  3.05 us
  transfers between devices with their start and end apart: 11, of which 6 were waited for; matrix products, arithmetic and copies ran while one was open for 0% of the time, Pallas kernels for 5%

profile of v3, /device:TPU:1, one launch (start us, length us, event | category | flops | bytes accessed | tf_op | source)
XLA Modules:
  0.0 80.4 jit_solution(4245561699948400537)
XLA Ops:
  0.0 5.6 %deposit.1 = (f32[768,128]{1,0:T(8,128)}, f32[40,128]{1,0:T(8,128)S(1)}, f32[48,128]{1,0:T(8,128)S(1)}, f32[40,128]{1,0:T(8,128)S(1)}, f32[40,128]{1,0:T(8,128)S...) custom-call(f32[1,1024]{1,0:T(1,128)} %bitcast.10, ...), custom_call_target="tpu_custom_call" | custom-call | tf_op jit(solution)/shard_map/deposit/pallas_call | solution.py:460
  5.7 15.7 %all-to-all-start = ((f32[256,1,384]{2,1,0:T(1,128)}), f32[256,1,384]{2,1,0:T(1,128)S(1)}, u32[]{:S(2)}, u32[]{:S(2)}) async-start(f32[256,1,384]{2,1,0:T(1,128)} %bitcast.2), calls=%async_computation | async-start | bytes 786432 | tf_op jit(solution)/shard_map/all_to_all | solution.py:441
  21.3 1.5 %collective-permute-start.1 = (f32[40,128]{1,0:T(8,128)S(1)}, f32[40,128]{1,0:T(8,128)S(1)}, u32[]{:S(2)}, u32[]{:S(2)}) collective-permute-start(f32[40,128]{1,0:T(8,128)S(1)} %get-tuple-element.24), channel_id=1, source_target_pairs={{0,64},{32,96},{64,128},{96,160},{128,192},{160,224},{192,0},{224,... | collective-permute-start | bytes 61448 | tf_op jit(solution)/shard_map/ppermute | solution.py:413
  22.8 3.0 %collective-permute-start.2 = (f32[40,128]{1,0:T(8,128)S(1)}, f32[40,128]{1,0:T(8,128)S(1)}, u32[]{:S(2)}, u32[]{:S(2)}) collective-permute-start(f32[40,128]{1,0:T(8,128)S(1)} %get-tuple-element.25), channel_id=1, source_target_pairs={{0,96},{32,128},{64,160},{96,192},{128,224},{160,0},{192,32},{224,... | collective-permute-start | bytes 61448 | tf_op jit(solution)/shard_map/ppermute | solution.py:413
  25.8 0.0 collective-permute-start
  25.8 0.5 collective-permute-start.6
  26.3 1.3 %collective-permute-start.3 = (f32[40,128]{1,0:T(8,128)S(1)}, f32[40,128]{1,0:T(8,128)S(1)}, u32[]{:S(2)}, u32[]{:S(2)}) collective-permute-start(f32[40,128]{1,0:T(8,128)S(1)} %get-tuple-element.26), channel_id=1, source_target_pairs={{0,128},{32,160},{64,192},{96,224},{128,0},{160,32},{192,64},{224,... | collective-permute-start | bytes 61448 | tf_op jit(solution)/shard_map/ppermute | solution.py:413
  27.6 0.0 collective-permute-done.1.rest_6_
  27.6 2.6 %collective-permute-start.4 = (f32[40,128]{1,0:T(8,128)S(1)}, f32[40,128]{1,0:T(8,128)S(1)}, u32[]{:S(2)}, u32[]{:S(2)}) collective-permute-start(f32[40,128]{1,0:T(8,128)S(1)} %get-tuple-element.27), channel_id=1, source_target_pairs={{0,160},{32,192},{64,224},{96,0},{128,32},{160,64},{192,96},{224,1... | collective-permute-start | bytes 61448 | tf_op jit(solution)/shard_map/ppermute | solution.py:413
  30.2 0.0 collective-permute-done.2.rest_7_
  30.2 0.6 collective-permute-start.5
  30.8 0.1 collective-permute-done.3.rest_8_
  30.8 2.0 %collective-permute-done.4.rest_9_ = f32[40,128]{1,0:T(8,128)S(1)} collective-permute-done((f32[40,128]{1,0:T(8,128)S(1)}, f32[40,128]{1,0:T(8,128)S(1)}, u32[]{:S(2)}, u32[]{:S(2)}) %collective-permute-start.4) | collective-permute-done | bytes 20512 | tf_op jit(solution)/shard_map/ppermute | solution.py:413
  32.8 0.7 collective-permute-done.5.rest_10_
  33.5 0.0 collective-permute-done.rest_5_
  33.5 0.0 collective-permute-done.6.rest_11_
  33.5 0.0 copy-start.13
  33.5 0.0 copy-start.14
  33.5 0.0 copy-start.12
  33.5 0.7 copy-done.12
  34.2 0.0 copy-start
  34.2 2.0 %spectrum.1 = (f32[256,256]{1,0:T(8,128)S(1)}, f32[24,128]{1,0:T(8,128)S(1)}, bf16[2,256,256]{2,1,0:T(8,128)(2,1)S(1)}, bf16[2,256,256]{2,1,0:T(8,128)(2,1)S(1)}...) custom-call(f32[8,128]{1,0:T(8,128)S(1)} %bitcast.11, ...), custom_call_target="tpu_custom_call" | custom-call | tf_op jit(solution)/shard_map/spectrum/pallas_call | solution.py:493
  36.2 0.0 copy-start.3
  36.2 0.7 copy-done.3
  37.0 0.0 copy-start.5
  37.0 0.7 copy-done.5
  37.7 0.7 copy-done.7
  38.4 0.7 copy-done.9
  39.0 0.7 all-to-all-done
  39.8 1.0 %copy-done.4 = bf16[2,320,256]{2,1,0:T(8,128)(2,1)S(1)} copy-done((bf16[2,320,256]{2,1,0:T(8,128)(2,1)S(1)}, bf16[2,320,256]{2,1,0:T(8,128)(2,1)}, u32[]{:S(2)}) %copy-start.4) | copy-done | bytes 327704
  40.7 0.9 %copy-done.6 = f32[256,256]{1,0:T(8,128)S(1)} copy-done((f32[256,256]{1,0:T(8,128)S(1)}, f32[256,256]{1,0:T(8,128)}, u32[]{:S(2)}) %copy-start.6) | copy-done | bytes 262168
  41.7 0.9 %copy-done.8 = bf16[2,256,256]{2,1,0:T(8,128)(2,1)S(1)} copy-done((bf16[2,256,256]{2,1,0:T(8,128)(2,1)S(1)}, bf16[2,256,256]{2,1,0:T(8,128)(2,1)}, u32[]{:S(2)}) %copy-start.8) | copy-done | bytes 262168
  42.6 0.9 %copy-done.10 = bf16[2,256,256]{2,1,0:T(8,128)(2,1)S(1)} copy-done((bf16[2,256,256]{2,1,0:T(8,128)(2,1)S(1)}, bf16[2,256,256]{2,1,0:T(8,128)(2,1)}, u32[]{:S(2)}) %copy-start.10) | copy-done | bytes 262168
  43.6 3.1 %plane.1 = f32[768,128]{1,0:T(8,128)} custom-call(f32[768,128]{1,0:T(8,128)S(1)} %bitcast.8, f32[256,256]{1,0:T(8,128)S(1)} %copy-done.6, bf16[2,256,256]{2,1,0:T(8,128)(2,1)S(1)} %copy-done.8, bf16[2,256,256]{2,1,0:T(8,128)(2,1)S(1)} %copy-done.10, bf16[2,256,320]{2,1,0:T(8,128)(2,1)S(1)} %get-tuple-element.33.second_ref, bf16[2,320,256]{2,1,0:T(8,128)(2,1)S(1)} %copy-done.4), custom_call_target="tpu_custom_call" | custom-call | tf_op jit(solution)/shard_map/plane/pallas_call | solution.py:516
  46.7 12.1 %all-to-all-start.1 = ((f32[256,1,384]{2,1,0:T(1,128)}), f32[256,1,384]{2,1,0:T(1,128)S(1)}, u32[]{:S(2)}, u32[]{:S(2)}) async-start(f32[256,1,384]{2,1,0:T(1,128)} %bitcast.5), calls=%async_computation.1 | async-start | bytes 786432 | tf_op jit(solution)/shard_map/all_to_all | solution.py:441
  58.7 1.6 %collective-permute-start.7 = (f32[24,128]{1,0:T(8,128)S(1)}, f32[24,128]{1,0:T(8,128)S(1)}, u32[]{:S(2)}, u32[]{:S(2)}) collective-permute-start(f32[24,128]{1,0:T(8,128)S(1)} %get-tuple-element.36.own_ref), channel_id=1, source_target_pairs={{0,1},{1,2},{2,3},{3,4},{4,5},{5,6},{6,7},{7,8},{8,9},{9,10},{10,1... | collective-permute-start | bytes 36872 | tf_op jit(solution)/shard_map/ppermute | solution.py:413
  60.3 5.3 %collective-permute-start.8 = (f32[24,128]{1,0:T(8,128)S(1)}, f32[24,128]{1,0:T(8,128)S(1)}, u32[]{:S(2)}, u32[]{:S(2)}) collective-permute-start(f32[24,128]{1,0:T(8,128)S(1)} %get-tuple-element.36.own_ref), channel_id=1, source_target_pairs={{0,31},{1,0},{2,1},{3,2},{4,3},{5,4},{6,5},{7,6},{8,7},{9,8},{10,9... | collective-permute-start | bytes 36872 | tf_op jit(solution)/shard_map/ppermute | solution.py:413
  66.2 5.3 %collective-permute-done.7.before_ref = f32[24,128]{1,0:T(8,128)S(1)} collective-permute-done((f32[24,128]{1,0:T(8,128)S(1)}, f32[24,128]{1,0:T(8,128)S(1)}, u32[]{:S(2)}, u32[]{:S(2)}) %collective-permute-start.7) | collective-permute-done | bytes 12320 | tf_op jit(solution)/shard_map/ppermute | solution.py:413
  71.6 0.0 collective-permute-done.8.after_ref
  71.6 0.0 copy-done.13
  71.6 0.0 copy-done.14
  71.6 0.0 copy-done
  71.6 1.9 %near.1.near_ref = f32[1,1024]{1,0:T(1,128)S(1)} custom-call(s32[1]{0:T(128)S(6)} %copy.17.count_ref, s32[32]{0:T(128)S(1)} %copy-done.13, s32[32]{0:T(128)S(1)} %copy-done.14, f32[24,128]{1,0:T(8,128)S(1)} %collective-permute-done.7.before_ref, f32[24,128]{1,0:T(8,128)S(1)} %get-tuple-element.36.own_ref, f32[24,128]{1,0:T(8,128)S(1)} %collective-permute-done.8.after_ref, ...), custom_call_target="tpu_custom_call" | custom-call | tf_op jit(solution)/shard_map/near/pallas_call | solution.py:421
  73.5 3.8 %all-to-all-done.1 = f32[256,1,384]{2,1,0:T(1,128)S(1)} async-done(((f32[256,1,384]{2,1,0:T(1,128)}), f32[256,1,384]{2,1,0:T(1,128)S(1)}, u32[]{:S(2)}, u32[]{:S(2)}) %all-to-all-start.1) | async-done | bytes 393248 | tf_op jit(solution)/shard_map/all_to_all | solution.py:441
  77.3 0.0 copy-done.1
  77.3 0.0 copy-done.2
  77.3 0.0 copy-done.11
  77.3 3.1 %gather.1 = f32[1,1024]{1,0:T(1,128)} custom-call(f32[768,128]{1,0:T(8,128)S(1)} %bitcast.9, s32[3,1024]{1,0:T(4,128)S(1)} %copy-done.11, f32[64,1024]{1,0:T(8,128)S(1)} %copy-done.1, bf16[2,256,256]{2,1,0:T(8,128)(2,1)S(1)} %copy-done.2, f32[1,1024]{1,0:T(1,128)S(1)} %near.1.near_ref), custom_call_target="tpu_custom_call" | custom-call | tf_op jit(solution)/shard_map/gather/pallas_call | solution.py:522
  (9 shorter events, 0.0 us)
Async XLA Ops:
  5.7 34.1 %all-to-all-start = ((f32[256,1,384]{2,1,0:T(1,128)}), f32[256,1,384]{2,1,0:T(1,128)S(1)}, u32[]{:S(2)}, u32[]{:S(2)}) async-start(f32[256,1,384]{2,1,0:T(1,128)} %bitcast.2), calls=%async_computation | async-start | bytes 786432 | tf_op jit(solution)/shard_map/all_to_all | solution.py:441
  21.3 6.3 %collective-permute-start.1 = (f32[40,128]{1,0:T(8,128)S(1)}, f32[40,128]{1,0:T(8,128)S(1)}, u32[]{:S(2)}, u32[]{:S(2)}) collective-permute-start(f32[40,128]{1,0:T(8,128)S(1)} %get-tuple-element.24), channel_id=1, source_target_pairs={{0,64},{32,96},{64,128},{96,160},{128,192},{160,224},{192,0},{224,... | collective-permute-start | bytes 61448 | tf_op jit(solution)/shard_map/ppermute | solution.py:413
  22.8 7.4 %collective-permute-start.2 = (f32[40,128]{1,0:T(8,128)S(1)}, f32[40,128]{1,0:T(8,128)S(1)}, u32[]{:S(2)}, u32[]{:S(2)}) collective-permute-start(f32[40,128]{1,0:T(8,128)S(1)} %get-tuple-element.25), channel_id=1, source_target_pairs={{0,96},{32,128},{64,160},{96,192},{128,224},{160,0},{192,32},{224,... | collective-permute-start | bytes 61448 | tf_op jit(solution)/shard_map/ppermute | solution.py:413
  25.8 7.7 %collective-permute-start = (f32[48,128]{1,0:T(8,128)S(1)}, f32[48,128]{1,0:T(8,128)S(1)}, u32[]{:S(2)}, u32[]{:S(2)}) collective-permute-start(f32[48,128]{1,0:T(8,128)S(1)} %get-tuple-element.23), channel_id=1, source_target_pairs={{0,32},{32,64},{64,96},{96,128},{128,160},{160,192},{192,224},{224... | collective-permute-start | bytes 73736 | tf_op jit(solution)/shard_map/ppermute | solution.py:413
  25.8 7.7 %collective-permute-start.6 = (f32[48,128]{1,0:T(8,128)S(1)}, f32[48,128]{1,0:T(8,128)S(1)}, u32[]{:S(2)}, u32[]{:S(2)}) collective-permute-start(f32[48,128]{1,0:T(8,128)S(1)} %get-tuple-element.29), channel_id=1, source_target_pairs={{0,224},{32,0},{64,32},{96,64},{128,96},{160,128},{192,160},{224,1... | collective-permute-start | bytes 73736 | tf_op jit(solution)/shard_map/ppermute | solution.py:413
  26.3 4.5 %collective-permute-start.3 = (f32[40,128]{1,0:T(8,128)S(1)}, f32[40,128]{1,0:T(8,128)S(1)}, u32[]{:S(2)}, u32[]{:S(2)}) collective-permute-start(f32[40,128]{1,0:T(8,128)S(1)} %get-tuple-element.26), channel_id=1, source_target_pairs={{0,128},{32,160},{64,192},{96,224},{128,0},{160,32},{192,64},{224,... | collective-permute-start | bytes 61448 | tf_op jit(solution)/shard_map/ppermute | solution.py:413
  27.6 5.2 %collective-permute-start.4 = (f32[40,128]{1,0:T(8,128)S(1)}, f32[40,128]{1,0:T(8,128)S(1)}, u32[]{:S(2)}, u32[]{:S(2)}) collective-permute-start(f32[40,128]{1,0:T(8,128)S(1)} %get-tuple-element.27), channel_id=1, source_target_pairs={{0,160},{32,192},{64,224},{96,0},{128,32},{160,64},{192,96},{224,1... | collective-permute-start | bytes 61448 | tf_op jit(solution)/shard_map/ppermute | solution.py:413
  30.2 3.3 %collective-permute-start.5 = (f32[40,128]{1,0:T(8,128)S(1)}, f32[40,128]{1,0:T(8,128)S(1)}, u32[]{:S(2)}, u32[]{:S(2)}) collective-permute-start(f32[40,128]{1,0:T(8,128)S(1)} %get-tuple-element.28), channel_id=1, source_target_pairs={{0,192},{32,224},{64,0},{96,32},{128,64},{160,96},{192,128},{224,1... | collective-permute-start | bytes 61448 | tf_op jit(solution)/shard_map/ppermute | solution.py:413
  33.5 38.1 %copy-start.13 = (s32[32]{0:T(128)S(1)}, s32[32]{0:T(128)}, u32[]{:S(2)}) copy-start(s32[32]{0:T(128)} %target_ref.1) | copy-start | bytes 388
  33.5 38.1 %copy-start.14 = (s32[32]{0:T(128)S(1)}, s32[32]{0:T(128)}, u32[]{:S(2)}) copy-start(s32[32]{0:T(128)} %source_ref.1) | copy-start | bytes 388
  33.5 0.7 copy-start.12
  34.2 37.4 %copy-start = (f32[32,128,128]{2,1,0:T(8,128)S(1)}, f32[32,128,128]{2,1,0:T(8,128)}, u32[]{:S(2)}) copy-start(f32[32,128,128]{2,1,0:T(8,128)} %tiles_ref.1) | copy-start | bytes 6291460
  36.2 0.7 copy-start.3
  37.0 0.7 copy-start.5
  37.7 0.7 copy-start.7
  38.4 0.7 copy-start.9
  39.7 1.0 %copy-start.4 = (bf16[2,320,256]{2,1,0:T(8,128)(2,1)S(1)}, bf16[2,320,256]{2,1,0:T(8,128)(2,1)}, u32[]{:S(2)}) copy-start(bf16[2,320,256]{2,1,0:T(8,128)(2,1)} %copy-done.3) | copy-start | bytes 983044
  40.7 0.9 %copy-start.6 = (f32[256,256]{1,0:T(8,128)S(1)}, f32[256,256]{1,0:T(8,128)}, u32[]{:S(2)}) copy-start(f32[256,256]{1,0:T(8,128)} %copy-done.5) | copy-start | bytes 786436
  41.7 0.9 %copy-start.8 = (bf16[2,256,256]{2,1,0:T(8,128)(2,1)S(1)}, bf16[2,256,256]{2,1,0:T(8,128)(2,1)}, u32[]{:S(2)}) copy-start(bf16[2,256,256]{2,1,0:T(8,128)(2,1)} %copy-done.7) | copy-start | bytes 786436
  42.6 0.9 %copy-start.10 = (bf16[2,256,256]{2,1,0:T(8,128)(2,1)S(1)}, bf16[2,256,256]{2,1,0:T(8,128)(2,1)}, u32[]{:S(2)}) copy-start(bf16[2,256,256]{2,1,0:T(8,128)(2,1)} %copy-done.9) | copy-start | bytes 786436
  43.6 33.7 %copy-start.1 = (f32[64,1024]{1,0:T(8,128)S(1)}, f32[64,1024]{1,0:T(8,128)}, u32[]{:S(2)}) copy-start(f32[64,1024]{1,0:T(8,128)} %weights_ref.1) | copy-start | bytes 786436
  43.6 33.7 %copy-start.2 = (bf16[2,256,256]{2,1,0:T(8,128)(2,1)S(1)}, bf16[2,256,256]{2,1,0:T(8,128)(2,1)}, u32[]{:S(2)}) copy-start(bf16[2,256,256]{2,1,0:T(8,128)(2,1)} %constant.12.clone.table_hbm.table_ref) | copy-start | bytes 786436
  43.6 33.7 %copy-start.11 = (s32[3,1024]{1,0:T(4,128)S(1)}, s32[3,1024]{1,0:T(4,128)}, u32[]{:S(2)}) copy-start(s32[3,1024]{1,0:T(4,128)} %anchors_ref.1) | copy-start | bytes 36868
  46.7 30.6 %all-to-all-start.1 = ((f32[256,1,384]{2,1,0:T(1,128)}), f32[256,1,384]{2,1,0:T(1,128)S(1)}, u32[]{:S(2)}, u32[]{:S(2)}) async-start(f32[256,1,384]{2,1,0:T(1,128)} %bitcast.5), calls=%async_computation.1 | async-start | bytes 786432 | tf_op jit(solution)/shard_map/all_to_all | solution.py:441
  58.7 12.8 %collective-permute-start.7 = (f32[24,128]{1,0:T(8,128)S(1)}, f32[24,128]{1,0:T(8,128)S(1)}, u32[]{:S(2)}, u32[]{:S(2)}) collective-permute-start(f32[24,128]{1,0:T(8,128)S(1)} %get-tuple-element.36.own_ref), channel_id=1, source_target_pairs={{0,1},{1,2},{2,3},{3,4},{4,5},{5,6},{6,7},{7,8},{8,9},{9,10},{10,1... | collective-permute-start | bytes 36872 | tf_op jit(solution)/shard_map/ppermute | solution.py:413
  60.3 11.3 %collective-permute-start.8 = (f32[24,128]{1,0:T(8,128)S(1)}, f32[24,128]{1,0:T(8,128)S(1)}, u32[]{:S(2)}, u32[]{:S(2)}) collective-permute-start(f32[24,128]{1,0:T(8,128)S(1)} %get-tuple-element.36.own_ref), channel_id=1, source_target_pairs={{0,31},{1,0},{2,1},{3,2},{4,3},{5,4},{6,5},{7,6},{8,7},{9,8},{10,9... | collective-permute-start | bytes 36872 | tf_op jit(solution)/shard_map/ppermute | solution.py:413

commit v4 on v3

--- a/solution.py
+++ b/solution.py
@@ -27,7 +27,10 @@
 F32 = jnp.float32
 BF16 = jnp.bfloat16
 BOTH = ("row", "col")
-PARAMS = pltpu.CompilerParams(vmem_limit_bytes=48 * 1024 * 1024)
+
+
+def params(mebibytes):
+    return pltpu.CompilerParams(vmem_limit_bytes=mebibytes * 1024 * 1024)
 
 
 def split_table(table):
@@ -60,18 +63,9 @@
             cell = (CELLS_A * (row + 1) - 1 + extra) % G
             for line in range(LINES_B):
                 outer[CELLS_A * slot + 2 * line + extra] = cas(np.array([cell]), steps)[0]
-    folded = np.minimum(steps, G - steps)
-    block, inside = folded // CELLS_A, folded % CELLS_A
-    mirrored = inside >= KEPT
-    owner = np.where(mirrored, ROWS - 1 - block, block)
-    inside = np.where(mirrored, CELLS_A - inside, inside)
-    chosen = np.zeros((2, G, ROWS * SENT), ml_dtypes.bfloat16)
-    for half in range(2):
-        chosen[half, steps, owner * SENT + half * KEPT + inside] = 1.0
     second = cas(steps, order)
     return {
         "lines": split_table(cas(plane, steps)),
-        "chosen": chosen,
         "first": split_table(cas(along_a, steps)),
         "outer": split_table(outer),
         "second": split_table(second),
@@ -227,36 +221,42 @@
         for half in range(2):
             rows = spectrum_ref[half, pl.ds(c, KEPT, stride=CELLS_B), :]
             sent[pl.ds(half * KEPT, KEPT), :] = rows
-    for shift in (1, ROWS - 1):
+    for shift in (0, 1, ROWS - 1):
         for block in range(8):
             at = pl.ds(block * LANES, LANES)
             sent_refs[shift][pl.ds(SENT + block, 1), :] = charges_ref[:, at]
 
 
-def spectrum_kernel(charges_ref, chosen_hbm, *rest):
-    tables_hbm, sent_refs = rest[:4], rest[4 : 4 + ROWS]
-    out_ref, beside_ref = rest[4 + ROWS : 6 + ROWS]
-    staged, (chosen_ref, joined, sem) = rest[6 + ROWS : 10 + ROWS], rest[10 + ROWS :]
-    pairs = [(chosen_hbm, chosen_ref), *zip(tables_hbm, staged)]
-    copies = [pltpu.make_async_copy(a, b, sem.at[n]) for n, (a, b) in enumerate(pairs)]
-    for copy in copies:
-        copy.start()
+def spectrum_kernel(*refs):
+    sent_refs, (out_ref, beside_ref, joined) = refs[:ROWS], refs[ROWS:]
     for shift, sent in enumerate(sent_refs):
         owner = (lax.axis_index("row") - shift) & (ROWS - 1)
         at = pl.ds(pl.multiple_of(owner * SENT, 8), SENT)
         joined[at, :] = sent[pl.ds(0, SENT), :]
-    beside_ref[pl.ds(0, 8), :] = sent_refs[1][pl.ds(SENT, 8), :]
-    beside_ref[pl.ds(8, 8), :] = charges_ref[...]
-    beside_ref[pl.ds(16, 8), :] = sent_refs[ROWS - 1][pl.ds(SENT, 8), :]
-    for copy in copies:
-        copy.wait()
+    for place, shift in enumerate((1, 0, ROWS - 1)):
+        beside_ref[pl.ds(8 * place, 8), :] = sent_refs[shift][pl.ds(SENT, 8), :]
+    line = lax.broadcasted_iota(jnp.int32, (G, ROWS * SENT), 0)
+    folded = jnp.minimum(line, G - line)
+    block, inside = folded >> 5, folded & (CELLS_A - 1)
+    mirrored = inside >= KEPT
+    owner = jnp.where(mirrored, ROWS - 1 - block, block)
+    inside = jnp.where(mirrored, CELLS_A - inside, inside)
+    place = lax.broadcasted_iota(jnp.int32, (G, ROWS * SENT), 1) - (owner * SENT + inside)
     parts = thirds(joined[...])
     for half in range(2):
-        value = sum(dot(chosen_ref[half], part) for part in parts)
+        chosen = jnp.where(place == half * KEPT, 1.0, 0.0).astype(BF16)
+        value = sum(dot(chosen, part) for part in parts)
         out_ref[:, pl.ds(LANES * half, LANES)] = value * (1.0 / (G * G * G))
 
 
-def plane_kernel(tiles_ref, spectrum_ref, first_ref, outer_ref, second_ref, flipped_ref, out_ref):
+def plane_kernel(tiles_ref, spectrum_ref, *rest):
+    tables_hbm, out_ref, tables_ref, sem = rest[:4], rest[4], rest[5:9], rest[9]
+    first_ref, outer_ref, second_ref, flipped_ref = tables_ref
+    copies = [
+        pltpu.make_async_copy(a, b, sem.at[n]) for n, (a, b) in enumerate(zip(tables_hbm, tables_ref))
+    ]
+    for copy in copies:
+        copy.start()
     lane = lax.broadcasted_iota(jnp.int32, (CELLS_A, LANES), 1)
     slots = [(lane >> 5) == s for s in range(4)]
     wide = lax.broadcasted_iota(jnp.int32, (CELLS_A, G), 1)
@@ -285,14 +285,19 @@
 
     rim = joined(LINES_B)
     half = []
-    for m, group in enumerate(GROUPS):
+    for group in GROUPS:
         rows = [
             jnp.concatenate([joined(line), jnp.where(pairs[line], rim, 0.0)], axis=1)
             for line in group
         ]
-        half.append(dot_split(halves(jnp.concatenate(rows, axis=0)), table(m)))
-    half = jnp.concatenate(half, axis=0)
-    image = dot_split((second_ref[0], second_ref[1]), halves(half)) * spectrum_ref[...]
+        half.append(halves(jnp.concatenate(rows, axis=0)))
+    copies[0].wait()
+    copies[1].wait()
+    half = [dot_split(rows, table(m)) for m, rows in enumerate(half)]
+    half = halves(jnp.concatenate(half, axis=0))
+    copies[2].wait()
+    image = dot_split((second_ref[0], second_ref[1]), half) * spectrum_ref[...]
+    copies[3].wait()
     half = dot_split((flipped_ref[0], flipped_ref[1]), halves(image))
     blocks, at = {}, 0
     for m, group in enumerate(GROUPS):
@@ -431,7 +436,7 @@
         out_specs=pl.BlockSpec((1, TRI), lambda step: (0, 0)),
         out_shape=jax.ShapeDtypeStruct((1, TRI), F32),
         scratch_shapes=[pltpu.VMEM((72, size), F32), pltpu.VMEM((TRI, size), F32)],
-        compiler_params=PARAMS,
+        compiler_params=params(8),
         name="near",
     )(near_count, near_target, near_source, before, beside, after, near_tiles)
 
@@ -456,7 +461,7 @@
     devices = ROWS * COLS
     packed = jax.ShapeDtypeStruct((devices * LINES // LANES, LANES), F32)
     hbm = pl.BlockSpec(memory_space=pltpu.HBM)
-    sizes = [SENT + 8 if shift in (1, ROWS - 1) else SENT for shift in range(ROWS)]
+    sizes = [SENT + 8 if shift in (0, 1, ROWS - 1) else SENT for shift in range(ROWS)]
     deposited, *sent = pl.pallas_call(
         deposit_kernel,
         out_shape=(packed, *[jax.ShapeDtypeStruct((size, LANES), F32) for size in sizes]),
@@ -472,7 +477,7 @@
             pltpu.VMEM((LINES, G), F32),
             pltpu.SemaphoreType.DMA((6,)),
         ],
-        compiler_params=PARAMS,
+        compiler_params=params(20),
         name="deposit",
     )(
         *[
@@ -488,34 +493,33 @@
     )
     received = exchange(deposited, BOTH, devices)
     sent = [shifted(value, "row", shift) if shift else value for shift, value in enumerate(sent)]
-    vmem = pl.BlockSpec(memory_space=pltpu.VMEM)
-    names = ("first", "outer", "second", "flipped")
-    spectrum, beside, *staged = pl.pallas_call(
+    spectrum, beside = pl.pallas_call(
         spectrum_kernel,
         out_shape=(
             jax.ShapeDtypeStruct((G, G), F32),
             jax.ShapeDtypeStruct((24, LANES), F32),
-            *[jax.ShapeDtypeStruct(table[name].shape, BF16) for name in names],
         ),
-        in_specs=[vmem, *[hbm] * 5, *[vmem] * ROWS],
+        scratch_shapes=[pltpu.VMEM((ROWS * SENT, LANES), F32)],
+        compiler_params=params(8),
+        name="spectrum",
+    )(*sent)
+    names = ("first", "outer", "second", "flipped")
+    vmem = pl.BlockSpec(memory_space=pltpu.VMEM)
+    handed = pl.pallas_call(
+        plane_kernel,
+        out_shape=packed,
+        in_specs=[vmem, vmem, *[hbm] * 4],
         scratch_shapes=[
-            pltpu.VMEM(table["chosen"].shape, BF16),
-            pltpu.VMEM((ROWS * SENT, LANES), F32),
-            pltpu.SemaphoreType.DMA((5,)),
+            *[pltpu.VMEM(table[name].shape, BF16) for name in names],
+            pltpu.SemaphoreType.DMA((4,)),
         ],
-        compiler_params=PARAMS,
-        name="spectrum",
+        compiler_params=params(12),
+        name="plane",
     )(
-        charges.reshape(8, LANES),
-        *[
-            pltpu.with_memory_space_constraint(table[name], pltpu.HBM)
-            for name in ("chosen", *names)
-        ],
-        *sent,
+        received,
+        spectrum,
+        *[pltpu.with_memory_space_constraint(table[name], pltpu.HBM) for name in names],
     )
-    handed = pl.pallas_call(
-        plane_kernel, out_shape=packed, compiler_params=PARAMS, name="plane"
-    )(received, spectrum, *staged)
     field = exchange(handed, BOTH, devices)
     beside, _ = lax.optimization_barrier((beside, handed))
     near = near_field(beside, near_count, near_target, near_source, near_tiles)
@@ -527,7 +531,7 @@
             pltpu.VMEM((4 * SPREAD, 2 * G), BF16),
             pltpu.VMEM((TRI // CHUNK, 4 * SPREAD, CHUNK), F32),
         ],
-        compiler_params=PARAMS,
+        compiler_params=params(20),
         name="gather",
     )(field, anchors, stencil_weights, table["lines"], near)
     return result.reshape(TRI)

time: 80.7 us -> 73 us (0.905)
  local copies, waits for them, and re-layouts: 7.34 us -> 0.03 us
  waiting for transfers between devices: 12.6 us -> 18.3 us
  starting transfers between devices: 44 us -> 39 us
  Pallas kernels: 15.7 us -> 14.7 us
    unnamed x30 -> x12, local copies, waits for them, and re-layouts: 7.34 us -> 0.03 us
    all_to_all x2, waiting for transfers between devices: 4.53 us -> 10.2 us  [exchange(): lax.all_to_all(shaped, axes, split_axis=0, concat_axis=0, tiled=True)]
    all_to_all x2, starting transfers between devices: 27.7 us -> 22.7 us  [exchange(): lax.all_to_all(shaped, axes, split_axis=0, concat_axis=0, tiled=True)]
    pallas_call x1, Pallas kernels: 2.02 us -> 0.49 us  [local(): pl.pallas_call(spectrum_kernel, out_shape=(jax.ShapeDtypeStruct((G, G), F...]
    pallas_call x1, Pallas kernels: 3.09 us -> 4.28 us  [local(): pl.pallas_call(plane_kernel, out_shape=packed, in_specs=[vmem, vmem, *[hb...]
  transfers between devices with their start and end apart: 11 -> 11, of which waited for: 6 -> 6; matrix products, arithmetic and copies ran while one was open for 0% -> 0% of each run, Pallas kernels for 5% -> 2%
where the time goes in v4:
time: 73 us; the launch traced here: 72.7 us
  starting transfers between devices  39 us (53%)
  waiting for transfers between devices  18.3 us (25%)
  Pallas kernels  14.7 us (20%)
  between operations  0.75 us (1%)
    all_to_all x2, starting transfers between devices, exchange(): lax.all_to_all(shaped, axes, split_axis=0, concat_axis=0, tiled=True)  22.7 us
    ppermute x9, starting transfers between devices, shifted(): lax.ppermute(value, axis, [(i, (i + by) % size) for i in range(size)])  16.3 us
    all_to_all x2, waiting for transfers between devices, exchange(): lax.all_to_all(shaped, axes, split_axis=0, concat_axis=0, tiled=True)  10.2 us
    ppermute x9, waiting for transfers between devices, shifted(): lax.ppermute(value, axis, [(i, (i + by) % size) for i in range(size)])  8.13 us
    pallas_call x1, Pallas kernels, local(): pl.pallas_call(deposit_kernel, out_shape=(packed, *[jax.ShapeDtypeStruct(...  5.64 us
    pallas_call x1, Pallas kernels, local(): pl.pallas_call(plane_kernel, out_shape=packed, in_specs=[vmem, vmem, *[hb...  4.28 us
    pallas_call x1, Pallas kernels, local(): pl.pallas_call(gather_kernel, out_shape=jax.ShapeDtypeStruct((1, TRI), F3...  3.05 us
  transfers between devices with their start and end apart: 11, of which 6 were waited for; matrix products, arithmetic and copies ran while one was open for 0% of the time, Pallas kernels for 2%

profile of v4, /device:TPU:1, one launch (start us, length us, event | category | flops | bytes accessed | tf_op | source)
XLA Modules:
  0.0 72.7 jit_solution(1965422551612411108)
XLA Ops:
  0.0 5.6 %deposit.1 = (f32[768,128]{1,0:T(8,128)}, f32[48,128]{1,0:T(8,128)S(1)}, f32[48,128]{1,0:T(8,128)S(1)}, f32[40,128]{1,0:T(8,128)S(1)}, f32[40,128]{1,0:T(8,128)S...) custom-call(f32[1,1024]{1,0:T(1,128)} %bitcast.10, ...), custom_call_target="tpu_custom_call" | custom-call | tf_op jit(solution)/shard_map/deposit/pallas_call | solution.py:465
  5.7 0.0 copy-start
  5.7 0.0 copy-start.4
  5.7 0.0 copy-start.5
  5.7 15.7 %all-to-all-start = ((f32[256,1,384]{2,1,0:T(1,128)}), f32[256,1,384]{2,1,0:T(1,128)S(1)}, u32[]{:S(2)}, u32[]{:S(2)}) async-start(f32[256,1,384]{2,1,0:T(1,128)} %bitcast.2), calls=%async_computation | async-start | bytes 786432 | tf_op jit(solution)/shard_map/all_to_all | solution.py:446
  21.4 1.5 %collective-permute-start.1 = (f32[40,128]{1,0:T(8,128)S(1)}, f32[40,128]{1,0:T(8,128)S(1)}, u32[]{:S(2)}, u32[]{:S(2)}) collective-permute-start(f32[40,128]{1,0:T(8,128)S(1)} %get-tuple-element.20), channel_id=1, source_target_pairs={{0,64},{32,96},{64,128},{96,160},{128,192},{160,224},{192,0},{224,... | collective-permute-start | bytes 61448 | tf_op jit(solution)/shard_map/ppermute | solution.py:418
  22.8 3.0 %collective-permute-start.2 = (f32[40,128]{1,0:T(8,128)S(1)}, f32[40,128]{1,0:T(8,128)S(1)}, u32[]{:S(2)}, u32[]{:S(2)}) collective-permute-start(f32[40,128]{1,0:T(8,128)S(1)} %get-tuple-element.21), channel_id=1, source_target_pairs={{0,96},{32,128},{64,160},{96,192},{128,224},{160,0},{192,32},{224,... | collective-permute-start | bytes 61448 | tf_op jit(solution)/shard_map/ppermute | solution.py:418
  25.8 0.0 collective-permute-start
  25.8 0.5 collective-permute-start.6
  26.3 1.3 %collective-permute-start.3 = (f32[40,128]{1,0:T(8,128)S(1)}, f32[40,128]{1,0:T(8,128)S(1)}, u32[]{:S(2)}, u32[]{:S(2)}) collective-permute-start(f32[40,128]{1,0:T(8,128)S(1)} %get-tuple-element.22), channel_id=1, source_target_pairs={{0,128},{32,160},{64,192},{96,224},{128,0},{160,32},{192,64},{224,... | collective-permute-start | bytes 61448 | tf_op jit(solution)/shard_map/ppermute | solution.py:418
  27.6 0.0 collective-permute-done.1.refs_2_
  27.6 2.6 %collective-permute-start.4 = (f32[40,128]{1,0:T(8,128)S(1)}, f32[40,128]{1,0:T(8,128)S(1)}, u32[]{:S(2)}, u32[]{:S(2)}) collective-permute-start(f32[40,128]{1,0:T(8,128)S(1)} %get-tuple-element.23), channel_id=1, source_target_pairs={{0,160},{32,192},{64,224},{96,0},{128,32},{160,64},{192,96},{224,1... | collective-permute-start | bytes 61448 | tf_op jit(solution)/shard_map/ppermute | solution.py:418
  30.2 0.0 collective-permute-done.2.refs_3_
  30.2 0.6 collective-permute-start.5
  30.8 0.1 collective-permute-done.3.refs_4_
  30.8 2.0 %collective-permute-done.4.refs_5_ = f32[40,128]{1,0:T(8,128)S(1)} collective-permute-done((f32[40,128]{1,0:T(8,128)S(1)}, f32[40,128]{1,0:T(8,128)S(1)}, u32[]{:S(2)}, u32[]{:S(2)}) %collective-permute-start.4) | collective-permute-done | bytes 20512 | tf_op jit(solution)/shard_map/ppermute | solution.py:418
  32.8 0.7 collective-permute-done.5.refs_6_
  33.5 0.0 collective-permute-done.refs_1_
  33.5 0.0 collective-permute-done.6.refs_7_
  33.5 0.5 spectrum.1
  34.0 5.8 %all-to-all-done = f32[256,1,384]{2,1,0:T(1,128)S(1)} async-done(((f32[256,1,384]{2,1,0:T(1,128)}), f32[256,1,384]{2,1,0:T(1,128)S(1)}, u32[]{:S(2)}, u32[]{:S(2)}) %all-to-all-start) | async-done | bytes 393248 | tf_op jit(solution)/shard_map/all_to_all | solution.py:446
  39.8 0.0 copy-start.1
  39.8 0.0 copy-start.2
  39.8 0.0 copy-start.3
  39.8 4.3 %plane.1 = f32[768,128]{1,0:T(8,128)} custom-call(f32[768,128]{1,0:T(8,128)S(1)} %bitcast.7, f32[256,256]{1,0:T(8,128)S(1)} %get-tuple-element.26.spectrum_ref, bf16[2,256,256]{2,1,0:T(8,128)(2,1)} %constant.11.clone.rest_0_, bf16[2,256,256]{2,1,0:T(8,128)(2,1)} %constant.12.clone.rest_1_, bf16[2,256,320]{2,1,0:T(8,128)(2,1)} %constant.13.clone.rest_2_, ...), custom_call_target="tpu_custom_call" | custom-call | tf_op jit(solution)/shard_map/plane/pallas_call | solution.py:508
  44.1 7.0 %all-to-all-start.1 = ((f32[256,1,384]{2,1,0:T(1,128)}), f32[256,1,384]{2,1,0:T(1,128)S(1)}, u32[]{:S(2)}, u32[]{:S(2)}) async-start(f32[256,1,384]{2,1,0:T(1,128)} %bitcast.4), calls=%async_computation.1 | async-start | bytes 786432 | tf_op jit(solution)/shard_map/all_to_all | solution.py:446
  51.1 1.8 %collective-permute-start.7 = (f32[24,128]{1,0:T(8,128)S(1)}, f32[24,128]{1,0:T(8,128)S(1)}, u32[]{:S(2)}, u32[]{:S(2)}) collective-permute-start(f32[24,128]{1,0:T(8,128)S(1)} %get-tuple-element.28.own_ref), channel_id=1, source_target_pairs={{0,1},{1,2},{2,3},{3,4},{4,5},{5,6},{6,7},{7,8},{8,9},{9,10},{10,1... | collective-permute-start | bytes 36872 | tf_op jit(solution)/shard_map/ppermute | solution.py:418
  52.9 5.1 %collective-permute-start.8 = (f32[24,128]{1,0:T(8,128)S(1)}, f32[24,128]{1,0:T(8,128)S(1)}, u32[]{:S(2)}, u32[]{:S(2)}) collective-permute-start(f32[24,128]{1,0:T(8,128)S(1)} %get-tuple-element.28.own_ref), channel_id=1, source_target_pairs={{0,31},{1,0},{2,1},{3,2},{4,3},{5,4},{6,5},{7,6},{8,7},{9,8},{10,9... | collective-permute-start | bytes 36872 | tf_op jit(solution)/shard_map/ppermute | solution.py:418
  58.6 5.4 %collective-permute-done.7.before_ref = f32[24,128]{1,0:T(8,128)S(1)} collective-permute-done((f32[24,128]{1,0:T(8,128)S(1)}, f32[24,128]{1,0:T(8,128)S(1)}, u32[]{:S(2)}, u32[]{:S(2)}) %collective-permute-start.7) | collective-permute-done | bytes 12320 | tf_op jit(solution)/shard_map/ppermute | solution.py:418
  64.0 0.0 collective-permute-done.8.after_ref
  64.0 0.0 copy-done
  64.0 0.0 copy-done.4
  64.0 0.0 copy-done.5
  64.0 1.2 %near.1.near_ref = f32[1,1024]{1,0:T(1,128)S(1)} custom-call(s32[1]{0:T(128)S(6)} %copy.16.count_ref, s32[32]{0:T(128)S(1)} %copy-done.4, s32[32]{0:T(128)S(1)} %copy-done.5, f32[24,128]{1,0:T(8,128)S(1)} %collective-permute-done.7.before_ref, f32[24,128]{1,0:T(8,128)S(1)} %get-tuple-element.28.own_ref, f32[24,128]{1,0:T(8,128)S(1)} %collective-permute-done.8.after_ref, ...), custom_call_target="tpu_custom_call" | custom-call | tf_op jit(solution)/shard_map/near/pallas_call | solution.py:426
  65.2 4.4 %all-to-all-done.1 = f32[256,1,384]{2,1,0:T(1,128)S(1)} async-done(((f32[256,1,384]{2,1,0:T(1,128)}), f32[256,1,384]{2,1,0:T(1,128)S(1)}, u32[]{:S(2)}, u32[]{:S(2)}) %all-to-all-start.1) | async-done | bytes 393248 | tf_op jit(solution)/shard_map/all_to_all | solution.py:446
  69.7 0.0 copy-done.1
  69.7 0.0 copy-done.2
  69.7 0.0 copy-done.3
  69.7 3.1 %gather.1 = f32[1,1024]{1,0:T(1,128)} custom-call(f32[768,128]{1,0:T(8,128)S(1)} %bitcast.8, s32[3,1024]{1,0:T(4,128)S(1)} %copy-done.3, f32[64,1024]{1,0:T(8,128)S(1)} %copy-done.1, bf16[2,256,256]{2,1,0:T(8,128)(2,1)S(1)} %copy-done.2, f32[1,1024]{1,0:T(1,128)S(1)} %near.1.near_ref), custom_call_target="tpu_custom_call" | custom-call | tf_op jit(solution)/shard_map/gather/pallas_call | solution.py:526
Async XLA Ops:
  5.7 58.4 %copy-start = (f32[32,128,128]{2,1,0:T(8,128)S(1)}, f32[32,128,128]{2,1,0:T(8,128)}, u32[]{:S(2)}) copy-start(f32[32,128,128]{2,1,0:T(8,128)} %tiles_ref.1) | copy-start | bytes 6291460
  5.7 58.4 %copy-start.4 = (s32[32]{0:T(128)S(1)}, s32[32]{0:T(128)}, u32[]{:S(2)}) copy-start(s32[32]{0:T(128)} %target_ref.1) | copy-start | bytes 388
  5.7 58.4 %copy-start.5 = (s32[32]{0:T(128)S(1)}, s32[32]{0:T(128)}, u32[]{:S(2)}) copy-start(s32[32]{0:T(128)} %source_ref.1) | copy-start | bytes 388
  5.7 34.1 %all-to-all-start = ((f32[256,1,384]{2,1,0:T(1,128)}), f32[256,1,384]{2,1,0:T(1,128)S(1)}, u32[]{:S(2)}, u32[]{:S(2)}) async-start(f32[256,1,384]{2,1,0:T(1,128)} %bitcast.2), calls=%async_computation | async-start | bytes 786432 | tf_op jit(solution)/shard_map/all_to_all | solution.py:446
  21.4 6.3 %collective-permute-start.1 = (f32[40,128]{1,0:T(8,128)S(1)}, f32[40,128]{1,0:T(8,128)S(1)}, u32[]{:S(2)}, u32[]{:S(2)}) collective-permute-start(f32[40,128]{1,0:T(8,128)S(1)} %get-tuple-element.20), channel_id=1, source_target_pairs={{0,64},{32,96},{64,128},{96,160},{128,192},{160,224},{192,0},{224,... | collective-permute-start | bytes 61448 | tf_op jit(solution)/shard_map/ppermute | solution.py:418
  22.8 7.4 %collective-permute-start.2 = (f32[40,128]{1,0:T(8,128)S(1)}, f32[40,128]{1,0:T(8,128)S(1)}, u32[]{:S(2)}, u32[]{:S(2)}) collective-permute-start(f32[40,128]{1,0:T(8,128)S(1)} %get-tuple-element.21), channel_id=1, source_target_pairs={{0,96},{32,128},{64,160},{96,192},{128,224},{160,0},{192,32},{224,... | collective-permute-start | bytes 61448 | tf_op jit(solution)/shard_map/ppermute | solution.py:418
  25.8 7.7 %collective-permute-start = (f32[48,128]{1,0:T(8,128)S(1)}, f32[48,128]{1,0:T(8,128)S(1)}, u32[]{:S(2)}, u32[]{:S(2)}) collective-permute-start(f32[48,128]{1,0:T(8,128)S(1)} %get-tuple-element.19), channel_id=1, source_target_pairs={{0,32},{32,64},{64,96},{96,128},{128,160},{160,192},{192,224},{224... | collective-permute-start | bytes 73736 | tf_op jit(solution)/shard_map/ppermute | solution.py:418
  25.8 7.7 %collective-permute-start.6 = (f32[48,128]{1,0:T(8,128)S(1)}, f32[48,128]{1,0:T(8,128)S(1)}, u32[]{:S(2)}, u32[]{:S(2)}) collective-permute-start(f32[48,128]{1,0:T(8,128)S(1)} %get-tuple-element.25), channel_id=1, source_target_pairs={{0,224},{32,0},{64,32},{96,64},{128,96},{160,128},{192,160},{224,1... | collective-permute-start | bytes 73736 | tf_op jit(solution)/shard_map/ppermute | solution.py:418
  26.3 4.5 %collective-permute-start.3 = (f32[40,128]{1,0:T(8,128)S(1)}, f32[40,128]{1,0:T(8,128)S(1)}, u32[]{:S(2)}, u32[]{:S(2)}) collective-permute-start(f32[40,128]{1,0:T(8,128)S(1)} %get-tuple-element.22), channel_id=1, source_target_pairs={{0,128},{32,160},{64,192},{96,224},{128,0},{160,32},{192,64},{224,... | collective-permute-start | bytes 61448 | tf_op jit(solution)/shard_map/ppermute | solution.py:418
  27.6 5.2 %collective-permute-start.4 = (f32[40,128]{1,0:T(8,128)S(1)}, f32[40,128]{1,0:T(8,128)S(1)}, u32[]{:S(2)}, u32[]{:S(2)}) collective-permute-start(f32[40,128]{1,0:T(8,128)S(1)} %get-tuple-element.23), channel_id=1, source_target_pairs={{0,160},{32,192},{64,224},{96,0},{128,32},{160,64},{192,96},{224,1... | collective-permute-start | bytes 61448 | tf_op jit(solution)/shard_map/ppermute | solution.py:418
  30.2 3.3 %collective-permute-start.5 = (f32[40,128]{1,0:T(8,128)S(1)}, f32[40,128]{1,0:T(8,128)S(1)}, u32[]{:S(2)}, u32[]{:S(2)}) collective-permute-start(f32[40,128]{1,0:T(8,128)S(1)} %get-tuple-element.24), channel_id=1, source_target_pairs={{0,192},{32,224},{64,0},{96,32},{128,64},{160,96},{192,128},{224,1... | collective-permute-start | bytes 61448 | tf_op jit(solution)/shard_map/ppermute | solution.py:418
  39.8 29.9 %copy-start.1 = (f32[64,1024]{1,0:T(8,128)S(1)}, f32[64,1024]{1,0:T(8,128)}, u32[]{:S(2)}) copy-start(f32[64,1024]{1,0:T(8,128)} %weights_ref.1) | copy-start | bytes 786436
  39.8 29.9 %copy-start.2 = (bf16[2,256,256]{2,1,0:T(8,128)(2,1)S(1)}, bf16[2,256,256]{2,1,0:T(8,128)(2,1)}, u32[]{:S(2)}) copy-start(bf16[2,256,256]{2,1,0:T(8,128)(2,1)} %constant.10.clone.table_hbm.table_ref) | copy-start | bytes 786436
  39.8 29.9 %copy-start.3 = (s32[3,1024]{1,0:T(4,128)S(1)}, s32[3,1024]{1,0:T(4,128)}, u32[]{:S(2)}) copy-start(s32[3,1024]{1,0:T(4,128)} %anchors_ref.1) | copy-start | bytes 36868
  44.1 25.6 %all-to-all-start.1 = ((f32[256,1,384]{2,1,0:T(1,128)}), f32[256,1,384]{2,1,0:T(1,128)S(1)}, u32[]{:S(2)}, u32[]{:S(2)}) async-start(f32[256,1,384]{2,1,0:T(1,128)} %bitcast.4), calls=%async_computation.1 | async-start | bytes 786432 | tf_op jit(solution)/shard_map/all_to_all | solution.py:446
  51.1 12.9 %collective-permute-start.7 = (f32[24,128]{1,0:T(8,128)S(1)}, f32[24,128]{1,0:T(8,128)S(1)}, u32[]{:S(2)}, u32[]{:S(2)}) collective-permute-start(f32[24,128]{1,0:T(8,128)S(1)} %get-tuple-element.28.own_ref), channel_id=1, source_target_pairs={{0,1},{1,2},{2,3},{3,4},{4,5},{5,6},{6,7},{7,8},{8,9},{9,10},{10,1... | collective-permute-start | bytes 36872 | tf_op jit(solution)/shard_map/ppermute | solution.py:418
  52.9 11.1 %collective-permute-start.8 = (f32[24,128]{1,0:T(8,128)S(1)}, f32[24,128]{1,0:T(8,128)S(1)}, u32[]{:S(2)}, u32[]{:S(2)}) collective-permute-start(f32[24,128]{1,0:T(8,128)S(1)} %get-tuple-element.28.own_ref), channel_id=1, source_target_pairs={{0,31},{1,0},{2,1},{3,2},{4,3},{5,4},{6,5},{7,6},{8,7},{9,8},{10,9... | collective-permute-start | bytes 36872 | tf_op jit(solution)/shard_map/ppermute | solution.py:418

commit v5 on v4

--- a/solution.py
+++ b/solution.py
@@ -1,3 +1,5 @@
+import math
+
 import jax
 import jax.numpy as jnp
 import ml_dtypes
@@ -23,6 +25,7 @@
 KEPT = CELLS_A // 2 + 1
 SENT = 40
 CHUNK = 256
+PART = 8
 GROUPS = ((0, 4, 8), (1, 5, 9), (2, 6), (3, 7))
 F32 = jnp.float32
 BF16 = jnp.bfloat16
@@ -48,29 +51,11 @@
     return 4 * (slot // 4) + (slot - block) % 4
 
 
-def tables():
+def line_table():
     steps = np.arange(G)
     device = np.arange(ROWS * COLS)
     plane = CELLS_B * (device % COLS) + device // COLS
-    along_a = (np.arange(G) - 1) % G
-    order = np.concatenate([
-        (CELLS_B * np.arange(COLS) - 1 + line) % G for group in GROUPS for line in group
-    ])
-    outer = np.zeros((G, G))
-    for slot in range(ROWS):
-        row = row_at(slot, LINES_B)
-        for extra in range(2):
-            cell = (CELLS_A * (row + 1) - 1 + extra) % G
-            for line in range(LINES_B):
-                outer[CELLS_A * slot + 2 * line + extra] = cas(np.array([cell]), steps)[0]
-    second = cas(steps, order)
-    return {
-        "lines": split_table(cas(plane, steps)),
-        "first": split_table(cas(along_a, steps)),
-        "outer": split_table(outer),
-        "second": split_table(second),
-        "flipped": split_table(second.T),
-    }
+    return split_table(cas(plane, steps))
 
 
 def halves(value):
@@ -91,11 +76,18 @@
     return lax.dot_general(left, right, (dims, ((), ())), preferred_element_type=F32)
 
 
-def dot_split(left, right, dims=((1,), (0,))):
-    left_high, left_low = left
-    right_high, right_low = right
-    cross = dot(left_high, right_low, dims) + dot(left_low, right_high, dims)
-    return dot(left_high, right_high, dims) + cross
+def dot_table(rows, table, dims=((1,), (0,))):
+    high, low = rows
+    size = high.shape[0]
+    both = dot(jnp.concatenate([high, low], axis=0), table[0], dims)
+    return both[:size] + (both[size:] + dot(high, table[1], dims))
+
+
+def table_dot(table, value, dims=((1,), (0,))):
+    high, low = value
+    size = table[0].shape[0]
+    both = dot(jnp.concatenate([table[0], table[1]], axis=0), high, dims)
+    return both[:size] + (both[size:] + dot(table[0], low, dims))
 
 
 def block_place(block):
@@ -196,23 +188,31 @@
     copies = [pltpu.make_async_copy(a, b, sem.at[n]) for n, (a, b) in enumerate(pairs)]
     for copy in copies:
         copy.start()
-    for copy in copies:
+    for copy in copies[:3]:
         copy.wait()
     scaled[...] = weights_ref[...] * charges_ref[...]
     places = [local_place(anchors_ref, pl.ds(tile * LANES, LANES)) for tile in range(TILES)]
-    hot = onehot(anchors_ref)
-    hot = jnp.concatenate([hot, hot], axis=1)
+    cells = lax.broadcasted_iota(jnp.int32, (LANES, G), 1)
+    hot = []
+    for tile in range(TILES):
+        row = anchors_ref[2:3, pl.ds(tile * LANES, LANES)]
+        column = jnp.broadcast_to(row, (LANES, LANES)).T
+        column = jnp.concatenate([column, column], axis=1)
+        hot.append(jnp.where(cells == column, 1.0, 0.0).astype(BF16))
+    hot = jnp.concatenate(hot + hot, axis=0)
     total = None
     for k in (1, 2, 3, 0):
         for tile in range(TILES):
             spread_tile(scaled, places[tile], spread, k, tile)
-        placed = dot(spread[k], hot, ((1,), (1,)))
+        placed = dot(spread[k], hot)
         placed = pltpu.roll(placed, k, 1) if k else placed
         total = placed if total is None else total + placed
     for block in range(LINES_B + 1):
         lines[block_place(block), :] = total[CELLS_A * block : CELLS_A * (block + 1)]
     lines[block_place(LINES_B + 1), :] = jnp.zeros((CELLS_A, G), F32)
-    result = dot_split((table_ref[0], table_ref[1]), halves(lines[...]), ((1,), (1,)))
+    for copy in copies[3:]:
+        copy.wait()
+    result = table_dot((table_ref[0], table_ref[1]), halves(lines[...]), ((1,), (1,)))
     for v in range(3):
         out_ref[pl.ds(v, G, stride=3), :] = result[:, LANES * v : LANES * (v + 1)]
     for shift, sent in enumerate(sent_refs):
@@ -227,8 +227,19 @@
             sent_refs[shift][pl.ds(SENT + block, 1), :] = charges_ref[:, at]
 
 
+def cas_of(turns):
+    centred = ((turns + 3 * G // 8) & (G - 1)) - G // 2
+    angle = (G // 4 - jnp.abs(centred)).astype(F32) * (2.0 * math.pi / G)
+    square = angle * angle
+    value = jnp.full_like(square, math.sqrt(2.0) / math.factorial(13))
+    for power in (11, 9, 7, 5, 3, 1):
+        sign = 1.0 if power % 4 == 1 else -1.0
+        value = value * square + sign * math.sqrt(2.0) / math.factorial(power)
+    return value * angle
+
+
 def spectrum_kernel(*refs):
-    sent_refs, (out_ref, beside_ref, joined) = refs[:ROWS], refs[ROWS:]
+    sent_refs, (out_ref, beside_ref, waves_ref, joined) = refs[:ROWS], refs[ROWS:]
     for shift, sent in enumerate(sent_refs):
         owner = (lax.axis_index("row") - shift) & (ROWS - 1)
         at = pl.ds(pl.multiple_of(owner * SENT, 8), SENT)
@@ -247,16 +258,12 @@
         chosen = jnp.where(place == half * KEPT, 1.0, 0.0).astype(BF16)
         value = sum(dot(chosen, part) for part in parts)
         out_ref[:, pl.ds(LANES * half, LANES)] = value * (1.0 / (G * G * G))
-
-
-def plane_kernel(tiles_ref, spectrum_ref, *rest):
-    tables_hbm, out_ref, tables_ref, sem = rest[:4], rest[4], rest[5:9], rest[9]
-    first_ref, outer_ref, second_ref, flipped_ref = tables_ref
-    copies = [
-        pltpu.make_async_copy(a, b, sem.at[n]) for n, (a, b) in enumerate(zip(tables_hbm, tables_ref))
-    ]
-    for copy in copies:
-        copy.start()
+        cell = lax.broadcasted_iota(jnp.int32, (G, LANES), 0) - 1
+        wave = lax.broadcasted_iota(jnp.int32, (G, LANES), 1) + LANES * half
+        waves_ref[half] = cas_of(cell * wave)
+
+
+def plane_kernel(tiles_ref, spectrum_ref, waves_ref, out_ref):
     lane = lax.broadcasted_iota(jnp.int32, (CELLS_A, LANES), 1)
     slots = [(lane >> 5) == s for s in range(4)]
     wide = lax.broadcasted_iota(jnp.int32, (CELLS_A, G), 1)
@@ -275,41 +282,55 @@
             parts.append(value)
         return jnp.concatenate(parts, axis=1)
 
+    def waves(start, count, stride=1):
+        rows = [waves_ref[half, pl.ds(start, count, stride=stride), :] for half in range(2)]
+        return jnp.concatenate(rows, axis=1)
+
+    first = halves(waves(0, G))
+    even = (lax.broadcasted_iota(jnp.int32, (CELLS_A, G), 0) & 1) == 0
+    outer = []
+    for slot in range(ROWS):
+        start = CELLS_A * ((row_at(slot, LINES_B) + 1) % ROWS)
+        outer.append(jnp.where(even, waves(start, 1), waves(start + 1, 1)))
+    outer = halves(jnp.concatenate(outer, axis=0))
+    lines = [line for group in GROUPS for line in group]
+    flipped = []
+    for line in lines:
+        rows = waves(line % CELLS_B, COLS, CELLS_B)
+        flipped.append(pltpu.roll(rows, COLS - 1, 0) if line >= CELLS_B else rows)
+    flipped = jnp.concatenate([*flipped, jnp.zeros((LINES - MAIN, G), F32)], axis=0)
+    second = halves(flipped.T[:, :MAIN])
+    flipped = halves(flipped[:MAIN])
+
     def table(m):
         order = [row_at(slot, m) for slot in range(ROWS)]
-        both = []
-        for part in range(2):
-            rows = [first_ref[part, pl.ds(CELLS_A * r, CELLS_A), :] for r in order]
-            both.append(jnp.concatenate([*rows, outer_ref[part]], axis=0))
-        return both
+        return [
+            jnp.concatenate([part[CELLS_A * r : CELLS_A * (r + 1)] for r in order], axis=0)
+            for part in first
+        ]
 
     rim = joined(LINES_B)
-    half = []
-    for group in GROUPS:
-        rows = [
-            jnp.concatenate([joined(line), jnp.where(pairs[line], rim, 0.0)], axis=1)
-            for line in group
-        ]
-        half.append(halves(jnp.concatenate(rows, axis=0)))
-    copies[0].wait()
-    copies[1].wait()
-    half = [dot_split(rows, table(m)) for m, rows in enumerate(half)]
-    half = halves(jnp.concatenate(half, axis=0))
-    copies[2].wait()
-    image = dot_split((second_ref[0], second_ref[1]), half) * spectrum_ref[...]
-    copies[3].wait()
-    half = dot_split((flipped_ref[0], flipped_ref[1]), halves(image))
+    main = [
+        halves(jnp.concatenate([joined(line) for line in group], axis=0)) for group in GROUPS
+    ]
+    rims = halves(jnp.concatenate([jnp.where(pairs[line], rim, 0.0) for line in lines], axis=0))
+    half = jnp.concatenate([dot_table(rows, table(m)) for m, rows in enumerate(main)], axis=0)
+    half = halves(half + dot_table(rims, outer))
+    image = table_dot(second, half) * spectrum_ref[...]
+    half = halves(table_dot(flipped, halves(image)))
+    rims = dot_table(half, outer, ((1,), (1,)))
     blocks, at = {}, 0
     for m, group in enumerate(GROUPS):
         size = CELLS_A * len(group)
-        value = dot_split(halves(half[at : at + size]), table(m), ((1,), (1,)))
+        rows = [part[at : at + size] for part in half]
+        value = dot_table(rows, table(m), ((1,), (1,)))
         for place, line in enumerate(group):
             blocks[line] = value[CELLS_A * place : CELLS_A * (place + 1)]
         at += size
     zero = jnp.zeros((CELLS_A, G), F32)
     rim = zero
-    for line in range(LINES_B):
-        rim = jnp.where(pairs[line], blocks[line][:, G:], rim)
+    for place, line in enumerate(lines):
+        rim = jnp.where(pairs[line], rims[CELLS_A * place : CELLS_A * (place + 1)], rim)
     blocks[LINES_B], blocks[LINES_B + 1] = rim, zero
     for r in range(ROWS):
         lanes = slice(LANES * (r // 4), LANES * (r // 4 + 1))
@@ -360,7 +381,7 @@
 ):
     turned = [field_ref[pl.ds(v, G, stride=3), :].T for v in range(3)]
     turned = halves(jnp.concatenate(turned, axis=0))
-    lines[...] = dot_split(turned, (table_ref[0], table_ref[1]))
+    lines[...] = dot_table(turned, (table_ref[0], table_ref[1]))
     field = jnp.concatenate([lines[block_place(b), :] for b in range(LINES_B + 1)], axis=0)
     for k in range(4):
         high, low = halves(pltpu.roll(field, G - k, 1) if k else field)
@@ -381,36 +402,38 @@
 
 
 def near_kernel(
-    count_ref, target_ref, source_ref, before_ref, own_ref, after_ref, tiles_ref, out_ref,
-    charges_ref, total,
+    count_ref, target_ref, source_ref, before_ref, own_ref, after_ref, tiles_hbm, out_ref,
+    charges_ref, total, tiles_ref, sem,
 ):
-    step = pl.program_id(0)
-    per_step, size = tiles_ref.shape[0], tiles_ref.shape[1]
-
-    @pl.when(step == 0)
-    def _():
-        total[...] = jnp.zeros_like(total)
-        for place, ref in enumerate((before_ref, own_ref, after_ref)):
-            charges_ref[pl.ds(24 * place, 24), :] = ref[...]
-
-    def slot(u, carry):
-        place = step * per_step + u
+    size = LANES
+    parts = tiles_hbm.shape[0] // PART
+    copies = []
+    for part in range(parts):
+        at = pl.ds(PART * part, PART)
+        copies.append(pltpu.make_async_copy(tiles_hbm.at[at], tiles_ref.at[at], sem.at[part]))
+    for copy in copies:
+        copy.start()
+    total[...] = jnp.zeros_like(total)
+    for place, ref in enumerate((before_ref, own_ref, after_ref)):
+        charges_ref[pl.ds(24 * place, 24), :] = ref[...]
+
+    def slot(place, carry):
         rows = pl.ds(pl.multiple_of(target_ref[place] * size, size), size)
         code = source_ref[place]
         neighbour = code >> 3
         row = neighbour // 3
         line = 24 * (neighbour - 3 * row) + 8 * row + (code & 7)
         source = charges_ref[pl.ds(line, 1), :]
-        total[rows, :] = total[rows, :] + tiles_ref[u] * source
+        total[rows, :] = total[rows, :] + tiles_ref[place] * source
         return carry
 
-    lax.fori_loop(0, jnp.clip(count_ref[0] - step * per_step, 0, per_step), slot, 0)
-
-    @pl.when(step == pl.num_programs(0) - 1)
-    def _():
-        ones = jnp.ones((8, size), BF16)
-        result = sum(dot(ones, part, ((1,), (1,))) for part in thirds(total[...]))
-        out_ref[...] = result[0:1]
+    for part, copy in enumerate(copies):
+        copy.wait()
+        start = PART * part
+        lax.fori_loop(start, jnp.clip(count_ref[0], start, start + PART), slot, 0)
+    ones = jnp.ones((8, size), BF16)
+    result = sum(dot(ones, part, ((1,), (1,))) for part in thirds(total[...]))
+    out_ref[...] = result[0:1]
 
 
 def shifted(value, axis, by):
@@ -421,24 +444,29 @@
 def near_field(beside, near_count, near_target, near_source, near_tiles):
     slots, size, _ = near_tiles.shape
     before, after = shifted(beside, "col", 1), shifted(beside, "col", -1)
-    per_step = 8
     smem = pl.BlockSpec(memory_space=pltpu.SMEM)
+    vmem = pl.BlockSpec(memory_space=pltpu.VMEM)
     return pl.pallas_call(
         near_kernel,
-        grid=(slots // per_step,),
-        in_specs=[
-            smem,
-            smem,
-            smem,
-            *[pl.BlockSpec((24, size), lambda step: (0, 0))] * 3,
-            pl.BlockSpec((per_step, size, size), lambda step: (step, 0, 0)),
+        in_specs=[smem, smem, smem, vmem, vmem, vmem, pl.BlockSpec(memory_space=pltpu.HBM)],
+        out_shape=jax.ShapeDtypeStruct((1, TRI), F32),
+        scratch_shapes=[
+            pltpu.VMEM((72, size), F32),
+            pltpu.VMEM((TRI, size), F32),
+            pltpu.VMEM((slots, size, size), F32),
+            pltpu.SemaphoreType.DMA((slots // PART,)),
         ],
-        out_specs=pl.BlockSpec((1, TRI), lambda step: (0, 0)),
-        out_shape=jax.ShapeDtypeStruct((1, TRI), F32),
-        scratch_shapes=[pltpu.VMEM((72, size), F32), pltpu.VMEM((TRI, size), F32)],
         compiler_params=params(8),
         name="near",
-    )(near_count, near_target, near_source, before, beside, after, near_tiles)
+    )(
+        near_count,
+        near_target,
+        near_source,
+        before,
+        beside,
+        after,
+        pltpu.with_memory_space_constraint(near_tiles, pltpu.HBM),
+    )
 
 
 def exchange(values, axes, pieces):
@@ -457,7 +485,7 @@
     near_source,
     near_tiles,
 ):
-    table = {name: jnp.asarray(value) for name, value in tables().items()}
+    table = jnp.asarray(line_table())
     devices = ROWS * COLS
     packed = jax.ShapeDtypeStruct((devices * LINES // LANES, LANES), F32)
     hbm = pl.BlockSpec(memory_space=pltpu.HBM)
@@ -486,40 +514,27 @@
                 charges.reshape(1, TRI),
                 anchors,
                 stencil_weights,
-                table["lines"],
+                table,
                 kernel_spectrum.reshape(CELLS_A * CELLS_B, G),
             )
         ]
     )
     received = exchange(deposited, BOTH, devices)
     sent = [shifted(value, "row", shift) if shift else value for shift, value in enumerate(sent)]
-    spectrum, beside = pl.pallas_call(
+    spectrum, beside, waves = pl.pallas_call(
         spectrum_kernel,
         out_shape=(
             jax.ShapeDtypeStruct((G, G), F32),
             jax.ShapeDtypeStruct((24, LANES), F32),
+            jax.ShapeDtypeStruct((2, G, LANES), F32),
         ),
         scratch_shapes=[pltpu.VMEM((ROWS * SENT, LANES), F32)],
         compiler_params=params(8),
         name="spectrum",
     )(*sent)
-    names = ("first", "outer", "second", "flipped")
-    vmem = pl.BlockSpec(memory_space=pltpu.VMEM)
     handed = pl.pallas_call(
-        plane_kernel,
-        out_shape=packed,
-        in_specs=[vmem, vmem, *[hbm] * 4],
-        scratch_shapes=[
-            *[pltpu.VMEM(table[name].shape, BF16) for name in names],
-            pltpu.SemaphoreType.DMA((4,)),
-        ],
-        compiler_params=params(12),
-        name="plane",
-    )(
-        received,
-        spectrum,
-        *[pltpu.with_memory_space_constraint(table[name], pltpu.HBM) for name in names],
-    )
+        plane_kernel, out_shape=packed, compiler_params=params(12), name="plane"
+    )(received, spectrum, waves)
     field = exchange(handed, BOTH, devices)
     beside, _ = lax.optimization_barrier((beside, handed))
     near = near_field(beside, near_count, near_target, near_source, near_tiles)
@@ -533,7 +548,7 @@
         ],
         compiler_params=params(20),
         name="gather",
-    )(field, anchors, stencil_weights, table["lines"], near)
+    )(field, anchors, stencil_weights, table, near)
     return result.reshape(TRI)
 
 

time: 73 us -> 71.4 us (0.978)
  waiting for transfers between devices: 18.3 us -> 16.9 us
    all_to_all x2, waiting for transfers between devices: 10.2 us -> 8.75 us  [exchange(): lax.all_to_all(shaped, axes, split_axis=0, concat_axis=0, tiled=True)]
  transfers between devices with their start and end apart: 11 -> 11, of which waited for: 6 -> 6; matrix products, arithmetic and copies ran while one was open for 0% -> 0% of each run, Pallas kernels for 2% -> 4%
where the time goes in v5:
time: 71.4 us; the launch traced here: 71.2 us
  starting transfers between devices  39.2 us (55%)
  waiting for transfers between devices  16.9 us (24%)
  Pallas kernels  14.4 us (20%)
    all_to_all x2, starting transfers between devices, exchange(): lax.all_to_all(shaped, axes, split_axis=0, concat_axis=0, tiled=True)  22.9 us
    ppermute x9, starting transfers between devices, shifted(): lax.ppermute(value, axis, [(i, (i + by) % size) for i in range(size)])  16.3 us
    all_to_all x2, waiting for transfers between devices, exchange(): lax.all_to_all(shaped, axes, split_axis=0, concat_axis=0, tiled=True)  8.75 us
    ppermute x9, waiting for transfers between devices, shifted(): lax.ppermute(value, axis, [(i, (i + by) % size) for i in range(size)])  8.13 us
    pallas_call x1, Pallas kernels, local(): pl.pallas_call(deposit_kernel, out_shape=(packed, *[jax.ShapeDtypeStruct(...  5.61 us
    pallas_call x1, Pallas kernels, local(): pl.pallas_call(gather_kernel, out_shape=jax.ShapeDtypeStruct((1, TRI), F3...  3.01 us
    pallas_call x1, Pallas kernels, local(): pl.pallas_call(plane_kernel, out_shape=packed, compiler_params=params(12)...  2.64 us
    pallas_call x1, Pallas kernels, near_field(): pl.pallas_call(near_kernel, in_specs=[smem, smem, smem, vmem, vmem, vmem,...  2.43 us
  transfers between devices with their start and end apart: 11, of which 6 were waited for; matrix products, arithmetic and copies ran while one was open for 0% of the time, Pallas kernels for 4%

profile of v5, /device:TPU:1, one launch (start us, length us, event | category | flops | bytes accessed | tf_op | source)
XLA Modules:
  0.0 71.2 jit_solution(9290430586711988285)
XLA Ops:
  0.0 0.0 copy-start.3
  0.0 0.0 copy-start.4
  0.0 5.6 %deposit.1 = (f32[768,128]{1,0:T(8,128)}, f32[48,128]{1,0:T(8,128)S(1)}, f32[48,128]{1,0:T(8,128)S(1)}, f32[40,128]{1,0:T(8,128)S(1)}, f32[40,128]{1,0:T(8,128)S...) custom-call(f32[1,1024]{1,0:T(1,128)} %bitcast.10, ...), custom_call_target="tpu_custom_call" | custom-call | tf_op jit(solution)/shard_map/deposit/pallas_call | solution.py:493
  5.6 15.7 %all-to-all-start = ((f32[256,1,384]{2,1,0:T(1,128)}), f32[256,1,384]{2,1,0:T(1,128)S(1)}, u32[]{:S(2)}, u32[]{:S(2)}) async-start(f32[256,1,384]{2,1,0:T(1,128)} %bitcast.2), calls=%async_computation | async-start | bytes 786432 | tf_op jit(solution)/shard_map/all_to_all | solution.py:474
  21.3 1.5 %collective-permute-start.1 = (f32[40,128]{1,0:T(8,128)S(1)}, f32[40,128]{1,0:T(8,128)S(1)}, u32[]{:S(2)}, u32[]{:S(2)}) collective-permute-start(f32[40,128]{1,0:T(8,128)S(1)} %get-tuple-element.21), channel_id=1, source_target_pairs={{0,64},{32,96},{64,128},{96,160},{128,192},{160,224},{192,0},{224,... | collective-permute-start | bytes 61448 | tf_op jit(solution)/shard_map/ppermute | solution.py:441
  22.8 3.0 %collective-permute-start.2 = (f32[40,128]{1,0:T(8,128)S(1)}, f32[40,128]{1,0:T(8,128)S(1)}, u32[]{:S(2)}, u32[]{:S(2)}) collective-permute-start(f32[40,128]{1,0:T(8,128)S(1)} %get-tuple-element.22), channel_id=1, source_target_pairs={{0,96},{32,128},{64,160},{96,192},{128,224},{160,0},{192,32},{224,... | collective-permute-start | bytes 61448 | tf_op jit(solution)/shard_map/ppermute | solution.py:441
  25.7 0.0 collective-permute-start
  25.7 0.5 collective-permute-start.6
  26.2 1.3 %collective-permute-start.3 = (f32[40,128]{1,0:T(8,128)S(1)}, f32[40,128]{1,0:T(8,128)S(1)}, u32[]{:S(2)}, u32[]{:S(2)}) collective-permute-start(f32[40,128]{1,0:T(8,128)S(1)} %get-tuple-element.23), channel_id=1, source_target_pairs={{0,128},{32,160},{64,192},{96,224},{128,0},{160,32},{192,64},{224,... | collective-permute-start | bytes 61448 | tf_op jit(solution)/shard_map/ppermute | solution.py:441
  27.5 0.0 collective-permute-done.1.refs_2_
  27.5 2.6 %collective-permute-start.4 = (f32[40,128]{1,0:T(8,128)S(1)}, f32[40,128]{1,0:T(8,128)S(1)}, u32[]{:S(2)}, u32[]{:S(2)}) collective-permute-start(f32[40,128]{1,0:T(8,128)S(1)} %get-tuple-element.24), channel_id=1, source_target_pairs={{0,160},{32,192},{64,224},{96,0},{128,32},{160,64},{192,96},{224,1... | collective-permute-start | bytes 61448 | tf_op jit(solution)/shard_map/ppermute | solution.py:441
  30.2 0.0 collective-permute-done.2.refs_3_
  30.2 0.6 collective-permute-start.5
  30.7 0.1 collective-permute-done.3.refs_4_
  30.8 2.0 %collective-permute-done.4.refs_5_ = f32[40,128]{1,0:T(8,128)S(1)} collective-permute-done((f32[40,128]{1,0:T(8,128)S(1)}, f32[40,128]{1,0:T(8,128)S(1)}, u32[]{:S(2)}, u32[]{:S(2)}) %collective-permute-start.4) | collective-permute-done | bytes 20512 | tf_op jit(solution)/shard_map/ppermute | solution.py:441
  32.8 0.7 collective-permute-done.5.refs_6_
  33.4 0.0 collective-permute-done.refs_1_
  33.4 0.0 collective-permute-done.6.refs_7_
  33.5 0.7 spectrum.1
  34.2 5.5 %all-to-all-done = f32[256,1,384]{2,1,0:T(1,128)S(1)} async-done(((f32[256,1,384]{2,1,0:T(1,128)}), f32[256,1,384]{2,1,0:T(1,128)S(1)}, u32[]{:S(2)}, u32[]{:S(2)}) %all-to-all-start) | async-done | bytes 393248 | tf_op jit(solution)/shard_map/all_to_all | solution.py:474
  39.7 0.0 copy-start
  39.7 0.0 copy-start.1
  39.7 0.0 copy-start.2
  39.7 2.6 %plane.1 = f32[768,128]{1,0:T(8,128)} custom-call(f32[768,128]{1,0:T(8,128)S(1)} %bitcast.8, f32[256,256]{1,0:T(8,128)S(1)} %get-tuple-element.27.spectrum_ref, f32[2,256,128]{2,1,0:T(8,128)S(1)} %get-tuple-element.28.waves_ref), custom_call_target="tpu_custom_call" | custom-call | tf_op jit(solution)/shard_map/plane/pallas_call | solution.py:535
  42.4 7.2 %all-to-all-start.1 = ((f32[256,1,384]{2,1,0:T(1,128)}), f32[256,1,384]{2,1,0:T(1,128)S(1)}, u32[]{:S(2)}, u32[]{:S(2)}) async-start(f32[256,1,384]{2,1,0:T(1,128)} %bitcast.4), calls=%async_computation.1 | async-start | bytes 786432 | tf_op jit(solution)/shard_map/all_to_all | solution.py:474
  49.6 1.8 %collective-permute-start.7 = (f32[24,128]{1,0:T(8,128)S(1)}, f32[24,128]{1,0:T(8,128)S(1)}, u32[]{:S(2)}, u32[]{:S(2)}) collective-permute-start(f32[24,128]{1,0:T(8,128)S(1)} %get-tuple-element.30.own_ref), channel_id=1, source_target_pairs={{0,1},{1,2},{2,3},{3,4},{4,5},{5,6},{6,7},{7,8},{8,9},{9,10},{10,1... | collective-permute-start | bytes 36872 | tf_op jit(solution)/shard_map/ppermute | solution.py:441
  51.4 5.1 %collective-permute-start.8 = (f32[24,128]{1,0:T(8,128)S(1)}, f32[24,128]{1,0:T(8,128)S(1)}, u32[]{:S(2)}, u32[]{:S(2)}) collective-permute-start(f32[24,128]{1,0:T(8,128)S(1)} %get-tuple-element.30.own_ref), channel_id=1, source_target_pairs={{0,31},{1,0},{2,1},{3,2},{4,3},{5,4},{6,5},{7,6},{8,7},{9,8},{10,9... | collective-permute-start | bytes 36872 | tf_op jit(solution)/shard_map/ppermute | solution.py:441
  57.1 5.4 %collective-permute-done.7.before_ref = f32[24,128]{1,0:T(8,128)S(1)} collective-permute-done((f32[24,128]{1,0:T(8,128)S(1)}, f32[24,128]{1,0:T(8,128)S(1)}, u32[]{:S(2)}, u32[]{:S(2)}) %collective-permute-start.7) | collective-permute-done | bytes 12320 | tf_op jit(solution)/shard_map/ppermute | solution.py:441
  62.5 0.0 collective-permute-done.8.after_ref
  62.5 0.0 copy-done.3
  62.5 0.0 copy-done.4
  62.5 2.4 %near.1.near_ref = f32[1,1024]{1,0:T(1,128)S(1)} custom-call(s32[1]{0:T(128)S(6)} %copy.12.count_ref, s32[32]{0:T(128)S(1)} %copy-done.3, s32[32]{0:T(128)S(1)} %copy-done.4, f32[24,128]{1,0:T(8,128)S(1)} %collective-permute-done.7.before_ref, f32[24,128]{1,0:T(8,128)S(1)} %get-tuple-element.30.own_ref, f32[24,128]{1,0:T(8,128)S(1)} %collective-permute-done.8.after_ref, ...), custom_call_target="tpu_custom_call" | custom-call | tf_op jit(solution)/shard_map/near/pallas_call | solution.py:449
  65.0 3.2 %all-to-all-done.1 = f32[256,1,384]{2,1,0:T(1,128)S(1)} async-done(((f32[256,1,384]{2,1,0:T(1,128)}), f32[256,1,384]{2,1,0:T(1,128)S(1)}, u32[]{:S(2)}, u32[]{:S(2)}) %all-to-all-start.1) | async-done | bytes 393248 | tf_op jit(solution)/shard_map/all_to_all | solution.py:474
  68.2 0.0 copy-done
  68.2 0.0 copy-done.1
  68.2 0.0 copy-done.2
  68.2 3.0 %gather.1 = f32[1,1024]{1,0:T(1,128)} custom-call(f32[768,128]{1,0:T(8,128)S(1)} %bitcast.7, s32[3,1024]{1,0:T(4,128)S(1)} %copy-done.2, f32[64,1024]{1,0:T(8,128)S(1)} %copy-done, bf16[2,256,256]{2,1,0:T(8,128)(2,1)S(1)} %copy-done.1, f32[1,1024]{1,0:T(1,128)S(1)} %near.1.near_ref), custom_call_target="tpu_custom_call" | custom-call | tf_op jit(solution)/shard_map/gather/pallas_call | solution.py:541
Async XLA Ops:
  0.0 62.5 %copy-start.3 = (s32[32]{0:T(128)S(1)}, s32[32]{0:T(128)}, u32[]{:S(2)}) copy-start(s32[32]{0:T(128)} %target_ref.1) | copy-start | bytes 388
  0.0 62.5 %copy-start.4 = (s32[32]{0:T(128)S(1)}, s32[32]{0:T(128)}, u32[]{:S(2)}) copy-start(s32[32]{0:T(128)} %source_ref.1) | copy-start | bytes 388
  5.6 34.1 %all-to-all-start = ((f32[256,1,384]{2,1,0:T(1,128)}), f32[256,1,384]{2,1,0:T(1,128)S(1)}, u32[]{:S(2)}, u32[]{:S(2)}) async-start(f32[256,1,384]{2,1,0:T(1,128)} %bitcast.2), calls=%async_computation | async-start | bytes 786432 | tf_op jit(solution)/shard_map/all_to_all | solution.py:474
  21.3 6.3 %collective-permute-start.1 = (f32[40,128]{1,0:T(8,128)S(1)}, f32[40,128]{1,0:T(8,128)S(1)}, u32[]{:S(2)}, u32[]{:S(2)}) collective-permute-start(f32[40,128]{1,0:T(8,128)S(1)} %get-tuple-element.21), channel_id=1, source_target_pairs={{0,64},{32,96},{64,128},{96,160},{128,192},{160,224},{192,0},{224,... | collective-permute-start | bytes 61448 | tf_op jit(solution)/shard_map/ppermute | solution.py:441
  22.8 7.4 %collective-permute-start.2 = (f32[40,128]{1,0:T(8,128)S(1)}, f32[40,128]{1,0:T(8,128)S(1)}, u32[]{:S(2)}, u32[]{:S(2)}) collective-permute-start(f32[40,128]{1,0:T(8,128)S(1)} %get-tuple-element.22), channel_id=1, source_target_pairs={{0,96},{32,128},{64,160},{96,192},{128,224},{160,0},{192,32},{224,... | collective-permute-start | bytes 61448 | tf_op jit(solution)/shard_map/ppermute | solution.py:441
  25.7 7.7 %collective-permute-start = (f32[48,128]{1,0:T(8,128)S(1)}, f32[48,128]{1,0:T(8,128)S(1)}, u32[]{:S(2)}, u32[]{:S(2)}) collective-permute-start(f32[48,128]{1,0:T(8,128)S(1)} %get-tuple-element.20), channel_id=1, source_target_pairs={{0,32},{32,64},{64,96},{96,128},{128,160},{160,192},{192,224},{224... | collective-permute-start | bytes 73736 | tf_op jit(solution)/shard_map/ppermute | solution.py:441
  25.7 7.7 %collective-permute-start.6 = (f32[48,128]{1,0:T(8,128)S(1)}, f32[48,128]{1,0:T(8,128)S(1)}, u32[]{:S(2)}, u32[]{:S(2)}) collective-permute-start(f32[48,128]{1,0:T(8,128)S(1)} %get-tuple-element.26), channel_id=1, source_target_pairs={{0,224},{32,0},{64,32},{96,64},{128,96},{160,128},{192,160},{224,1... | collective-permute-start | bytes 73736 | tf_op jit(solution)/shard_map/ppermute | solution.py:441
  26.2 4.5 %collective-permute-start.3 = (f32[40,128]{1,0:T(8,128)S(1)}, f32[40,128]{1,0:T(8,128)S(1)}, u32[]{:S(2)}, u32[]{:S(2)}) collective-permute-start(f32[40,128]{1,0:T(8,128)S(1)} %get-tuple-element.23), channel_id=1, source_target_pairs={{0,128},{32,160},{64,192},{96,224},{128,0},{160,32},{192,64},{224,... | collective-permute-start | bytes 61448 | tf_op jit(solution)/shard_map/ppermute | solution.py:441
  27.5 5.2 %collective-permute-start.4 = (f32[40,128]{1,0:T(8,128)S(1)}, f32[40,128]{1,0:T(8,128)S(1)}, u32[]{:S(2)}, u32[]{:S(2)}) collective-permute-start(f32[40,128]{1,0:T(8,128)S(1)} %get-tuple-element.24), channel_id=1, source_target_pairs={{0,160},{32,192},{64,224},{96,0},{128,32},{160,64},{192,96},{224,1... | collective-permute-start | bytes 61448 | tf_op jit(solution)/shard_map/ppermute | solution.py:441
  30.2 3.3 %collective-permute-start.5 = (f32[40,128]{1,0:T(8,128)S(1)}, f32[40,128]{1,0:T(8,128)S(1)}, u32[]{:S(2)}, u32[]{:S(2)}) collective-permute-start(f32[40,128]{1,0:T(8,128)S(1)} %get-tuple-element.25), channel_id=1, source_target_pairs={{0,192},{32,224},{64,0},{96,32},{128,64},{160,96},{192,128},{224,1... | collective-permute-start | bytes 61448 | tf_op jit(solution)/shard_map/ppermute | solution.py:441
  39.7 28.5 %copy-start = (f32[64,1024]{1,0:T(8,128)S(1)}, f32[64,1024]{1,0:T(8,128)}, u32[]{:S(2)}) copy-start(f32[64,1024]{1,0:T(8,128)} %weights_ref.1) | copy-start | bytes 786436
  39.7 28.5 %copy-start.1 = (bf16[2,256,256]{2,1,0:T(8,128)(2,1)S(1)}, bf16[2,256,256]{2,1,0:T(8,128)(2,1)}, u32[]{:S(2)}) copy-start(bf16[2,256,256]{2,1,0:T(8,128)(2,1)} %constant.2.clone.table_hbm.table_ref) | copy-start | bytes 786436
  39.7 28.5 %copy-start.2 = (s32[3,1024]{1,0:T(4,128)S(1)}, s32[3,1024]{1,0:T(4,128)}, u32[]{:S(2)}) copy-start(s32[3,1024]{1,0:T(4,128)} %anchors_ref.1) | copy-start | bytes 36868
  42.4 25.8 %all-to-all-start.1 = ((f32[256,1,384]{2,1,0:T(1,128)}), f32[256,1,384]{2,1,0:T(1,128)S(1)}, u32[]{:S(2)}, u32[]{:S(2)}) async-start(f32[256,1,384]{2,1,0:T(1,128)} %bitcast.4), calls=%async_computation.1 | async-start | bytes 786432 | tf_op jit(solution)/shard_map/all_to_all | solution.py:474
  49.6 12.9 %collective-permute-start.7 = (f32[24,128]{1,0:T(8,128)S(1)}, f32[24,128]{1,0:T(8,128)S(1)}, u32[]{:S(2)}, u32[]{:S(2)}) collective-permute-start(f32[24,128]{1,0:T(8,128)S(1)} %get-tuple-element.30.own_ref), channel_id=1, source_target_pairs={{0,1},{1,2},{2,3},{3,4},{4,5},{5,6},{6,7},{7,8},{8,9},{9,10},{10,1... | collective-permute-start | bytes 36872 | tf_op jit(solution)/shard_map/ppermute | solution.py:441
  51.4 11.1 %collective-permute-start.8 = (f32[24,128]{1,0:T(8,128)S(1)}, f32[24,128]{1,0:T(8,128)S(1)}, u32[]{:S(2)}, u32[]{:S(2)}) collective-permute-start(f32[24,128]{1,0:T(8,128)S(1)} %get-tuple-element.30.own_ref), channel_id=1, source_target_pairs={{0,31},{1,0},{2,1},{3,2},{4,3},{5,4},{6,5},{7,6},{8,7},{9,8},{10,9... | collective-permute-start | bytes 36872 | tf_op jit(solution)/shard_map/ppermute | solution.py:441

commit v6 on v5

--- a/solution.py
+++ b/solution.py
@@ -64,6 +64,11 @@
     return high, low
 
 
+def paired(value):
+    high = value.astype(BF16).astype(F32)
+    return jnp.concatenate([high, value - high], axis=0).astype(BF16)
+
+
 def thirds(value):
     parts = []
     for _ in range(3):
@@ -136,39 +141,44 @@
 
 def spread_tile(scaled, place, spread, k, tile):
     at = pl.ds(tile * LANES, LANES)
-    low_at = pl.ds(TRI + tile * LANES, LANES)
     zero = jnp.zeros((8, LANES), F32)
+    none = jnp.zeros((16, LANES), BF16)
     near_masks, next_masks, groups, bits = masks_of(place)
-    blocks = [two_rows(stencil_rows(scaled, j, k, at), near_masks, next_masks) for j in range(4)]
-    for mask, shift, count in zip(bits, (1, 2, 4), (5, 7, 10)):
+    _, group, second = place
+    group, second = [jnp.concatenate([part, part], axis=0) for part in (group, second)]
+    wide_groups = [group == g for g in range(4)]
+    wide_bits = [(second & bit) != 0 for bit in (1, 2, 4)]
+    blocks, rims = [], []
+    for j in range(4):
+        rows = two_rows(stencil_rows(scaled, j, k, at), near_masks, next_masks)
+        blocks.append([paired(row) for row in rows])
+        rim = jnp.where(groups[3], rows[1], zero)
+        rim = rim + pltpu.roll(rim, 2, 0)
+        rims.append(rim + pltpu.roll(rim, 4, 0))
+    for mask, shift, count in zip(wide_bits, (1, 2, 4), (5, 7, 10)):
         wider = []
         for line in range(count):
             if line < shift:
-                wider.append([jnp.where(mask, zero, low) for low in blocks[line]])
+                wider.append([jnp.where(mask, none, low) for low in blocks[line]])
             elif line >= len(blocks):
-                wider.append([jnp.where(mask, high, zero) for high in blocks[line - shift]])
+                wider.append([jnp.where(mask, high, none) for high in blocks[line - shift]])
             else:
                 pairs = zip(blocks[line - shift], blocks[line])
                 wider.append([jnp.where(mask, high, low) for high, low in pairs])
         blocks = wider
-    extras = [zero] * 4
     for line in range(LINES_B):
         near, after = blocks[line]
-        pieces = []
         for v in range(4):
-            piece = jnp.where(groups[v], near, zero)
-            pieces.append(jnp.where(groups[v - 1], after, piece) if v else piece)
-        high, low = halves(jnp.concatenate(pieces, axis=0))
-        rows = pl.ds(CELLS_A * line, CELLS_A)
-        spread[k, rows, at] = high
-        spread[k, rows, low_at] = low
-        last = jnp.where(groups[3], after, zero)
-        if line % 4:
-            last = extras[line // 4] + pltpu.roll(last, 2 * (line % 4), 0)
-        extras[line // 4] = last
-    high, low = halves(jnp.concatenate(extras, axis=0))
-    spread[k, pl.ds(MAIN, CELLS_A), at] = high
-    spread[k, pl.ds(MAIN, CELLS_A), low_at] = low
+            piece = jnp.where(wide_groups[v], near, none)
+            piece = jnp.where(wide_groups[v - 1], after, piece) if v else piece
+            spread[k, pl.ds(2 * (CELLS_A * line + 8 * v), 16), at] = piece
+    beyond = (lax.broadcasted_iota(jnp.int32, (8, LANES), 0) >> 1) - place[2]
+    for v in range(3):
+        piece = zero
+        for j in range(4):
+            piece = jnp.where(beyond == j - 4 * v, rims[j], piece)
+        spread[k, pl.ds(2 * (MAIN + 8 * v), 16), at] = paired(piece)
+    spread[k, pl.ds(2 * (MAIN + 24), 16), at] = none
 
 
 def deposit_kernel(
@@ -199,12 +209,13 @@
         column = jnp.broadcast_to(row, (LANES, LANES)).T
         column = jnp.concatenate([column, column], axis=1)
         hot.append(jnp.where(cells == column, 1.0, 0.0).astype(BF16))
-    hot = jnp.concatenate(hot + hot, axis=0)
+    hot = jnp.concatenate(hot, axis=0)
     total = None
     for k in (1, 2, 3, 0):
         for tile in range(TILES):
             spread_tile(scaled, places[tile], spread, k, tile)
-        placed = dot(spread[k], hot)
+        placed = dot(spread[k], hot).reshape(SPREAD // 8, 2, 8, G)
+        placed = (placed[:, 0] + placed[:, 1]).reshape(SPREAD, G)
         placed = pltpu.roll(placed, k, 1) if k else placed
         total = placed if total is None else total + placed
     for block in range(LINES_B + 1):
@@ -501,7 +512,7 @@
             pltpu.VMEM((2, G, G), BF16),
             pltpu.VMEM((2, CELLS_B * KEPT, LANES), F32),
             pltpu.VMEM((64, TRI), F32),
-            pltpu.VMEM((4, SPREAD, 2 * TRI), BF16),
+            pltpu.VMEM((4, 2 * SPREAD, TRI), BF16),
             pltpu.VMEM((LINES, G), F32),
             pltpu.SemaphoreType.DMA((6,)),
         ],

time: 71.4 us -> 70.4 us (0.986)
  Pallas kernels: 14.4 us -> 13.4 us
    pallas_call x1, Pallas kernels: 5.61 us -> 4.64 us  [local(): pl.pallas_call(deposit_kernel, out_shape=(packed, *[jax.ShapeDtypeStruct(...]
where the time goes in v6:
time: 70.4 us; the launch traced here: 70.2 us
  starting transfers between devices  39.2 us (56%)
  waiting for transfers between devices  16.9 us (24%)
  Pallas kernels  13.4 us (19%)
  between operations  0.71 us (1%)
    all_to_all x2, starting transfers between devices, exchange(): lax.all_to_all(shaped, axes, split_axis=0, concat_axis=0, tiled=True)  22.9 us
    ppermute x9, starting transfers between devices, shifted(): lax.ppermute(value, axis, [(i, (i + by) % size) for i in range(size)])  16.3 us
    all_to_all x2, waiting for transfers between devices, exchange(): lax.all_to_all(shaped, axes, split_axis=0, concat_axis=0, tiled=True)  8.75 us
    ppermute x9, waiting for transfers between devices, shifted(): lax.ppermute(value, axis, [(i, (i + by) % size) for i in range(size)])  8.13 us
    pallas_call x1, Pallas kernels, local(): pl.pallas_call(deposit_kernel, out_shape=(packed, *[jax.ShapeDtypeStruct(...  4.64 us
    pallas_call x1, Pallas kernels, local(): pl.pallas_call(gather_kernel, out_shape=jax.ShapeDtypeStruct((1, TRI), F3...  3.01 us
    pallas_call x1, Pallas kernels, local(): pl.pallas_call(plane_kernel, out_shape=packed, compiler_params=params(12)...  2.64 us
    pallas_call x1, Pallas kernels, near_field(): pl.pallas_call(near_kernel, in_specs=[smem, smem, smem, vmem, vmem, vmem,...  2.43 us
  transfers between devices with their start and end apart: 11, of which 6 were waited for; matrix products, arithmetic and copies ran while one was open for 0% of the time, Pallas kernels for 4%

profile of v6, /device:TPU:1, one launch (start us, length us, event | category | flops | bytes accessed | tf_op | source)
XLA Modules:
  0.0 70.2 jit_solution(17908026852167238117)
XLA Ops:
  0.0 0.0 copy-start.3
  0.0 0.0 copy-start.4
  0.0 4.6 %deposit.1 = (f32[768,128]{1,0:T(8,128)}, f32[48,128]{1,0:T(8,128)S(1)}, f32[48,128]{1,0:T(8,128)S(1)}, f32[40,128]{1,0:T(8,128)S(1)}, f32[40,128]{1,0:T(8,128)S...) custom-call(f32[1,1024]{1,0:T(1,128)} %bitcast.10, ...), custom_call_target="tpu_custom_call" | custom-call | tf_op jit(solution)/shard_map/deposit/pallas_call | solution.py:504
  4.7 15.7 %all-to-all-start = ((f32[256,1,384]{2,1,0:T(1,128)}), f32[256,1,384]{2,1,0:T(1,128)S(1)}, u32[]{:S(2)}, u32[]{:S(2)}) async-start(f32[256,1,384]{2,1,0:T(1,128)} %bitcast.2), calls=%async_computation | async-start | bytes 786432 | tf_op jit(solution)/shard_map/all_to_all | solution.py:485
  20.3 1.5 %collective-permute-start.1 = (f32[40,128]{1,0:T(8,128)S(1)}, f32[40,128]{1,0:T(8,128)S(1)}, u32[]{:S(2)}, u32[]{:S(2)}) collective-permute-start(f32[40,128]{1,0:T(8,128)S(1)} %get-tuple-element.21), channel_id=1, source_target_pairs={{0,64},{32,96},{64,128},{96,160},{128,192},{160,224},{192,0},{224,... | collective-permute-start | bytes 61448 | tf_op jit(solution)/shard_map/ppermute | solution.py:452
  21.8 3.0 %collective-permute-start.2 = (f32[40,128]{1,0:T(8,128)S(1)}, f32[40,128]{1,0:T(8,128)S(1)}, u32[]{:S(2)}, u32[]{:S(2)}) collective-permute-start(f32[40,128]{1,0:T(8,128)S(1)} %get-tuple-element.22), channel_id=1, source_target_pairs={{0,96},{32,128},{64,160},{96,192},{128,224},{160,0},{192,32},{224,... | collective-permute-start | bytes 61448 | tf_op jit(solution)/shard_map/ppermute | solution.py:452
  24.8 0.0 collective-permute-start
  24.8 0.5 collective-permute-start.6
  25.3 1.3 %collective-permute-start.3 = (f32[40,128]{1,0:T(8,128)S(1)}, f32[40,128]{1,0:T(8,128)S(1)}, u32[]{:S(2)}, u32[]{:S(2)}) collective-permute-start(f32[40,128]{1,0:T(8,128)S(1)} %get-tuple-element.23), channel_id=1, source_target_pairs={{0,128},{32,160},{64,192},{96,224},{128,0},{160,32},{192,64},{224,... | collective-permute-start | bytes 61448 | tf_op jit(solution)/shard_map/ppermute | solution.py:452
  26.6 0.0 collective-permute-done.1.refs_2_
  26.6 2.6 %collective-permute-start.4 = (f32[40,128]{1,0:T(8,128)S(1)}, f32[40,128]{1,0:T(8,128)S(1)}, u32[]{:S(2)}, u32[]{:S(2)}) collective-permute-start(f32[40,128]{1,0:T(8,128)S(1)} %get-tuple-element.24), channel_id=1, source_target_pairs={{0,160},{32,192},{64,224},{96,0},{128,32},{160,64},{192,96},{224,1... | collective-permute-start | bytes 61448 | tf_op jit(solution)/shard_map/ppermute | solution.py:452
  29.2 0.0 collective-permute-done.2.refs_3_
  29.2 0.6 collective-permute-start.5
  29.8 0.1 collective-permute-done.3.refs_4_
  29.8 2.0 %collective-permute-done.4.refs_5_ = f32[40,128]{1,0:T(8,128)S(1)} collective-permute-done((f32[40,128]{1,0:T(8,128)S(1)}, f32[40,128]{1,0:T(8,128)S(1)}, u32[]{:S(2)}, u32[]{:S(2)}) %collective-permute-start.4) | collective-permute-done | bytes 20512 | tf_op jit(solution)/shard_map/ppermute | solution.py:452
  31.8 0.7 collective-permute-done.5.refs_6_
  32.5 0.0 collective-permute-done.refs_1_
  32.5 0.0 collective-permute-done.6.refs_7_
  32.5 0.7 %spectrum.1 = (f32[256,256]{1,0:T(8,128)S(1)}, f32[24,128]{1,0:T(8,128)S(1)}, f32[2,256,128]{2,1,0:T(8,128)S(1)}) custom-call(f32[48,128]{1,0:T(8,128)S(1)} %get-tuple-element.19.refs_0_, f32[48,128]{1,0:T(8,128)S(1)} %collective-permute-done.refs_1_, f32[40,128]{1,0:T(8,128)S(1)} %collective-permute-done.1.refs_2_, ...), custom_call_target="tpu_custom_call" | custom-call | tf_op jit(solution)/shard_map/spectrum/pallas_call | solution.py:535
  33.2 5.5 %all-to-all-done = f32[256,1,384]{2,1,0:T(1,128)S(1)} async-done(((f32[256,1,384]{2,1,0:T(1,128)}), f32[256,1,384]{2,1,0:T(1,128)S(1)}, u32[]{:S(2)}, u32[]{:S(2)}) %all-to-all-start) | async-done | bytes 393248 | tf_op jit(solution)/shard_map/all_to_all | solution.py:485
  38.7 0.0 copy-start
  38.7 0.0 copy-start.1
  38.7 0.0 copy-start.2
  38.7 2.6 %plane.1 = f32[768,128]{1,0:T(8,128)} custom-call(f32[768,128]{1,0:T(8,128)S(1)} %bitcast.8, f32[256,256]{1,0:T(8,128)S(1)} %get-tuple-element.27.spectrum_ref, f32[2,256,128]{2,1,0:T(8,128)S(1)} %get-tuple-element.28.waves_ref), custom_call_target="tpu_custom_call" | custom-call | tf_op jit(solution)/shard_map/plane/pallas_call | solution.py:546
  41.4 7.2 %all-to-all-start.1 = ((f32[256,1,384]{2,1,0:T(1,128)}), f32[256,1,384]{2,1,0:T(1,128)S(1)}, u32[]{:S(2)}, u32[]{:S(2)}) async-start(f32[256,1,384]{2,1,0:T(1,128)} %bitcast.4), calls=%async_computation.1 | async-start | bytes 786432 | tf_op jit(solution)/shard_map/all_to_all | solution.py:485
  48.6 1.6 %collective-permute-start.7 = (f32[24,128]{1,0:T(8,128)S(1)}, f32[24,128]{1,0:T(8,128)S(1)}, u32[]{:S(2)}, u32[]{:S(2)}) collective-permute-start(f32[24,128]{1,0:T(8,128)S(1)} %get-tuple-element.30.own_ref), channel_id=1, source_target_pairs={{0,1},{1,2},{2,3},{3,4},{4,5},{5,6},{6,7},{7,8},{8,9},{9,10},{10,1... | collective-permute-start | bytes 36872 | tf_op jit(solution)/shard_map/ppermute | solution.py:452
  50.2 5.3 %collective-permute-start.8 = (f32[24,128]{1,0:T(8,128)S(1)}, f32[24,128]{1,0:T(8,128)S(1)}, u32[]{:S(2)}, u32[]{:S(2)}) collective-permute-start(f32[24,128]{1,0:T(8,128)S(1)} %get-tuple-element.30.own_ref), channel_id=1, source_target_pairs={{0,31},{1,0},{2,1},{3,2},{4,3},{5,4},{6,5},{7,6},{8,7},{9,8},{10,9... | collective-permute-start | bytes 36872 | tf_op jit(solution)/shard_map/ppermute | solution.py:452
  56.1 5.4 %collective-permute-done.7.before_ref = f32[24,128]{1,0:T(8,128)S(1)} collective-permute-done((f32[24,128]{1,0:T(8,128)S(1)}, f32[24,128]{1,0:T(8,128)S(1)}, u32[]{:S(2)}, u32[]{:S(2)}) %collective-permute-start.7) | collective-permute-done | bytes 12320 | tf_op jit(solution)/shard_map/ppermute | solution.py:452
  61.5 0.0 collective-permute-done.8.after_ref
  61.5 0.0 copy-done.3
  61.5 0.0 copy-done.4
  61.5 2.4 %near.1.near_ref = f32[1,1024]{1,0:T(1,128)S(1)} custom-call(s32[1]{0:T(128)S(6)} %copy.12.count_ref, s32[32]{0:T(128)S(1)} %copy-done.3, s32[32]{0:T(128)S(1)} %copy-done.4, f32[24,128]{1,0:T(8,128)S(1)} %collective-permute-done.7.before_ref, f32[24,128]{1,0:T(8,128)S(1)} %get-tuple-element.30.own_ref, f32[24,128]{1,0:T(8,128)S(1)} %collective-permute-done.8.after_ref, ...), custom_call_target="tpu_custom_call" | custom-call | tf_op jit(solution)/shard_map/near/pallas_call | solution.py:460
  64.0 3.2 %all-to-all-done.1 = f32[256,1,384]{2,1,0:T(1,128)S(1)} async-done(((f32[256,1,384]{2,1,0:T(1,128)}), f32[256,1,384]{2,1,0:T(1,128)S(1)}, u32[]{:S(2)}, u32[]{:S(2)}) %all-to-all-start.1) | async-done | bytes 393248 | tf_op jit(solution)/shard_map/all_to_all | solution.py:485
  67.2 0.0 copy-done
  67.2 0.0 copy-done.1
  67.2 0.0 copy-done.2
  67.2 3.0 %gather.1 = f32[1,1024]{1,0:T(1,128)} custom-call(f32[768,128]{1,0:T(8,128)S(1)} %bitcast.7, s32[3,1024]{1,0:T(4,128)S(1)} %copy-done.2, f32[64,1024]{1,0:T(8,128)S(1)} %copy-done, bf16[2,256,256]{2,1,0:T(8,128)(2,1)S(1)} %copy-done.1, f32[1,1024]{1,0:T(1,128)S(1)} %near.1.near_ref), custom_call_target="tpu_custom_call" | custom-call | tf_op jit(solution)/shard_map/gather/pallas_call | solution.py:552
Async XLA Ops:
  0.0 61.5 %copy-start.3 = (s32[32]{0:T(128)S(1)}, s32[32]{0:T(128)}, u32[]{:S(2)}) copy-start(s32[32]{0:T(128)} %target_ref.1) | copy-start | bytes 388
  0.0 61.5 %copy-start.4 = (s32[32]{0:T(128)S(1)}, s32[32]{0:T(128)}, u32[]{:S(2)}) copy-start(s32[32]{0:T(128)} %source_ref.1) | copy-start | bytes 388
  4.7 34.1 %all-to-all-start = ((f32[256,1,384]{2,1,0:T(1,128)}), f32[256,1,384]{2,1,0:T(1,128)S(1)}, u32[]{:S(2)}, u32[]{:S(2)}) async-start(f32[256,1,384]{2,1,0:T(1,128)} %bitcast.2), calls=%async_computation | async-start | bytes 786432 | tf_op jit(solution)/shard_map/all_to_all | solution.py:485
  20.3 6.3 %collective-permute-start.1 = (f32[40,128]{1,0:T(8,128)S(1)}, f32[40,128]{1,0:T(8,128)S(1)}, u32[]{:S(2)}, u32[]{:S(2)}) collective-permute-start(f32[40,128]{1,0:T(8,128)S(1)} %get-tuple-element.21), channel_id=1, source_target_pairs={{0,64},{32,96},{64,128},{96,160},{128,192},{160,224},{192,0},{224,... | collective-permute-start | bytes 61448 | tf_op jit(solution)/shard_map/ppermute | solution.py:452
  21.8 7.4 %collective-permute-start.2 = (f32[40,128]{1,0:T(8,128)S(1)}, f32[40,128]{1,0:T(8,128)S(1)}, u32[]{:S(2)}, u32[]{:S(2)}) collective-permute-start(f32[40,128]{1,0:T(8,128)S(1)} %get-tuple-element.22), channel_id=1, source_target_pairs={{0,96},{32,128},{64,160},{96,192},{128,224},{160,0},{192,32},{224,... | collective-permute-start | bytes 61448 | tf_op jit(solution)/shard_map/ppermute | solution.py:452
  24.8 7.7 %collective-permute-start = (f32[48,128]{1,0:T(8,128)S(1)}, f32[48,128]{1,0:T(8,128)S(1)}, u32[]{:S(2)}, u32[]{:S(2)}) collective-permute-start(f32[48,128]{1,0:T(8,128)S(1)} %get-tuple-element.20), channel_id=1, source_target_pairs={{0,32},{32,64},{64,96},{96,128},{128,160},{160,192},{192,224},{224... | collective-permute-start | bytes 73736 | tf_op jit(solution)/shard_map/ppermute | solution.py:452
  24.8 7.7 %collective-permute-start.6 = (f32[48,128]{1,0:T(8,128)S(1)}, f32[48,128]{1,0:T(8,128)S(1)}, u32[]{:S(2)}, u32[]{:S(2)}) collective-permute-start(f32[48,128]{1,0:T(8,128)S(1)} %get-tuple-element.26), channel_id=1, source_target_pairs={{0,224},{32,0},{64,32},{96,64},{128,96},{160,128},{192,160},{224,1... | collective-permute-start | bytes 73736 | tf_op jit(solution)/shard_map/ppermute | solution.py:452
  25.3 4.5 %collective-permute-start.3 = (f32[40,128]{1,0:T(8,128)S(1)}, f32[40,128]{1,0:T(8,128)S(1)}, u32[]{:S(2)}, u32[]{:S(2)}) collective-permute-start(f32[40,128]{1,0:T(8,128)S(1)} %get-tuple-element.23), channel_id=1, source_target_pairs={{0,128},{32,160},{64,192},{96,224},{128,0},{160,32},{192,64},{224,... | collective-permute-start | bytes 61448 | tf_op jit(solution)/shard_map/ppermute | solution.py:452
  26.6 5.2 %collective-permute-start.4 = (f32[40,128]{1,0:T(8,128)S(1)}, f32[40,128]{1,0:T(8,128)S(1)}, u32[]{:S(2)}, u32[]{:S(2)}) collective-permute-start(f32[40,128]{1,0:T(8,128)S(1)} %get-tuple-element.24), channel_id=1, source_target_pairs={{0,160},{32,192},{64,224},{96,0},{128,32},{160,64},{192,96},{224,1... | collective-permute-start | bytes 61448 | tf_op jit(solution)/shard_map/ppermute | solution.py:452
  29.2 3.3 %collective-permute-start.5 = (f32[40,128]{1,0:T(8,128)S(1)}, f32[40,128]{1,0:T(8,128)S(1)}, u32[]{:S(2)}, u32[]{:S(2)}) collective-permute-start(f32[40,128]{1,0:T(8,128)S(1)} %get-tuple-element.25), channel_id=1, source_target_pairs={{0,192},{32,224},{64,0},{96,32},{128,64},{160,96},{192,128},{224,1... | collective-permute-start | bytes 61448 | tf_op jit(solution)/shard_map/ppermute | solution.py:452
  38.7 28.5 %copy-start = (f32[64,1024]{1,0:T(8,128)S(1)}, f32[64,1024]{1,0:T(8,128)}, u32[]{:S(2)}) copy-start(f32[64,1024]{1,0:T(8,128)} %weights_ref.1) | copy-start | bytes 786436
  38.7 28.5 %copy-start.1 = (bf16[2,256,256]{2,1,0:T(8,128)(2,1)S(1)}, bf16[2,256,256]{2,1,0:T(8,128)(2,1)}, u32[]{:S(2)}) copy-start(bf16[2,256,256]{2,1,0:T(8,128)(2,1)} %constant.2.clone.table_hbm.table_ref) | copy-start | bytes 786436
  38.7 28.5 %copy-start.2 = (s32[3,1024]{1,0:T(4,128)S(1)}, s32[3,1024]{1,0:T(4,128)}, u32[]{:S(2)}) copy-start(s32[3,1024]{1,0:T(4,128)} %anchors_ref.1) | copy-start | bytes 36868
  41.4 25.8 %all-to-all-start.1 = ((f32[256,1,384]{2,1,0:T(1,128)}), f32[256,1,384]{2,1,0:T(1,128)S(1)}, u32[]{:S(2)}, u32[]{:S(2)}) async-start(f32[256,1,384]{2,1,0:T(1,128)} %bitcast.4), calls=%async_computation.1 | async-start | bytes 786432 | tf_op jit(solution)/shard_map/all_to_all | solution.py:485
  48.6 12.9 %collective-permute-start.7 = (f32[24,128]{1,0:T(8,128)S(1)}, f32[24,128]{1,0:T(8,128)S(1)}, u32[]{:S(2)}, u32[]{:S(2)}) collective-permute-start(f32[24,128]{1,0:T(8,128)S(1)} %get-tuple-element.30.own_ref), channel_id=1, source_target_pairs={{0,1},{1,2},{2,3},{3,4},{4,5},{5,6},{6,7},{7,8},{8,9},{9,10},{10,1... | collective-permute-start | bytes 36872 | tf_op jit(solution)/shard_map/ppermute | solution.py:452
  50.2 11.3 %collective-permute-start.8 = (f32[24,128]{1,0:T(8,128)S(1)}, f32[24,128]{1,0:T(8,128)S(1)}, u32[]{:S(2)}, u32[]{:S(2)}) collective-permute-start(f32[24,128]{1,0:T(8,128)S(1)} %get-tuple-element.30.own_ref), channel_id=1, source_target_pairs={{0,31},{1,0},{2,1},{3,2},{4,3},{5,4},{6,5},{7,6},{8,7},{9,8},{10,9... | collective-permute-start | bytes 36872 | tf_op jit(solution)/shard_map/ppermute | solution.py:452

commit v7 on v6

--- a/solution.py
+++ b/solution.py
@@ -22,8 +22,8 @@
 SPREAD = MAIN + CELLS_A
 LANES = 128
 TILES = TRI // LANES
-KEPT = CELLS_A // 2 + 1
-SENT = 40
+HALF = ROWS // 2
+SENT = 2 * CELLS_A + 8
 CHUNK = 256
 PART = 8
 GROUPS = ((0, 4, 8), (1, 5, 9), (2, 6), (3, 7))
@@ -184,15 +184,15 @@
 def deposit_kernel(
     charges_hbm, anchors_hbm, weights_hbm, table_hbm, spectrum_hbm, out_ref, *rest
 ):
-    sent_refs = rest[:ROWS]
-    charges_ref, anchors_ref, weights_ref, table_ref, spectrum_ref = rest[ROWS : ROWS + 5]
-    scaled, spread, lines, sem = rest[ROWS + 5 :]
+    first_ref, sent_refs = rest[0], rest[1 : 1 + HALF]
+    charges_ref, anchors_ref, weights_ref, table_ref, spectrum_ref = rest[1 + HALF : 6 + HALF]
+    scaled, spread, lines, sem = rest[6 + HALF :]
     pairs = (
         (weights_hbm, weights_ref),
         (anchors_hbm, anchors_ref),
         (charges_hbm, charges_ref),
-        (spectrum_hbm.at[pl.ds(0, CELLS_B * KEPT), pl.ds(0, LANES)], spectrum_ref.at[0]),
-        (spectrum_hbm.at[pl.ds(0, CELLS_B * KEPT), pl.ds(LANES, LANES)], spectrum_ref.at[1]),
+        (spectrum_hbm.at[:, pl.ds(0, LANES)], spectrum_ref.at[0]),
+        (spectrum_hbm.at[:, pl.ds(LANES, LANES)], spectrum_ref.at[1]),
         (table_hbm, table_ref),
     )
     copies = [pltpu.make_async_copy(a, b, sem.at[n]) for n, (a, b) in enumerate(pairs)]
@@ -226,16 +226,38 @@
     result = table_dot((table_ref[0], table_ref[1]), halves(lines[...]), ((1,), (1,)))
     for v in range(3):
         out_ref[pl.ds(v, G, stride=3), :] = result[:, LANES * v : LANES * (v + 1)]
-    for shift, sent in enumerate(sent_refs):
-        c = (lax.axis_index("row") + shift) & (ROWS - 1)
-        sent[pl.ds(SENT - 8, 8), :] = jnp.zeros((8, LANES), F32)
+    for half in range(2):
+        first_ref[pl.ds(CELLS_B * half, CELLS_B), :] = spectrum_ref[half, pl.ds(0, CELLS_B), :]
+    for step, sent in enumerate(sent_refs):
+        c = lax.axis_index("row") ^ step
         for half in range(2):
-            rows = spectrum_ref[half, pl.ds(c, KEPT, stride=CELLS_B), :]
-            sent[pl.ds(half * KEPT, KEPT), :] = rows
-    for shift in (0, 1, ROWS - 1):
-        for block in range(8):
-            at = pl.ds(block * LANES, LANES)
-            sent_refs[shift][pl.ds(SENT + block, 1), :] = charges_ref[:, at]
+            rows = spectrum_ref[half, pl.ds(c, CELLS_A, stride=CELLS_B), :]
+            sent[pl.ds(CELLS_A * half, CELLS_A), :] = rows
+    for block in range(8):
+        charges = charges_ref[:, pl.ds(block * LANES, LANES)]
+        first_ref[pl.ds(16 + block, 1), :] = charges
+        for sent in sent_refs:
+            sent[pl.ds(2 * CELLS_A + block, 1), :] = charges
+
+
+def join_kernel(first_ref, *refs):
+    row = lax.axis_index("row")
+    for step in range(1, HALF):
+        sent, out = refs[step - 1], refs[step + HALF - 2]
+        out[pl.ds(0, SENT), :] = sent[...]
+        out[pl.ds(SENT, 8), :] = line_of(first_ref, row ^ step)
+
+
+def line_of(first_ref, c):
+    halves_of = [first_ref[pl.ds(c + CELLS_B * half, 1), :] for half in range(2)]
+    return jnp.concatenate([*halves_of, jnp.zeros((6, LANES), F32)], axis=0)
+
+
+def waves_kernel(_, waves_ref):
+    for half in range(2):
+        cell = lax.broadcasted_iota(jnp.int32, (G, LANES), 0) - 1
+        wave = lax.broadcasted_iota(jnp.int32, (G, LANES), 1) + LANES * half
+        waves_ref[half] = cas_of(cell * wave)
 
 
 def cas_of(turns):
@@ -249,29 +271,37 @@
     return value * angle
 
 
-def spectrum_kernel(*refs):
-    sent_refs, (out_ref, beside_ref, waves_ref, joined) = refs[:ROWS], refs[ROWS:]
-    for shift, sent in enumerate(sent_refs):
-        owner = (lax.axis_index("row") - shift) & (ROWS - 1)
-        at = pl.ds(pl.multiple_of(owner * SENT, 8), SENT)
-        joined[at, :] = sent[pl.ds(0, SENT), :]
-    for place, shift in enumerate((1, 0, ROWS - 1)):
-        beside_ref[pl.ds(8 * place, 8), :] = sent_refs[shift][pl.ds(SENT, 8), :]
-    line = lax.broadcasted_iota(jnp.int32, (G, ROWS * SENT), 0)
-    folded = jnp.minimum(line, G - line)
-    block, inside = folded >> 5, folded & (CELLS_A - 1)
-    mirrored = inside >= KEPT
-    owner = jnp.where(mirrored, ROWS - 1 - block, block)
-    inside = jnp.where(mirrored, CELLS_A - inside, inside)
-    place = lax.broadcasted_iota(jnp.int32, (G, ROWS * SENT), 1) - (owner * SENT + inside)
+def spectrum_kernel(first_ref, own_ref, *refs):
+    received, (out_ref, beside_ref, joined) = refs[: HALF - 1], refs[HALF - 1 :]
+    row = lax.axis_index("row")
+    place = row & (HALF - 1)
+    missing = line_of(first_ref, row)
+    for step, ref in enumerate((own_ref, *received)):
+        at = pl.ds(pl.multiple_of(2 * CELLS_A * (place ^ step), 2 * CELLS_A), 2 * CELLS_A)
+        joined[at, :] = ref[pl.ds(0, 2 * CELLS_A), :]
+        if step:
+            missing = jnp.where(place ^ step == HALF - 1, ref[pl.ds(SENT, 8), :], missing)
+    joined[pl.ds(2 * CELLS_A * HALF, 8), :] = missing
+    charges = pl.ds(2 * CELLS_A, 8)
+    nearest = received[0][charges, :]
+    outside = (place == 0) | (place == HALF - 1)
+    other = jnp.where(outside, first_ref[pl.ds(16, 8), :], received[2][charges, :])
+    odd = (row & 1) == 1
+    beside_ref[pl.ds(0, 8), :] = jnp.where(odd, nearest, other)
+    beside_ref[pl.ds(8, 8), :] = own_ref[charges, :]
+    beside_ref[pl.ds(16, 8), :] = jnp.where(odd, other, nearest)
+    shape = (G, joined.shape[0])
+    line = lax.broadcasted_iota(jnp.int32, shape, 0)
+    line = jnp.minimum(line, G - line)
+    line = jnp.where(row >= HALF, G // 2 - line, line)
+    source = 2 * CELLS_A * (line >> 5) + (line & (CELLS_A - 1))
+    pitch = jnp.where(line == G // 2, 1, CELLS_A)
+    source = lax.broadcasted_iota(jnp.int32, shape, 1) - source
     parts = thirds(joined[...])
     for half in range(2):
-        chosen = jnp.where(place == half * KEPT, 1.0, 0.0).astype(BF16)
+        chosen = jnp.where(source == half * pitch, 1.0, 0.0).astype(BF16)
         value = sum(dot(chosen, part) for part in parts)
         out_ref[:, pl.ds(LANES * half, LANES)] = value * (1.0 / (G * G * G))
-        cell = lax.broadcasted_iota(jnp.int32, (G, LANES), 0) - 1
-        wave = lax.broadcasted_iota(jnp.int32, (G, LANES), 1) + LANES * half
-        waves_ref[half] = cas_of(cell * wave)
 
 
 def plane_kernel(tiles_ref, spectrum_ref, waves_ref, out_ref):
@@ -480,6 +510,10 @@
     )
 
 
+def swapped(value, mask):
+    return lax.ppermute(value, "row", [(i, i ^ mask) for i in range(ROWS)])
+
+
 def exchange(values, axes, pieces):
     shaped = values.reshape(pieces, 1, values.size // pieces)
     moved = lax.all_to_all(shaped, axes, split_axis=0, concat_axis=0, tiled=True)
@@ -500,17 +534,16 @@
     devices = ROWS * COLS
     packed = jax.ShapeDtypeStruct((devices * LINES // LANES, LANES), F32)
     hbm = pl.BlockSpec(memory_space=pltpu.HBM)
-    sizes = [SENT + 8 if shift in (0, 1, ROWS - 1) else SENT for shift in range(ROWS)]
-    deposited, *sent = pl.pallas_call(
+    deposited, first, *sent = pl.pallas_call(
         deposit_kernel,
-        out_shape=(packed, *[jax.ShapeDtypeStruct((size, LANES), F32) for size in sizes]),
+        out_shape=(packed, *[jax.ShapeDtypeStruct((size, LANES), F32) for size in (24, *[SENT] * HALF)]),
         in_specs=[hbm] * 5,
         scratch_shapes=[
             pltpu.VMEM((1, TRI), F32),
             pltpu.VMEM((3, TRI), jnp.int32),
             pltpu.VMEM((64, TRI), F32),
             pltpu.VMEM((2, G, G), BF16),
-            pltpu.VMEM((2, CELLS_B * KEPT, LANES), F32),
+            pltpu.VMEM((2, CELLS_A * CELLS_B, LANES), F32),
             pltpu.VMEM((64, TRI), F32),
             pltpu.VMEM((4, 2 * SPREAD, TRI), BF16),
             pltpu.VMEM((LINES, G), F32),
@@ -531,18 +564,30 @@
         ]
     )
     received = exchange(deposited, BOTH, devices)
-    sent = [shifted(value, "row", shift) if shift else value for shift, value in enumerate(sent)]
-    spectrum, beside, waves = pl.pallas_call(
+    first = swapped(first, ROWS - 1)
+    joined = pl.pallas_call(
+        join_kernel,
+        out_shape=[jax.ShapeDtypeStruct((SENT + 8, LANES), F32)] * (HALF - 1),
+        compiler_params=params(8),
+        name="join",
+    )(first, *sent[1:])
+    joined = [swapped(value, step + 1) for step, value in enumerate(joined)]
+    waves = pl.pallas_call(
+        waves_kernel,
+        out_shape=jax.ShapeDtypeStruct((2, G, LANES), F32),
+        compiler_params=params(8),
+        name="waves",
+    )(first)
+    spectrum, beside = pl.pallas_call(
         spectrum_kernel,
         out_shape=(
             jax.ShapeDtypeStruct((G, G), F32),
             jax.ShapeDtypeStruct((24, LANES), F32),
-            jax.ShapeDtypeStruct((2, G, LANES), F32),
         ),
-        scratch_shapes=[pltpu.VMEM((ROWS * SENT, LANES), F32)],
+        scratch_shapes=[pltpu.VMEM((2 * CELLS_A * HALF + 8, LANES), F32)],
         compiler_params=params(8),
         name="spectrum",
-    )(*sent)
+    )(first, sent[0], *joined)
     handed = pl.pallas_call(
         plane_kernel, out_shape=packed, compiler_params=params(12), name="plane"
     )(received, spectrum, waves)

time: 70.4 us -> 69.2 us (0.983)
  starting transfers between devices: 39.2 us -> 35 us
  waiting for transfers between devices: 16.9 us -> 19.7 us
    ppermute x9 -> x2, starting transfers between devices: 16.3 us -> 6.66 us  [shifted(): lax.ppermute(value, axis, [(i, (i + by) % size) for i in range(size)])]
    ppermute x0 -> x4, starting transfers between devices: none -> 6.74 us  [swapped(): return lax.ppermute(value, 'row', [(i, i ^ mask) for i in range(ROWS)])]
    ppermute x0 -> x4, waiting for transfers between devices: none -> 5.5 us  [swapped(): return lax.ppermute(value, 'row', [(i, i ^ mask) for i in range(ROWS)])]
    ppermute x9 -> x2, waiting for transfers between devices: 8.13 us -> 5.58 us  [shifted(): lax.ppermute(value, axis, [(i, (i + by) % size) for i in range(size)])]
    all_to_all x2, starting transfers between devices: 22.9 us -> 21.6 us  [exchange(): lax.all_to_all(shaped, axes, split_axis=0, concat_axis=0, tiled=True)]
  transfers between devices with their start and end apart: 11 -> 8, of which waited for: 6 -> 6; matrix products, arithmetic and copies ran while one was open for 0% -> 0% of each run, Pallas kernels for 4% -> 5%
where the time goes in v7:
time: 69.2 us; the launch traced here: 69 us
  starting transfers between devices  35 us (51%)
  waiting for transfers between devices  19.7 us (28%)
  Pallas kernels  13.5 us (20%)
  between operations  0.73 us (1%)
    all_to_all x2, starting transfers between devices, exchange(): lax.all_to_all(shaped, axes, split_axis=0, concat_axis=0, tiled=True)  21.6 us
    all_to_all x2, waiting for transfers between devices, exchange(): lax.all_to_all(shaped, axes, split_axis=0, concat_axis=0, tiled=True)  8.65 us
    ppermute x4, starting transfers between devices, swapped(): return lax.ppermute(value, 'row', [(i, i ^ mask) for i in range(ROWS)])  6.74 us
    ppermute x2, starting transfers between devices, shifted(): lax.ppermute(value, axis, [(i, (i + by) % size) for i in range(size)])  6.66 us
    ppermute x2, waiting for transfers between devices, shifted(): lax.ppermute(value, axis, [(i, (i + by) % size) for i in range(size)])  5.58 us
    ppermute x4, waiting for transfers between devices, swapped(): return lax.ppermute(value, 'row', [(i, i ^ mask) for i in range(ROWS)])  5.5 us
    pallas_call x1, Pallas kernels, local(): pl.pallas_call(deposit_kernel, out_shape=(packed, *[jax.ShapeDtypeStruct(...  4.65 us
    pallas_call x1, Pallas kernels, local(): pl.pallas_call(gather_kernel, out_shape=jax.ShapeDtypeStruct((1, TRI), F3...  3.02 us
  transfers between devices with their start and end apart: 8, of which 6 were waited for; matrix products, arithmetic and copies ran while one was open for 0% of the time, Pallas kernels for 5%

profile of v7, /device:TPU:1, one launch (start us, length us, event | category | flops | bytes accessed | tf_op | source)
XLA Modules:
  0.0 69.0 jit_solution(2367290437496860025)
XLA Ops:
  0.0 0.0 copy-start.3
  0.0 0.0 copy-start.4
  0.0 4.6 %deposit.1 = (f32[768,128]{1,0:T(8,128)}, f32[24,128]{1,0:T(8,128)S(1)}, f32[72,128]{1,0:T(8,128)S(1)}, f32[72,128]{1,0:T(8,128)S(1)}, f32[72,128]{1,0:T(8,128)S(1)}, /*index=5*/f32[72,128]{1,0:T(8,128)S(1)}) custom-call(f32[1,1024]{1,0:T(1,128)} %bitcast.10, s32[3,1024]{1,0:T(4,128)} %anchors_ref.1, f32[64,1024]{1,0:T(8,128)} %weights_ref.1, ...), custom_call_target="tpu_custom_call" | custom-call | tf_op jit(solution)/shard_map/deposit/pallas_call | solution.py:537
  4.7 15.7 %all-to-all-start = ((f32[256,1,384]{2,1,0:T(1,128)}), f32[256,1,384]{2,1,0:T(1,128)S(1)}, u32[]{:S(2)}, u32[]{:S(2)}) async-start(f32[256,1,384]{2,1,0:T(1,128)} %bitcast.2), calls=%async_computation | async-start | bytes 786432 | tf_op jit(solution)/shard_map/all_to_all | solution.py:519
  20.3 3.0 %collective-permute-start = (f32[24,128]{1,0:T(8,128)S(1)}, f32[24,128]{1,0:T(8,128)S(1)}, u32[]{:S(2)}, u32[]{:S(2)}) collective-permute-start(f32[24,128]{1,0:T(8,128)S(1)} %get-tuple-element.18), channel_id=1, source_target_pairs={{0,224},{32,192},{64,160},{96,128},{128,96},{160,64},{192,32},{224... | collective-permute-start | bytes 36872 | tf_op jit(solution)/shard_map/ppermute | solution.py:514
  23.3 1.7 %collective-permute-done.first_ref._ = f32[24,128]{1,0:T(8,128)S(1)} collective-permute-done((f32[24,128]{1,0:T(8,128)S(1)}, f32[24,128]{1,0:T(8,128)S(1)}, u32[]{:S(2)}, u32[]{:S(2)}) %collective-permute-start) | collective-permute-done | bytes 12320 | tf_op jit(solution)/shard_map/ppermute | solution.py:514
  25.1 2.0 %collective-permute-start.1 = (f32[80,128]{1,0:T(8,128)S(1)}, f32[80,128]{1,0:T(8,128)S(1)}, u32[]{:S(2)}, u32[]{:S(2)}) collective-permute-start(f32[80,128]{1,0:T(8,128)S(1)} %get-tuple-element.23), channel_id=1, source_target_pairs={{0,32},{32,0},{64,96},{96,64},{128,160},{160,128},{192,224},{224,1... | collective-permute-start | bytes 122888 | tf_op jit(solution)/shard_map/ppermute | solution.py:514
  27.1 0.0 collective-permute-start.2
  27.1 1.7 %collective-permute-start.3 = (f32[80,128]{1,0:T(8,128)S(1)}, f32[80,128]{1,0:T(8,128)S(1)}, u32[]{:S(2)}, u32[]{:S(2)}) collective-permute-start(f32[80,128]{1,0:T(8,128)S(1)} %get-tuple-element.25), channel_id=1, source_target_pairs={{0,96},{32,64},{64,32},{96,0},{128,224},{160,192},{192,160},{224,1... | collective-permute-start | bytes 122888 | tf_op jit(solution)/shard_map/ppermute | solution.py:514
  28.8 0.2 waves.1.waves_ref
  29.0 0.0 collective-permute-done.1.refs_0_
  29.1 1.9 %collective-permute-done.2.refs_1_ = f32[80,128]{1,0:T(8,128)S(1)} collective-permute-done((f32[80,128]{1,0:T(8,128)S(1)}, f32[80,128]{1,0:T(8,128)S(1)}, u32[]{:S(2)}, u32[]{:S(2)}) %collective-permute-start.2) | collective-permute-done | bytes 40992 | tf_op jit(solution)/shard_map/ppermute | solution.py:514
  31.0 1.8 %collective-permute-done.3.refs_2_ = f32[80,128]{1,0:T(8,128)S(1)} collective-permute-done((f32[80,128]{1,0:T(8,128)S(1)}, f32[80,128]{1,0:T(8,128)S(1)}, u32[]{:S(2)}, u32[]{:S(2)}) %collective-permute-start.3) | collective-permute-done | bytes 40992 | tf_op jit(solution)/shard_map/ppermute | solution.py:514
  32.8 0.5 spectrum.1
  33.3 5.4 %all-to-all-done = f32[256,1,384]{2,1,0:T(1,128)S(1)} async-done(((f32[256,1,384]{2,1,0:T(1,128)}), f32[256,1,384]{2,1,0:T(1,128)S(1)}, u32[]{:S(2)}, u32[]{:S(2)}) %all-to-all-start) | async-done | bytes 393248 | tf_op jit(solution)/shard_map/all_to_all | solution.py:519
  38.8 0.0 copy-start
  38.8 0.0 copy-start.1
  38.8 0.0 copy-start.2
  38.8 2.7 %plane.1 = f32[768,128]{1,0:T(8,128)} custom-call(f32[768,128]{1,0:T(8,128)S(1)} %bitcast.8, f32[256,256]{1,0:T(8,128)S(1)} %get-tuple-element.26.spectrum_ref, f32[2,256,128]{2,1,0:T(8,128)S(1)} %waves.1.waves_ref), custom_call_target="tpu_custom_call" | custom-call | tf_op jit(solution)/shard_map/plane/pallas_call | solution.py:591
  41.4 6.0 %all-to-all-start.1 = ((f32[256,1,384]{2,1,0:T(1,128)}), f32[256,1,384]{2,1,0:T(1,128)S(1)}, u32[]{:S(2)}, u32[]{:S(2)}) async-start(f32[256,1,384]{2,1,0:T(1,128)} %bitcast.4), calls=%async_computation.1 | async-start | bytes 786432 | tf_op jit(solution)/shard_map/all_to_all | solution.py:519
  47.4 1.6 %collective-permute-start.4 = (f32[24,128]{1,0:T(8,128)S(1)}, f32[24,128]{1,0:T(8,128)S(1)}, u32[]{:S(2)}, u32[]{:S(2)}) collective-permute-start(f32[24,128]{1,0:T(8,128)S(1)} %get-tuple-element.28.own_ref), channel_id=1, source_target_pairs={{0,1},{1,2},{2,3},{3,4},{4,5},{5,6},{6,7},{7,8},{8,9},{9,10},{10,1... | collective-permute-start | bytes 36872 | tf_op jit(solution)/shard_map/ppermute | solution.py:482
  49.0 5.1 %collective-permute-start.5 = (f32[24,128]{1,0:T(8,128)S(1)}, f32[24,128]{1,0:T(8,128)S(1)}, u32[]{:S(2)}, u32[]{:S(2)}) collective-permute-start(f32[24,128]{1,0:T(8,128)S(1)} %get-tuple-element.28.own_ref), channel_id=1, source_target_pairs={{0,31},{1,0},{2,1},{3,2},{4,3},{5,4},{6,5},{7,6},{8,7},{9,8},{10,9... | collective-permute-start | bytes 36872 | tf_op jit(solution)/shard_map/ppermute | solution.py:482
  54.7 5.6 %collective-permute-done.4.before_ref = f32[24,128]{1,0:T(8,128)S(1)} collective-permute-done((f32[24,128]{1,0:T(8,128)S(1)}, f32[24,128]{1,0:T(8,128)S(1)}, u32[]{:S(2)}, u32[]{:S(2)}) %collective-permute-start.4) | collective-permute-done | bytes 12320 | tf_op jit(solution)/shard_map/ppermute | solution.py:482
  60.3 0.0 collective-permute-done.5.after_ref
  60.3 0.0 copy-done.3
  60.3 0.0 copy-done.4
  60.3 2.4 %near.1.near_ref = f32[1,1024]{1,0:T(1,128)S(1)} custom-call(s32[1]{0:T(128)S(6)} %copy.12.count_ref, s32[32]{0:T(128)S(1)} %copy-done.3, s32[32]{0:T(128)S(1)} %copy-done.4, f32[24,128]{1,0:T(8,128)S(1)} %collective-permute-done.4.before_ref, f32[24,128]{1,0:T(8,128)S(1)} %get-tuple-element.28.own_ref, f32[24,128]{1,0:T(8,128)S(1)} %collective-permute-done.5.after_ref, ...), custom_call_target="tpu_custom_call" | custom-call | tf_op jit(solution)/shard_map/near/pallas_call | solution.py:490
  62.8 3.2 %all-to-all-done.1 = f32[256,1,384]{2,1,0:T(1,128)S(1)} async-done(((f32[256,1,384]{2,1,0:T(1,128)}), f32[256,1,384]{2,1,0:T(1,128)S(1)}, u32[]{:S(2)}, u32[]{:S(2)}) %all-to-all-start.1) | async-done | bytes 393248 | tf_op jit(solution)/shard_map/all_to_all | solution.py:519
  66.0 0.0 copy-done
  66.0 0.0 copy-done.1
  66.0 0.0 copy-done.2
  66.0 3.0 %gather.1 = f32[1,1024]{1,0:T(1,128)} custom-call(f32[768,128]{1,0:T(8,128)S(1)} %bitcast.7, s32[3,1024]{1,0:T(4,128)S(1)} %copy-done.2, f32[64,1024]{1,0:T(8,128)S(1)} %copy-done, bf16[2,256,256]{2,1,0:T(8,128)(2,1)S(1)} %copy-done.1, f32[1,1024]{1,0:T(1,128)S(1)} %near.1.near_ref), custom_call_target="tpu_custom_call" | custom-call | tf_op jit(solution)/shard_map/gather/pallas_call | solution.py:597
  (1 shorter events, 0.0 us)
Async XLA Ops:
  0.0 60.3 %copy-start.3 = (s32[32]{0:T(128)S(1)}, s32[32]{0:T(128)}, u32[]{:S(2)}) copy-start(s32[32]{0:T(128)} %target_ref.1) | copy-start | bytes 388
  0.0 60.3 %copy-start.4 = (s32[32]{0:T(128)S(1)}, s32[32]{0:T(128)}, u32[]{:S(2)}) copy-start(s32[32]{0:T(128)} %source_ref.1) | copy-start | bytes 388
  4.7 34.1 %all-to-all-start = ((f32[256,1,384]{2,1,0:T(1,128)}), f32[256,1,384]{2,1,0:T(1,128)S(1)}, u32[]{:S(2)}, u32[]{:S(2)}) async-start(f32[256,1,384]{2,1,0:T(1,128)} %bitcast.2), calls=%async_computation | async-start | bytes 786432 | tf_op jit(solution)/shard_map/all_to_all | solution.py:519
  20.3 4.7 %collective-permute-start = (f32[24,128]{1,0:T(8,128)S(1)}, f32[24,128]{1,0:T(8,128)S(1)}, u32[]{:S(2)}, u32[]{:S(2)}) collective-permute-start(f32[24,128]{1,0:T(8,128)S(1)} %get-tuple-element.18), channel_id=1, source_target_pairs={{0,224},{32,192},{64,160},{96,128},{128,96},{160,64},{192,32},{224... | collective-permute-start | bytes 36872 | tf_op jit(solution)/shard_map/ppermute | solution.py:514
  25.1 4.0 %collective-permute-start.1 = (f32[80,128]{1,0:T(8,128)S(1)}, f32[80,128]{1,0:T(8,128)S(1)}, u32[]{:S(2)}, u32[]{:S(2)}) collective-permute-start(f32[80,128]{1,0:T(8,128)S(1)} %get-tuple-element.23), channel_id=1, source_target_pairs={{0,32},{32,0},{64,96},{96,64},{128,160},{160,128},{192,224},{224,1... | collective-permute-start | bytes 122888 | tf_op jit(solution)/shard_map/ppermute | solution.py:514
  27.1 3.9 %collective-permute-start.2 = (f32[80,128]{1,0:T(8,128)S(1)}, f32[80,128]{1,0:T(8,128)S(1)}, u32[]{:S(2)}, u32[]{:S(2)}) collective-permute-start(f32[80,128]{1,0:T(8,128)S(1)} %get-tuple-element.24), channel_id=1, source_target_pairs={{0,64},{32,96},{64,0},{96,32},{128,192},{160,224},{192,128},{224,1... | collective-permute-start | bytes 122888 | tf_op jit(solution)/shard_map/ppermute | solution.py:514
  27.1 5.7 %collective-permute-start.3 = (f32[80,128]{1,0:T(8,128)S(1)}, f32[80,128]{1,0:T(8,128)S(1)}, u32[]{:S(2)}, u32[]{:S(2)}) collective-permute-start(f32[80,128]{1,0:T(8,128)S(1)} %get-tuple-element.25), channel_id=1, source_target_pairs={{0,96},{32,64},{64,32},{96,0},{128,224},{160,192},{192,160},{224,1... | collective-permute-start | bytes 122888 | tf_op jit(solution)/shard_map/ppermute | solution.py:514
  38.8 27.2 %copy-start = (f32[64,1024]{1,0:T(8,128)S(1)}, f32[64,1024]{1,0:T(8,128)}, u32[]{:S(2)}) copy-start(f32[64,1024]{1,0:T(8,128)} %weights_ref.1) | copy-start | bytes 786436
  38.8 27.2 %copy-start.1 = (bf16[2,256,256]{2,1,0:T(8,128)(2,1)S(1)}, bf16[2,256,256]{2,1,0:T(8,128)(2,1)}, u32[]{:S(2)}) copy-start(bf16[2,256,256]{2,1,0:T(8,128)(2,1)} %constant.2.clone.table_hbm.table_ref) | copy-start | bytes 786436
  38.8 27.2 %copy-start.2 = (s32[3,1024]{1,0:T(4,128)S(1)}, s32[3,1024]{1,0:T(4,128)}, u32[]{:S(2)}) copy-start(s32[3,1024]{1,0:T(4,128)} %anchors_ref.1) | copy-start | bytes 36868
  41.4 24.6 %all-to-all-start.1 = ((f32[256,1,384]{2,1,0:T(1,128)}), f32[256,1,384]{2,1,0:T(1,128)S(1)}, u32[]{:S(2)}, u32[]{:S(2)}) async-start(f32[256,1,384]{2,1,0:T(1,128)} %bitcast.4), calls=%async_computation.1 | async-start | bytes 786432 | tf_op jit(solution)/shard_map/all_to_all | solution.py:519
  47.4 12.9 %collective-permute-start.4 = (f32[24,128]{1,0:T(8,128)S(1)}, f32[24,128]{1,0:T(8,128)S(1)}, u32[]{:S(2)}, u32[]{:S(2)}) collective-permute-start(f32[24,128]{1,0:T(8,128)S(1)} %get-tuple-element.28.own_ref), channel_id=1, source_target_pairs={{0,1},{1,2},{2,3},{3,4},{4,5},{5,6},{6,7},{7,8},{8,9},{9,10},{10,1... | collective-permute-start | bytes 36872 | tf_op jit(solution)/shard_map/ppermute | solution.py:482
  49.0 11.3 %collective-permute-start.5 = (f32[24,128]{1,0:T(8,128)S(1)}, f32[24,128]{1,0:T(8,128)S(1)}, u32[]{:S(2)}, u32[]{:S(2)}) collective-permute-start(f32[24,128]{1,0:T(8,128)S(1)} %get-tuple-element.28.own_ref), channel_id=1, source_target_pairs={{0,31},{1,0},{2,1},{3,2},{4,3},{5,4},{6,5},{7,6},{8,7},{9,8},{10,9... | collective-permute-start | bytes 36872 | tf_op jit(solution)/shard_map/ppermute | solution.py:482

commit v8 on v7

--- a/solution.py
+++ b/solution.py
@@ -26,6 +26,7 @@
 SENT = 2 * CELLS_A + 8
 CHUNK = 256
 PART = 8
+SHIFTS = 5
 GROUPS = ((0, 4, 8), (1, 5, 9), (2, 6), (3, 7))
 F32 = jnp.float32
 BF16 = jnp.bfloat16
@@ -101,8 +102,8 @@
 
 
 def onehot(anchors_ref):
-    cells = lax.broadcasted_iota(jnp.int32, (G, TRI), 0)
-    matched = cells == anchors_ref[2:3, :]
+    cells = lax.broadcasted_iota(jnp.int32, (LANES, TRI), 0)
+    matched = cells == anchors_ref[2:3, :] >> 1
     return jnp.where(matched, 1.0, 0.0).astype(BF16)
 
 
@@ -383,16 +384,18 @@
             out_ref[pl.ds(96 * r + v, CELLS_A, stride=3), :] = value
 
 
-def gather_tile(weights_ref, place, picked, tile, base, at):
+def gather_tile(weights_ref, anchors_ref, place, picked, tile, base, at):
     near_masks, next_masks, groups, bits = masks_of(place)
     weights_at = pl.ds(tile * LANES, LANES)
+    odd = jnp.broadcast_to((anchors_ref[2:3, weights_at] & 1) != 0, (8, LANES))
     total = jnp.zeros((8, LANES), F32)
-    for k in range(4):
+    before = None
+    for shift in range(SHIFTS):
         blocks = []
         for line in range(LINES_B):
-            start = SPREAD * k + CELLS_A * line
+            start = SPREAD * shift + CELLS_A * line
             rows = [picked[base, pl.ds(start + 8 * v, 8), at] for v in range(4)]
-            last = picked[base, pl.ds(SPREAD * k + MAIN + 8 * (line // 4), 8), at]
+            last = picked[base, pl.ds(SPREAD * shift + MAIN + 8 * (line // 4), 8), at]
             rows.append(pltpu.roll(last, 8 - 2 * (line % 4), 0) if line % 4 else last)
             pair = []
             for skip in range(2):
@@ -401,19 +404,22 @@
                     chosen = jnp.where(groups[g], rows[g + skip], chosen)
                 pair.append(chosen)
             blocks.append(pair)
-        for mask, shift, count in zip(bits[::-1], (4, 2, 1), (7, 5, 4)):
+        for mask, width, count in zip(bits[::-1], (4, 2, 1), (7, 5, 4)):
             fewer = []
             for line in range(count):
                 low = blocks[line]
-                if line + shift < len(blocks):
-                    high = blocks[line + shift]
+                if line + width < len(blocks):
+                    high = blocks[line + width]
                     low = [jnp.where(mask, h, l) for h, l in zip(high, low)]
                 fewer.append(low)
             blocks = fewer
-        for j in range(4):
-            rows = stencil_rows(weights_ref, j, k, weights_at)
-            near, after = two_rows(rows, near_masks, next_masks)
-            total = total + (near * blocks[j][0] + after * blocks[j][1])
+        if shift:
+            for j in range(4):
+                rows = stencil_rows(weights_ref, j, shift - 1, weights_at)
+                weights = two_rows(rows, near_masks, next_masks)
+                for weight, high, low in zip(weights, blocks[j], before[j]):
+                    total = total + weight * jnp.where(odd, high, low)
+        before = blocks
     return jnp.sum(total, axis=0, keepdims=True)
 
 
@@ -424,10 +430,12 @@
     turned = halves(jnp.concatenate(turned, axis=0))
     lines[...] = dot_table(turned, (table_ref[0], table_ref[1]))
     field = jnp.concatenate([lines[block_place(b), :] for b in range(LINES_B + 1)], axis=0)
-    for k in range(4):
-        high, low = halves(pltpu.roll(field, G - k, 1) if k else field)
-        parts[pl.ds(SPREAD * k, SPREAD), pl.ds(0, G)] = high
-        parts[pl.ds(SPREAD * k, SPREAD), pl.ds(G, G)] = low
+    for shift in range(SHIFTS):
+        value = field[:, LANES * (shift % 2) : LANES * (shift % 2 + 1)]
+        high, low = halves(pltpu.roll(value, LANES - shift // 2, 1) if shift > 1 else value)
+        rows = pl.ds(SPREAD * shift, SPREAD)
+        parts[rows, pl.ds(0, LANES)] = high
+        parts[rows, pl.ds(LANES, LANES)] = low
     hot = onehot(anchors_ref)
     hot = jnp.concatenate([hot, hot], axis=0)
     for chunk in range(TRI // CHUNK):
@@ -437,7 +445,7 @@
             at = pl.ds(tile * LANES, LANES)
             place = local_place(anchors_ref, at)
             value = gather_tile(
-                weights_ref, place, picked, tile, chunk, pl.ds(step * LANES, LANES)
+                weights_ref, anchors_ref, place, picked, tile, chunk, pl.ds(step * LANES, LANES)
             )
             out_ref[:, at] = value + near_ref[:, at]
 
@@ -530,7 +538,9 @@
     near_source,
     near_tiles,
 ):
-    table = jnp.asarray(line_table())
+    lines = line_table()
+    table = jnp.asarray(lines)
+    turned = jnp.asarray(np.concatenate([lines[:, :, 0::2], lines[:, :, 1::2]], axis=2))
     devices = ROWS * COLS
     packed = jax.ShapeDtypeStruct((devices * LINES // LANES, LANES), F32)
     hbm = pl.BlockSpec(memory_space=pltpu.HBM)
@@ -599,12 +609,12 @@
         out_shape=jax.ShapeDtypeStruct((1, TRI), F32),
         scratch_shapes=[
             pltpu.VMEM((LINES, G), F32),
-            pltpu.VMEM((4 * SPREAD, 2 * G), BF16),
-            pltpu.VMEM((TRI // CHUNK, 4 * SPREAD, CHUNK), F32),
+            pltpu.VMEM((SHIFTS * SPREAD, G), BF16),
+            pltpu.VMEM((TRI // CHUNK, SHIFTS * SPREAD, CHUNK), F32),
         ],
         compiler_params=params(20),
         name="gather",
-    )(field, anchors, stencil_weights, table, near)
+    )(field, anchors, stencil_weights, turned, near)
     return result.reshape(TRI)
 
 

time: 69.2 us -> 68.8 us (level)
  no operation moved by 1% of the time
where the time goes in v8:
time: 68.8 us; the launch traced here: 68.6 us
  starting transfers between devices  35.1 us (51%)
  waiting for transfers between devices  19.7 us (29%)
  Pallas kernels  13 us (19%)
  between operations  0.73 us (1%)
    all_to_all x2, starting transfers between devices, exchange(): lax.all_to_all(shaped, axes, split_axis=0, concat_axis=0, tiled=True)  21.7 us
    all_to_all x2, waiting for transfers between devices, exchange(): lax.all_to_all(shaped, axes, split_axis=0, concat_axis=0, tiled=True)  8.65 us
    ppermute x4, starting transfers between devices, swapped(): return lax.ppermute(value, 'row', [(i, i ^ mask) for i in range(ROWS)])  6.74 us
    ppermute x2, starting transfers between devices, shifted(): lax.ppermute(value, axis, [(i, (i + by) % size) for i in range(size)])  6.66 us
    ppermute x2, waiting for transfers between devices, shifted(): lax.ppermute(value, axis, [(i, (i + by) % size) for i in range(size)])  5.58 us
    ppermute x4, waiting for transfers between devices, swapped(): return lax.ppermute(value, 'row', [(i, i ^ mask) for i in range(ROWS)])  5.5 us
    pallas_call x1, Pallas kernels, local(): pl.pallas_call(deposit_kernel, out_shape=(packed, *[jax.ShapeDtypeStruct(...  4.65 us
    pallas_call x1, Pallas kernels, local(): pl.pallas_call(plane_kernel, out_shape=packed, compiler_params=params(12)...  2.65 us
  transfers between devices with their start and end apart: 8, of which 6 were waited for; matrix products, arithmetic and copies ran while one was open for 0% of the time, Pallas kernels for 5%

profile of v8, /device:TPU:1, one launch (start us, length us, event | category | flops | bytes accessed | tf_op | source)
XLA Modules:
  0.0 68.6 jit_solution(17108428757770240784)
XLA Ops:
  0.0 0.0 copy-start.3
  0.0 0.0 copy-start.4
  0.0 4.6 %deposit.1 = (f32[768,128]{1,0:T(8,128)}, f32[24,128]{1,0:T(8,128)S(1)}, f32[72,128]{1,0:T(8,128)S(1)}, f32[72,128]{1,0:T(8,128)S(1)}, f32[72,128]{1,0:T(8,128)S(1)}, /*index=5*/f32[72,128]{1,0:T(8,128)S(1)}) custom-call(f32[1,1024]{1,0:T(1,128)} %bitcast.10, s32[3,1024]{1,0:T(4,128)} %anchors_ref.1, f32[64,1024]{1,0:T(8,128)} %weights_ref.1, ...), custom_call_target="tpu_custom_call" | custom-call | tf_op jit(solution)/shard_map/deposit/pallas_call | solution.py:547
  4.7 15.7 %all-to-all-start = ((f32[256,1,384]{2,1,0:T(1,128)}), f32[256,1,384]{2,1,0:T(1,128)S(1)}, u32[]{:S(2)}, u32[]{:S(2)}) async-start(f32[256,1,384]{2,1,0:T(1,128)} %bitcast.2), calls=%async_computation | async-start | bytes 786432 | tf_op jit(solution)/shard_map/all_to_all | solution.py:527
  20.3 3.0 %collective-permute-start = (f32[24,128]{1,0:T(8,128)S(1)}, f32[24,128]{1,0:T(8,128)S(1)}, u32[]{:S(2)}, u32[]{:S(2)}) collective-permute-start(f32[24,128]{1,0:T(8,128)S(1)} %get-tuple-element.18), channel_id=1, source_target_pairs={{0,224},{32,192},{64,160},{96,128},{128,96},{160,64},{192,32},{224... | collective-permute-start | bytes 36872 | tf_op jit(solution)/shard_map/ppermute | solution.py:522
  23.3 1.7 %collective-permute-done.first_ref._ = f32[24,128]{1,0:T(8,128)S(1)} collective-permute-done((f32[24,128]{1,0:T(8,128)S(1)}, f32[24,128]{1,0:T(8,128)S(1)}, u32[]{:S(2)}, u32[]{:S(2)}) %collective-permute-start) | collective-permute-done | bytes 12320 | tf_op jit(solution)/shard_map/ppermute | solution.py:522
  25.1 2.0 %collective-permute-start.1 = (f32[80,128]{1,0:T(8,128)S(1)}, f32[80,128]{1,0:T(8,128)S(1)}, u32[]{:S(2)}, u32[]{:S(2)}) collective-permute-start(f32[80,128]{1,0:T(8,128)S(1)} %get-tuple-element.23), channel_id=1, source_target_pairs={{0,32},{32,0},{64,96},{96,64},{128,160},{160,128},{192,224},{224,1... | collective-permute-start | bytes 122888 | tf_op jit(solution)/shard_map/ppermute | solution.py:522
  27.1 0.0 collective-permute-start.2
  27.1 1.7 %collective-permute-start.3 = (f32[80,128]{1,0:T(8,128)S(1)}, f32[80,128]{1,0:T(8,128)S(1)}, u32[]{:S(2)}, u32[]{:S(2)}) collective-permute-start(f32[80,128]{1,0:T(8,128)S(1)} %get-tuple-element.25), channel_id=1, source_target_pairs={{0,96},{32,64},{64,32},{96,0},{128,224},{160,192},{192,160},{224,1... | collective-permute-start | bytes 122888 | tf_op jit(solution)/shard_map/ppermute | solution.py:522
  28.8 0.2 waves.1.waves_ref
  29.1 0.0 collective-permute-done.1.refs_0_
  29.1 1.9 %collective-permute-done.2.refs_1_ = f32[80,128]{1,0:T(8,128)S(1)} collective-permute-done((f32[80,128]{1,0:T(8,128)S(1)}, f32[80,128]{1,0:T(8,128)S(1)}, u32[]{:S(2)}, u32[]{:S(2)}) %collective-permute-start.2) | collective-permute-done | bytes 40992 | tf_op jit(solution)/shard_map/ppermute | solution.py:522
  31.0 1.8 %collective-permute-done.3.refs_2_ = f32[80,128]{1,0:T(8,128)S(1)} collective-permute-done((f32[80,128]{1,0:T(8,128)S(1)}, f32[80,128]{1,0:T(8,128)S(1)}, u32[]{:S(2)}, u32[]{:S(2)}) %collective-permute-start.3) | collective-permute-done | bytes 40992 | tf_op jit(solution)/shard_map/ppermute | solution.py:522
  32.8 0.5 spectrum.1
  33.3 5.4 %all-to-all-done = f32[256,1,384]{2,1,0:T(1,128)S(1)} async-done(((f32[256,1,384]{2,1,0:T(1,128)}), f32[256,1,384]{2,1,0:T(1,128)S(1)}, u32[]{:S(2)}, u32[]{:S(2)}) %all-to-all-start) | async-done | bytes 393248 | tf_op jit(solution)/shard_map/all_to_all | solution.py:527
  38.8 0.0 copy-start
  38.8 0.0 copy-start.1
  38.8 0.0 copy-start.2
  38.8 2.7 %plane.1 = f32[768,128]{1,0:T(8,128)} custom-call(f32[768,128]{1,0:T(8,128)S(1)} %bitcast.8, f32[256,256]{1,0:T(8,128)S(1)} %get-tuple-element.26.spectrum_ref, f32[2,256,128]{2,1,0:T(8,128)S(1)} %waves.1.waves_ref), custom_call_target="tpu_custom_call" | custom-call | tf_op jit(solution)/shard_map/plane/pallas_call | solution.py:601
  41.4 6.0 %all-to-all-start.1 = ((f32[256,1,384]{2,1,0:T(1,128)}), f32[256,1,384]{2,1,0:T(1,128)S(1)}, u32[]{:S(2)}, u32[]{:S(2)}) async-start(f32[256,1,384]{2,1,0:T(1,128)} %bitcast.4), calls=%async_computation.1 | async-start | bytes 786432 | tf_op jit(solution)/shard_map/all_to_all | solution.py:527
  47.4 1.6 %collective-permute-start.4 = (f32[24,128]{1,0:T(8,128)S(1)}, f32[24,128]{1,0:T(8,128)S(1)}, u32[]{:S(2)}, u32[]{:S(2)}) collective-permute-start(f32[24,128]{1,0:T(8,128)S(1)} %get-tuple-element.28.own_ref), channel_id=1, source_target_pairs={{0,1},{1,2},{2,3},{3,4},{4,5},{5,6},{6,7},{7,8},{8,9},{9,10},{10,1... | collective-permute-start | bytes 36872 | tf_op jit(solution)/shard_map/ppermute | solution.py:490
  49.0 5.1 %collective-permute-start.5 = (f32[24,128]{1,0:T(8,128)S(1)}, f32[24,128]{1,0:T(8,128)S(1)}, u32[]{:S(2)}, u32[]{:S(2)}) collective-permute-start(f32[24,128]{1,0:T(8,128)S(1)} %get-tuple-element.28.own_ref), channel_id=1, source_target_pairs={{0,31},{1,0},{2,1},{3,2},{4,3},{5,4},{6,5},{7,6},{8,7},{9,8},{10,9... | collective-permute-start | bytes 36872 | tf_op jit(solution)/shard_map/ppermute | solution.py:490
  54.7 5.6 %collective-permute-done.4.before_ref = f32[24,128]{1,0:T(8,128)S(1)} collective-permute-done((f32[24,128]{1,0:T(8,128)S(1)}, f32[24,128]{1,0:T(8,128)S(1)}, u32[]{:S(2)}, u32[]{:S(2)}) %collective-permute-start.4) | collective-permute-done | bytes 12320 | tf_op jit(solution)/shard_map/ppermute | solution.py:490
  60.3 0.0 collective-permute-done.5.after_ref
  60.3 0.0 copy-done.3
  60.3 0.0 copy-done.4
  60.3 2.4 %near.1.near_ref = f32[1,1024]{1,0:T(1,128)S(1)} custom-call(s32[1]{0:T(128)S(6)} %copy.13.count_ref, s32[32]{0:T(128)S(1)} %copy-done.3, s32[32]{0:T(128)S(1)} %copy-done.4, f32[24,128]{1,0:T(8,128)S(1)} %collective-permute-done.4.before_ref, f32[24,128]{1,0:T(8,128)S(1)} %get-tuple-element.28.own_ref, f32[24,128]{1,0:T(8,128)S(1)} %collective-permute-done.5.after_ref, ...), custom_call_target="tpu_custom_call" | custom-call | tf_op jit(solution)/shard_map/near/pallas_call | solution.py:498
  62.8 3.2 %all-to-all-done.1 = f32[256,1,384]{2,1,0:T(1,128)S(1)} async-done(((f32[256,1,384]{2,1,0:T(1,128)}), f32[256,1,384]{2,1,0:T(1,128)S(1)}, u32[]{:S(2)}, u32[]{:S(2)}) %all-to-all-start.1) | async-done | bytes 393248 | tf_op jit(solution)/shard_map/all_to_all | solution.py:527
  66.0 0.0 copy-done
  66.0 0.0 copy-done.1
  66.0 0.0 copy-done.2
  66.0 2.6 %gather.1 = f32[1,1024]{1,0:T(1,128)} custom-call(f32[768,128]{1,0:T(8,128)S(1)} %bitcast.7, s32[3,1024]{1,0:T(4,128)S(1)} %copy-done.2, f32[64,1024]{1,0:T(8,128)S(1)} %copy-done, bf16[2,256,256]{2,1,0:T(8,128)(2,1)S(1)} %copy-done.1, f32[1,1024]{1,0:T(1,128)S(1)} %near.1.near_ref), custom_call_target="tpu_custom_call" | custom-call | tf_op jit(solution)/shard_map/gather/pallas_call | solution.py:607
  (1 shorter events, 0.0 us)
Async XLA Ops:
  0.0 60.3 %copy-start.3 = (s32[32]{0:T(128)S(1)}, s32[32]{0:T(128)}, u32[]{:S(2)}) copy-start(s32[32]{0:T(128)} %target_ref.1) | copy-start | bytes 388
  0.0 60.3 %copy-start.4 = (s32[32]{0:T(128)S(1)}, s32[32]{0:T(128)}, u32[]{:S(2)}) copy-start(s32[32]{0:T(128)} %source_ref.1) | copy-start | bytes 388
  4.7 34.1 %all-to-all-start = ((f32[256,1,384]{2,1,0:T(1,128)}), f32[256,1,384]{2,1,0:T(1,128)S(1)}, u32[]{:S(2)}, u32[]{:S(2)}) async-start(f32[256,1,384]{2,1,0:T(1,128)} %bitcast.2), calls=%async_computation | async-start | bytes 786432 | tf_op jit(solution)/shard_map/all_to_all | solution.py:527
  20.3 4.7 %collective-permute-start = (f32[24,128]{1,0:T(8,128)S(1)}, f32[24,128]{1,0:T(8,128)S(1)}, u32[]{:S(2)}, u32[]{:S(2)}) collective-permute-start(f32[24,128]{1,0:T(8,128)S(1)} %get-tuple-element.18), channel_id=1, source_target_pairs={{0,224},{32,192},{64,160},{96,128},{128,96},{160,64},{192,32},{224... | collective-permute-start | bytes 36872 | tf_op jit(solution)/shard_map/ppermute | solution.py:522
  25.1 4.0 %collective-permute-start.1 = (f32[80,128]{1,0:T(8,128)S(1)}, f32[80,128]{1,0:T(8,128)S(1)}, u32[]{:S(2)}, u32[]{:S(2)}) collective-permute-start(f32[80,128]{1,0:T(8,128)S(1)} %get-tuple-element.23), channel_id=1, source_target_pairs={{0,32},{32,0},{64,96},{96,64},{128,160},{160,128},{192,224},{224,1... | collective-permute-start | bytes 122888 | tf_op jit(solution)/shard_map/ppermute | solution.py:522
  27.1 3.9 %collective-permute-start.2 = (f32[80,128]{1,0:T(8,128)S(1)}, f32[80,128]{1,0:T(8,128)S(1)}, u32[]{:S(2)}, u32[]{:S(2)}) collective-permute-start(f32[80,128]{1,0:T(8,128)S(1)} %get-tuple-element.24), channel_id=1, source_target_pairs={{0,64},{32,96},{64,0},{96,32},{128,192},{160,224},{192,128},{224,1... | collective-permute-start | bytes 122888 | tf_op jit(solution)/shard_map/ppermute | solution.py:522
  27.1 5.7 %collective-permute-start.3 = (f32[80,128]{1,0:T(8,128)S(1)}, f32[80,128]{1,0:T(8,128)S(1)}, u32[]{:S(2)}, u32[]{:S(2)}) collective-permute-start(f32[80,128]{1,0:T(8,128)S(1)} %get-tuple-element.25), channel_id=1, source_target_pairs={{0,96},{32,64},{64,32},{96,0},{128,224},{160,192},{192,160},{224,1... | collective-permute-start | bytes 122888 | tf_op jit(solution)/shard_map/ppermute | solution.py:522
  38.8 27.2 %copy-start = (f32[64,1024]{1,0:T(8,128)S(1)}, f32[64,1024]{1,0:T(8,128)}, u32[]{:S(2)}) copy-start(f32[64,1024]{1,0:T(8,128)} %weights_ref.1) | copy-start | bytes 786436
  38.8 27.2 %copy-start.1 = (bf16[2,256,256]{2,1,0:T(8,128)(2,1)S(1)}, bf16[2,256,256]{2,1,0:T(8,128)(2,1)}, u32[]{:S(2)}) copy-start(bf16[2,256,256]{2,1,0:T(8,128)(2,1)} %constant.5.clone.table_ref) | copy-start | bytes 786436
  38.8 27.2 %copy-start.2 = (s32[3,1024]{1,0:T(4,128)S(1)}, s32[3,1024]{1,0:T(4,128)}, u32[]{:S(2)}) copy-start(s32[3,1024]{1,0:T(4,128)} %anchors_ref.1) | copy-start | bytes 36868
  41.4 24.5 %all-to-all-start.1 = ((f32[256,1,384]{2,1,0:T(1,128)}), f32[256,1,384]{2,1,0:T(1,128)S(1)}, u32[]{:S(2)}, u32[]{:S(2)}) async-start(f32[256,1,384]{2,1,0:T(1,128)} %bitcast.4), calls=%async_computation.1 | async-start | bytes 786432 | tf_op jit(solution)/shard_map/all_to_all | solution.py:527
  47.4 12.9 %collective-permute-start.4 = (f32[24,128]{1,0:T(8,128)S(1)}, f32[24,128]{1,0:T(8,128)S(1)}, u32[]{:S(2)}, u32[]{:S(2)}) collective-permute-start(f32[24,128]{1,0:T(8,128)S(1)} %get-tuple-element.28.own_ref), channel_id=1, source_target_pairs={{0,1},{1,2},{2,3},{3,4},{4,5},{5,6},{6,7},{7,8},{8,9},{9,10},{10,1... | collective-permute-start | bytes 36872 | tf_op jit(solution)/shard_map/ppermute | solution.py:490
  49.0 11.3 %collective-permute-start.5 = (f32[24,128]{1,0:T(8,128)S(1)}, f32[24,128]{1,0:T(8,128)S(1)}, u32[]{:S(2)}, u32[]{:S(2)}) collective-permute-start(f32[24,128]{1,0:T(8,128)S(1)} %get-tuple-element.28.own_ref), channel_id=1, source_target_pairs={{0,31},{1,0},{2,1},{3,2},{4,3},{5,4},{6,5},{7,6},{8,7},{9,8},{10,9... | collective-permute-start | bytes 36872 | tf_op jit(solution)/shard_map/ppermute | solution.py:490

commit v9 on v8

--- a/solution.py
+++ b/solution.py
@@ -192,8 +192,8 @@
         (weights_hbm, weights_ref),
         (anchors_hbm, anchors_ref),
         (charges_hbm, charges_ref),
-        (spectrum_hbm.at[:, pl.ds(0, LANES)], spectrum_ref.at[0]),
-        (spectrum_hbm.at[:, pl.ds(LANES, LANES)], spectrum_ref.at[1]),
+        (spectrum_hbm.at[:, pl.ds(0, LANES)], spectrum_ref.at[0, pl.ds(0, G)]),
+        (spectrum_hbm.at[:, pl.ds(LANES, LANES)], spectrum_ref.at[1, pl.ds(0, G)]),
         (table_hbm, table_ref),
     )
     copies = [pltpu.make_async_copy(a, b, sem.at[n]) for n, (a, b) in enumerate(pairs)]
@@ -500,7 +500,7 @@
         in_specs=[smem, smem, smem, vmem, vmem, vmem, pl.BlockSpec(memory_space=pltpu.HBM)],
         out_shape=jax.ShapeDtypeStruct((1, TRI), F32),
         scratch_shapes=[
-            pltpu.VMEM((72, size), F32),
+            pltpu.VMEM((80, size), F32),
             pltpu.VMEM((TRI, size), F32),
             pltpu.VMEM((slots, size, size), F32),
             pltpu.SemaphoreType.DMA((slots // PART,)),
@@ -553,7 +553,7 @@
             pltpu.VMEM((3, TRI), jnp.int32),
             pltpu.VMEM((64, TRI), F32),
             pltpu.VMEM((2, G, G), BF16),
-            pltpu.VMEM((2, CELLS_A * CELLS_B, LANES), F32),
+            pltpu.VMEM((2, CELLS_A * CELLS_B + 8, LANES), F32),
             pltpu.VMEM((64, TRI), F32),
             pltpu.VMEM((4, 2 * SPREAD, TRI), BF16),
             pltpu.VMEM((LINES, G), F32),

time: 68.8 us -> 68.8 us (level)
  no operation moved by 1% of the time
where the time goes in v9:
time: 68.8 us; the launch traced here: 68.5 us
  starting transfers between devices  35 us (51%)
  waiting for transfers between devices  19.7 us (29%)
  Pallas kernels  13 us (19%)
  between operations  0.73 us (1%)
    all_to_all x2, starting transfers between devices, exchange(): lax.all_to_all(shaped, axes, split_axis=0, concat_axis=0, tiled=True)  21.6 us
    all_to_all x2, waiting for transfers between devices, exchange(): lax.all_to_all(shaped, axes, split_axis=0, concat_axis=0, tiled=True)  8.65 us
    ppermute x4, starting transfers between devices, swapped(): return lax.ppermute(value, 'row', [(i, i ^ mask) for i in range(ROWS)])  6.74 us
    ppermute x2, starting transfers between devices, shifted(): lax.ppermute(value, axis, [(i, (i + by) % size) for i in range(size)])  6.66 us
    ppermute x2, waiting for transfers between devices, shifted(): lax.ppermute(value, axis, [(i, (i + by) % size) for i in range(size)])  5.58 us
    ppermute x4, waiting for transfers between devices, swapped(): return lax.ppermute(value, 'row', [(i, i ^ mask) for i in range(ROWS)])  5.5 us
    pallas_call x1, Pallas kernels, local(): pl.pallas_call(deposit_kernel, out_shape=(packed, *[jax.ShapeDtypeStruct(...  4.64 us
    pallas_call x1, Pallas kernels, local(): pl.pallas_call(plane_kernel, out_shape=packed, compiler_params=params(12)...  2.65 us
  transfers between devices with their start and end apart: 8, of which 6 were waited for; matrix products, arithmetic and copies ran while one was open for 0% of the time, Pallas kernels for 5%

profile of v9, /device:TPU:1, one launch (start us, length us, event | category | flops | bytes accessed | tf_op | source)
XLA Modules:
  0.0 68.5 jit_solution(16572786498273376923)
XLA Ops:
  0.0 0.0 copy-start.3
  0.0 0.0 copy-start.4
  0.0 4.6 %deposit.1 = (f32[768,128]{1,0:T(8,128)}, f32[24,128]{1,0:T(8,128)S(1)}, f32[72,128]{1,0:T(8,128)S(1)}, f32[72,128]{1,0:T(8,128)S(1)}, f32[72,128]{1,0:T(8,128)S(1)}, /*index=5*/f32[72,128]{1,0:T(8,128)S(1)}) custom-call(f32[1,1024]{1,0:T(1,128)} %bitcast.10, s32[3,1024]{1,0:T(4,128)} %anchors_ref.1, f32[64,1024]{1,0:T(8,128)} %weights_ref.1, ...), custom_call_target="tpu_custom_call" | custom-call | tf_op jit(solution)/shard_map/deposit/pallas_call | solution.py:547
  4.7 15.7 %all-to-all-start = ((f32[256,1,384]{2,1,0:T(1,128)}), f32[256,1,384]{2,1,0:T(1,128)S(1)}, u32[]{:S(2)}, u32[]{:S(2)}) async-start(f32[256,1,384]{2,1,0:T(1,128)} %bitcast.2), calls=%async_computation | async-start | bytes 786432 | tf_op jit(solution)/shard_map/all_to_all | solution.py:527
  20.3 3.0 %collective-permute-start = (f32[24,128]{1,0:T(8,128)S(1)}, f32[24,128]{1,0:T(8,128)S(1)}, u32[]{:S(2)}, u32[]{:S(2)}) collective-permute-start(f32[24,128]{1,0:T(8,128)S(1)} %get-tuple-element.18), channel_id=1, source_target_pairs={{0,224},{32,192},{64,160},{96,128},{128,96},{160,64},{192,32},{224... | collective-permute-start | bytes 36872 | tf_op jit(solution)/shard_map/ppermute | solution.py:522
  23.3 1.7 %collective-permute-done.first_ref._ = f32[24,128]{1,0:T(8,128)S(1)} collective-permute-done((f32[24,128]{1,0:T(8,128)S(1)}, f32[24,128]{1,0:T(8,128)S(1)}, u32[]{:S(2)}, u32[]{:S(2)}) %collective-permute-start) | collective-permute-done | bytes 12320 | tf_op jit(solution)/shard_map/ppermute | solution.py:522
  25.1 2.0 %collective-permute-start.1 = (f32[80,128]{1,0:T(8,128)S(1)}, f32[80,128]{1,0:T(8,128)S(1)}, u32[]{:S(2)}, u32[]{:S(2)}) collective-permute-start(f32[80,128]{1,0:T(8,128)S(1)} %get-tuple-element.23), channel_id=1, source_target_pairs={{0,32},{32,0},{64,96},{96,64},{128,160},{160,128},{192,224},{224,1... | collective-permute-start | bytes 122888 | tf_op jit(solution)/shard_map/ppermute | solution.py:522
  27.1 0.0 collective-permute-start.2
  27.1 1.7 %collective-permute-start.3 = (f32[80,128]{1,0:T(8,128)S(1)}, f32[80,128]{1,0:T(8,128)S(1)}, u32[]{:S(2)}, u32[]{:S(2)}) collective-permute-start(f32[80,128]{1,0:T(8,128)S(1)} %get-tuple-element.25), channel_id=1, source_target_pairs={{0,96},{32,64},{64,32},{96,0},{128,224},{160,192},{192,160},{224,1... | collective-permute-start | bytes 122888 | tf_op jit(solution)/shard_map/ppermute | solution.py:522
  28.8 0.2 waves.1.waves_ref
  29.0 0.0 collective-permute-done.1.refs_0_
  29.1 1.9 %collective-permute-done.2.refs_1_ = f32[80,128]{1,0:T(8,128)S(1)} collective-permute-done((f32[80,128]{1,0:T(8,128)S(1)}, f32[80,128]{1,0:T(8,128)S(1)}, u32[]{:S(2)}, u32[]{:S(2)}) %collective-permute-start.2) | collective-permute-done | bytes 40992 | tf_op jit(solution)/shard_map/ppermute | solution.py:522
  31.0 1.8 %collective-permute-done.3.refs_2_ = f32[80,128]{1,0:T(8,128)S(1)} collective-permute-done((f32[80,128]{1,0:T(8,128)S(1)}, f32[80,128]{1,0:T(8,128)S(1)}, u32[]{:S(2)}, u32[]{:S(2)}) %collective-permute-start.3) | collective-permute-done | bytes 40992 | tf_op jit(solution)/shard_map/ppermute | solution.py:522
  32.8 0.5 spectrum.1
  33.3 5.4 %all-to-all-done = f32[256,1,384]{2,1,0:T(1,128)S(1)} async-done(((f32[256,1,384]{2,1,0:T(1,128)}), f32[256,1,384]{2,1,0:T(1,128)S(1)}, u32[]{:S(2)}, u32[]{:S(2)}) %all-to-all-start) | async-done | bytes 393248 | tf_op jit(solution)/shard_map/all_to_all | solution.py:527
  38.8 0.0 copy-start
  38.8 0.0 copy-start.1
  38.8 0.0 copy-start.2
  38.8 2.7 %plane.1 = f32[768,128]{1,0:T(8,128)} custom-call(f32[768,128]{1,0:T(8,128)S(1)} %bitcast.8, f32[256,256]{1,0:T(8,128)S(1)} %get-tuple-element.26.spectrum_ref, f32[2,256,128]{2,1,0:T(8,128)S(1)} %waves.1.waves_ref), custom_call_target="tpu_custom_call" | custom-call | tf_op jit(solution)/shard_map/plane/pallas_call | solution.py:601
  41.4 6.0 %all-to-all-start.1 = ((f32[256,1,384]{2,1,0:T(1,128)}), f32[256,1,384]{2,1,0:T(1,128)S(1)}, u32[]{:S(2)}, u32[]{:S(2)}) async-start(f32[256,1,384]{2,1,0:T(1,128)} %bitcast.4), calls=%async_computation.1 | async-start | bytes 786432 | tf_op jit(solution)/shard_map/all_to_all | solution.py:527
  47.4 1.6 %collective-permute-start.4 = (f32[24,128]{1,0:T(8,128)S(1)}, f32[24,128]{1,0:T(8,128)S(1)}, u32[]{:S(2)}, u32[]{:S(2)}) collective-permute-start(f32[24,128]{1,0:T(8,128)S(1)} %get-tuple-element.28.own_ref), channel_id=1, source_target_pairs={{0,1},{1,2},{2,3},{3,4},{4,5},{5,6},{6,7},{7,8},{8,9},{9,10},{10,1... | collective-permute-start | bytes 36872 | tf_op jit(solution)/shard_map/ppermute | solution.py:490
  49.0 5.1 %collective-permute-start.5 = (f32[24,128]{1,0:T(8,128)S(1)}, f32[24,128]{1,0:T(8,128)S(1)}, u32[]{:S(2)}, u32[]{:S(2)}) collective-permute-start(f32[24,128]{1,0:T(8,128)S(1)} %get-tuple-element.28.own_ref), channel_id=1, source_target_pairs={{0,31},{1,0},{2,1},{3,2},{4,3},{5,4},{6,5},{7,6},{8,7},{9,8},{10,9... | collective-permute-start | bytes 36872 | tf_op jit(solution)/shard_map/ppermute | solution.py:490
  54.7 5.6 %collective-permute-done.4.before_ref = f32[24,128]{1,0:T(8,128)S(1)} collective-permute-done((f32[24,128]{1,0:T(8,128)S(1)}, f32[24,128]{1,0:T(8,128)S(1)}, u32[]{:S(2)}, u32[]{:S(2)}) %collective-permute-start.4) | collective-permute-done | bytes 12320 | tf_op jit(solution)/shard_map/ppermute | solution.py:490
  60.3 0.0 collective-permute-done.5.after_ref
  60.3 0.0 copy-done.3
  60.3 0.0 copy-done.4
  60.3 2.4 %near.1.near_ref = f32[1,1024]{1,0:T(1,128)S(1)} custom-call(s32[1]{0:T(128)S(6)} %copy.13.count_ref, s32[32]{0:T(128)S(1)} %copy-done.3, s32[32]{0:T(128)S(1)} %copy-done.4, f32[24,128]{1,0:T(8,128)S(1)} %collective-permute-done.4.before_ref, f32[24,128]{1,0:T(8,128)S(1)} %get-tuple-element.28.own_ref, f32[24,128]{1,0:T(8,128)S(1)} %collective-permute-done.5.after_ref, ...), custom_call_target="tpu_custom_call" | custom-call | tf_op jit(solution)/shard_map/near/pallas_call | solution.py:498
  62.7 3.2 %all-to-all-done.1 = f32[256,1,384]{2,1,0:T(1,128)S(1)} async-done(((f32[256,1,384]{2,1,0:T(1,128)}), f32[256,1,384]{2,1,0:T(1,128)S(1)}, u32[]{:S(2)}, u32[]{:S(2)}) %all-to-all-start.1) | async-done | bytes 393248 | tf_op jit(solution)/shard_map/all_to_all | solution.py:527
  66.0 0.0 copy-done
  66.0 0.0 copy-done.1
  66.0 0.0 copy-done.2
  66.0 2.6 %gather.1 = f32[1,1024]{1,0:T(1,128)} custom-call(f32[768,128]{1,0:T(8,128)S(1)} %bitcast.7, s32[3,1024]{1,0:T(4,128)S(1)} %copy-done.2, f32[64,1024]{1,0:T(8,128)S(1)} %copy-done, bf16[2,256,256]{2,1,0:T(8,128)(2,1)S(1)} %copy-done.1, f32[1,1024]{1,0:T(1,128)S(1)} %near.1.near_ref), custom_call_target="tpu_custom_call" | custom-call | tf_op jit(solution)/shard_map/gather/pallas_call | solution.py:607
  (1 shorter events, 0.0 us)
Async XLA Ops:
  0.0 60.3 %copy-start.3 = (s32[32]{0:T(128)S(1)}, s32[32]{0:T(128)}, u32[]{:S(2)}) copy-start(s32[32]{0:T(128)} %target_ref.1) | copy-start | bytes 388
  0.0 60.3 %copy-start.4 = (s32[32]{0:T(128)S(1)}, s32[32]{0:T(128)}, u32[]{:S(2)}) copy-start(s32[32]{0:T(128)} %source_ref.1) | copy-start | bytes 388
  4.7 34.1 %all-to-all-start = ((f32[256,1,384]{2,1,0:T(1,128)}), f32[256,1,384]{2,1,0:T(1,128)S(1)}, u32[]{:S(2)}, u32[]{:S(2)}) async-start(f32[256,1,384]{2,1,0:T(1,128)} %bitcast.2), calls=%async_computation | async-start | bytes 786432 | tf_op jit(solution)/shard_map/all_to_all | solution.py:527
  20.3 4.7 %collective-permute-start = (f32[24,128]{1,0:T(8,128)S(1)}, f32[24,128]{1,0:T(8,128)S(1)}, u32[]{:S(2)}, u32[]{:S(2)}) collective-permute-start(f32[24,128]{1,0:T(8,128)S(1)} %get-tuple-element.18), channel_id=1, source_target_pairs={{0,224},{32,192},{64,160},{96,128},{128,96},{160,64},{192,32},{224... | collective-permute-start | bytes 36872 | tf_op jit(solution)/shard_map/ppermute | solution.py:522
  25.1 4.0 %collective-permute-start.1 = (f32[80,128]{1,0:T(8,128)S(1)}, f32[80,128]{1,0:T(8,128)S(1)}, u32[]{:S(2)}, u32[]{:S(2)}) collective-permute-start(f32[80,128]{1,0:T(8,128)S(1)} %get-tuple-element.23), channel_id=1, source_target_pairs={{0,32},{32,0},{64,96},{96,64},{128,160},{160,128},{192,224},{224,1... | collective-permute-start | bytes 122888 | tf_op jit(solution)/shard_map/ppermute | solution.py:522
  27.1 3.9 %collective-permute-start.2 = (f32[80,128]{1,0:T(8,128)S(1)}, f32[80,128]{1,0:T(8,128)S(1)}, u32[]{:S(2)}, u32[]{:S(2)}) collective-permute-start(f32[80,128]{1,0:T(8,128)S(1)} %get-tuple-element.24), channel_id=1, source_target_pairs={{0,64},{32,96},{64,0},{96,32},{128,192},{160,224},{192,128},{224,1... | collective-permute-start | bytes 122888 | tf_op jit(solution)/shard_map/ppermute | solution.py:522
  27.1 5.7 %collective-permute-start.3 = (f32[80,128]{1,0:T(8,128)S(1)}, f32[80,128]{1,0:T(8,128)S(1)}, u32[]{:S(2)}, u32[]{:S(2)}) collective-permute-start(f32[80,128]{1,0:T(8,128)S(1)} %get-tuple-element.25), channel_id=1, source_target_pairs={{0,96},{32,64},{64,32},{96,0},{128,224},{160,192},{192,160},{224,1... | collective-permute-start | bytes 122888 | tf_op jit(solution)/shard_map/ppermute | solution.py:522
  38.8 27.2 %copy-start = (f32[64,1024]{1,0:T(8,128)S(1)}, f32[64,1024]{1,0:T(8,128)}, u32[]{:S(2)}) copy-start(f32[64,1024]{1,0:T(8,128)} %weights_ref.1) | copy-start | bytes 786436
  38.8 27.2 %copy-start.1 = (bf16[2,256,256]{2,1,0:T(8,128)(2,1)S(1)}, bf16[2,256,256]{2,1,0:T(8,128)(2,1)}, u32[]{:S(2)}) copy-start(bf16[2,256,256]{2,1,0:T(8,128)(2,1)} %constant.5.clone.table_ref) | copy-start | bytes 786436
  38.8 27.2 %copy-start.2 = (s32[3,1024]{1,0:T(4,128)S(1)}, s32[3,1024]{1,0:T(4,128)}, u32[]{:S(2)}) copy-start(s32[3,1024]{1,0:T(4,128)} %anchors_ref.1) | copy-start | bytes 36868
  41.4 24.5 %all-to-all-start.1 = ((f32[256,1,384]{2,1,0:T(1,128)}), f32[256,1,384]{2,1,0:T(1,128)S(1)}, u32[]{:S(2)}, u32[]{:S(2)}) async-start(f32[256,1,384]{2,1,0:T(1,128)} %bitcast.4), calls=%async_computation.1 | async-start | bytes 786432 | tf_op jit(solution)/shard_map/all_to_all | solution.py:527
  47.4 12.9 %collective-permute-start.4 = (f32[24,128]{1,0:T(8,128)S(1)}, f32[24,128]{1,0:T(8,128)S(1)}, u32[]{:S(2)}, u32[]{:S(2)}) collective-permute-start(f32[24,128]{1,0:T(8,128)S(1)} %get-tuple-element.28.own_ref), channel_id=1, source_target_pairs={{0,1},{1,2},{2,3},{3,4},{4,5},{5,6},{6,7},{7,8},{8,9},{9,10},{10,1... | collective-permute-start | bytes 36872 | tf_op jit(solution)/shard_map/ppermute | solution.py:490
  49.0 11.3 %collective-permute-start.5 = (f32[24,128]{1,0:T(8,128)S(1)}, f32[24,128]{1,0:T(8,128)S(1)}, u32[]{:S(2)}, u32[]{:S(2)}) collective-permute-start(f32[24,128]{1,0:T(8,128)S(1)} %get-tuple-element.28.own_ref), channel_id=1, source_target_pairs={{0,31},{1,0},{2,1},{3,2},{4,3},{5,4},{6,5},{7,6},{8,7},{9,8},{10,9... | collective-permute-start | bytes 36872 | tf_op jit(solution)/shard_map/ppermute | solution.py:490

commit v10 on v9

--- a/solution.py
+++ b/solution.py
@@ -439,7 +439,10 @@
     hot = onehot(anchors_ref)
     hot = jnp.concatenate([hot, hot], axis=0)
     for chunk in range(TRI // CHUNK):
-        picked[chunk] = dot(parts[...], hot[:, CHUNK * chunk : CHUNK * (chunk + 1)])
+        columns = hot[:, CHUNK * chunk : CHUNK * (chunk + 1)]
+        for first, count in ((0, 2), (2, 3)) if chunk == 0 else ((0, SHIFTS),):
+            rows = pl.ds(SPREAD * first, SPREAD * count)
+            picked[chunk, rows, :] = dot(parts[rows, :], columns)
         for step in range(CHUNK // LANES):
             tile = chunk * (CHUNK // LANES) + step
             at = pl.ds(tile * LANES, LANES)

time: 68.8 us -> 68.8 us (level)
  no operation moved by 1% of the time
where the time goes in v10:
time: 68.8 us; the launch traced here: 68.6 us
  starting transfers between devices  35 us (51%)
  waiting for transfers between devices  19.7 us (29%)
  Pallas kernels  13 us (19%)
  between operations  0.73 us (1%)
    all_to_all x2, starting transfers between devices, exchange(): lax.all_to_all(shaped, axes, split_axis=0, concat_axis=0, tiled=True)  21.6 us
    all_to_all x2, waiting for transfers between devices, exchange(): lax.all_to_all(shaped, axes, split_axis=0, concat_axis=0, tiled=True)  8.65 us
    ppermute x4, starting transfers between devices, swapped(): return lax.ppermute(value, 'row', [(i, i ^ mask) for i in range(ROWS)])  6.74 us
    ppermute x2, starting transfers between devices, shifted(): lax.ppermute(value, axis, [(i, (i + by) % size) for i in range(size)])  6.66 us
    ppermute x2, waiting for transfers between devices, shifted(): lax.ppermute(value, axis, [(i, (i + by) % size) for i in range(size)])  5.58 us
    ppermute x4, waiting for transfers between devices, swapped(): return lax.ppermute(value, 'row', [(i, i ^ mask) for i in range(ROWS)])  5.5 us
    pallas_call x1, Pallas kernels, local(): pl.pallas_call(deposit_kernel, out_shape=(packed, *[jax.ShapeDtypeStruct(...  4.64 us
    pallas_call x1, Pallas kernels, local(): pl.pallas_call(plane_kernel, out_shape=packed, compiler_params=params(12)...  2.65 us
  transfers between devices with their start and end apart: 8, of which 6 were waited for; matrix products, arithmetic and copies ran while one was open for 0% of the time, Pallas kernels for 5%

profile of v10, /device:TPU:1, one launch (start us, length us, event | category | flops | bytes accessed | tf_op | source)
XLA Modules:
  0.0 68.6 jit_solution(17542079467762932069)
XLA Ops:
  0.0 0.0 copy-start.3
  0.0 0.0 copy-start.4
  0.0 4.6 %deposit.1 = (f32[768,128]{1,0:T(8,128)}, f32[24,128]{1,0:T(8,128)S(1)}, f32[72,128]{1,0:T(8,128)S(1)}, f32[72,128]{1,0:T(8,128)S(1)}, f32[72,128]{1,0:T(8,128)S(1)}, /*index=5*/f32[72,128]{1,0:T(8,128)S(1)}) custom-call(f32[1,1024]{1,0:T(1,128)} %bitcast.10, s32[3,1024]{1,0:T(4,128)} %anchors_ref.1, f32[64,1024]{1,0:T(8,128)} %weights_ref.1, ...), custom_call_target="tpu_custom_call" | custom-call | tf_op jit(solution)/shard_map/deposit/pallas_call | solution.py:550
  4.7 15.7 %all-to-all-start = ((f32[256,1,384]{2,1,0:T(1,128)}), f32[256,1,384]{2,1,0:T(1,128)S(1)}, u32[]{:S(2)}, u32[]{:S(2)}) async-start(f32[256,1,384]{2,1,0:T(1,128)} %bitcast.2), calls=%async_computation | async-start | bytes 786432 | tf_op jit(solution)/shard_map/all_to_all | solution.py:530
  20.3 3.0 %collective-permute-start = (f32[24,128]{1,0:T(8,128)S(1)}, f32[24,128]{1,0:T(8,128)S(1)}, u32[]{:S(2)}, u32[]{:S(2)}) collective-permute-start(f32[24,128]{1,0:T(8,128)S(1)} %get-tuple-element.18), channel_id=1, source_target_pairs={{0,224},{32,192},{64,160},{96,128},{128,96},{160,64},{192,32},{224... | collective-permute-start | bytes 36872 | tf_op jit(solution)/shard_map/ppermute | solution.py:525
  23.3 1.7 %collective-permute-done.first_ref._ = f32[24,128]{1,0:T(8,128)S(1)} collective-permute-done((f32[24,128]{1,0:T(8,128)S(1)}, f32[24,128]{1,0:T(8,128)S(1)}, u32[]{:S(2)}, u32[]{:S(2)}) %collective-permute-start) | collective-permute-done | bytes 12320 | tf_op jit(solution)/shard_map/ppermute | solution.py:525
  25.1 2.0 %collective-permute-start.1 = (f32[80,128]{1,0:T(8,128)S(1)}, f32[80,128]{1,0:T(8,128)S(1)}, u32[]{:S(2)}, u32[]{:S(2)}) collective-permute-start(f32[80,128]{1,0:T(8,128)S(1)} %get-tuple-element.23), channel_id=1, source_target_pairs={{0,32},{32,0},{64,96},{96,64},{128,160},{160,128},{192,224},{224,1... | collective-permute-start | bytes 122888 | tf_op jit(solution)/shard_map/ppermute | solution.py:525
  27.1 0.0 collective-permute-start.2
  27.1 1.7 %collective-permute-start.3 = (f32[80,128]{1,0:T(8,128)S(1)}, f32[80,128]{1,0:T(8,128)S(1)}, u32[]{:S(2)}, u32[]{:S(2)}) collective-permute-start(f32[80,128]{1,0:T(8,128)S(1)} %get-tuple-element.25), channel_id=1, source_target_pairs={{0,96},{32,64},{64,32},{96,0},{128,224},{160,192},{192,160},{224,1... | collective-permute-start | bytes 122888 | tf_op jit(solution)/shard_map/ppermute | solution.py:525
  28.8 0.2 waves.1.waves_ref
  29.0 0.0 collective-permute-done.1.refs_0_
  29.1 1.9 %collective-permute-done.2.refs_1_ = f32[80,128]{1,0:T(8,128)S(1)} collective-permute-done((f32[80,128]{1,0:T(8,128)S(1)}, f32[80,128]{1,0:T(8,128)S(1)}, u32[]{:S(2)}, u32[]{:S(2)}) %collective-permute-start.2) | collective-permute-done | bytes 40992 | tf_op jit(solution)/shard_map/ppermute | solution.py:525
  31.0 1.8 %collective-permute-done.3.refs_2_ = f32[80,128]{1,0:T(8,128)S(1)} collective-permute-done((f32[80,128]{1,0:T(8,128)S(1)}, f32[80,128]{1,0:T(8,128)S(1)}, u32[]{:S(2)}, u32[]{:S(2)}) %collective-permute-start.3) | collective-permute-done | bytes 40992 | tf_op jit(solution)/shard_map/ppermute | solution.py:525
  32.8 0.5 spectrum.1
  33.3 5.4 %all-to-all-done = f32[256,1,384]{2,1,0:T(1,128)S(1)} async-done(((f32[256,1,384]{2,1,0:T(1,128)}), f32[256,1,384]{2,1,0:T(1,128)S(1)}, u32[]{:S(2)}, u32[]{:S(2)}) %all-to-all-start) | async-done | bytes 393248 | tf_op jit(solution)/shard_map/all_to_all | solution.py:530
  38.8 0.0 copy-start
  38.8 0.0 copy-start.1
  38.8 0.0 copy-start.2
  38.8 2.7 %plane.1 = f32[768,128]{1,0:T(8,128)} custom-call(f32[768,128]{1,0:T(8,128)S(1)} %bitcast.8, f32[256,256]{1,0:T(8,128)S(1)} %get-tuple-element.26.spectrum_ref, f32[2,256,128]{2,1,0:T(8,128)S(1)} %waves.1.waves_ref), custom_call_target="tpu_custom_call" | custom-call | tf_op jit(solution)/shard_map/plane/pallas_call | solution.py:604
  41.4 6.0 %all-to-all-start.1 = ((f32[256,1,384]{2,1,0:T(1,128)}), f32[256,1,384]{2,1,0:T(1,128)S(1)}, u32[]{:S(2)}, u32[]{:S(2)}) async-start(f32[256,1,384]{2,1,0:T(1,128)} %bitcast.4), calls=%async_computation.1 | async-start | bytes 786432 | tf_op jit(solution)/shard_map/all_to_all | solution.py:530
  47.4 1.6 %collective-permute-start.4 = (f32[24,128]{1,0:T(8,128)S(1)}, f32[24,128]{1,0:T(8,128)S(1)}, u32[]{:S(2)}, u32[]{:S(2)}) collective-permute-start(f32[24,128]{1,0:T(8,128)S(1)} %get-tuple-element.28.own_ref), channel_id=1, source_target_pairs={{0,1},{1,2},{2,3},{3,4},{4,5},{5,6},{6,7},{7,8},{8,9},{9,10},{10,1... | collective-permute-start | bytes 36872 | tf_op jit(solution)/shard_map/ppermute | solution.py:493
  49.0 5.1 %collective-permute-start.5 = (f32[24,128]{1,0:T(8,128)S(1)}, f32[24,128]{1,0:T(8,128)S(1)}, u32[]{:S(2)}, u32[]{:S(2)}) collective-permute-start(f32[24,128]{1,0:T(8,128)S(1)} %get-tuple-element.28.own_ref), channel_id=1, source_target_pairs={{0,31},{1,0},{2,1},{3,2},{4,3},{5,4},{6,5},{7,6},{8,7},{9,8},{10,9... | collective-permute-start | bytes 36872 | tf_op jit(solution)/shard_map/ppermute | solution.py:493
  54.7 5.6 %collective-permute-done.4.before_ref = f32[24,128]{1,0:T(8,128)S(1)} collective-permute-done((f32[24,128]{1,0:T(8,128)S(1)}, f32[24,128]{1,0:T(8,128)S(1)}, u32[]{:S(2)}, u32[]{:S(2)}) %collective-permute-start.4) | collective-permute-done | bytes 12320 | tf_op jit(solution)/shard_map/ppermute | solution.py:493
  60.3 0.0 collective-permute-done.5.after_ref
  60.3 0.0 copy-done.3
  60.3 0.0 copy-done.4
  60.3 2.4 %near.1.near_ref = f32[1,1024]{1,0:T(1,128)S(1)} custom-call(s32[1]{0:T(128)S(6)} %copy.13.count_ref, s32[32]{0:T(128)S(1)} %copy-done.3, s32[32]{0:T(128)S(1)} %copy-done.4, f32[24,128]{1,0:T(8,128)S(1)} %collective-permute-done.4.before_ref, f32[24,128]{1,0:T(8,128)S(1)} %get-tuple-element.28.own_ref, f32[24,128]{1,0:T(8,128)S(1)} %collective-permute-done.5.after_ref, ...), custom_call_target="tpu_custom_call" | custom-call | tf_op jit(solution)/shard_map/near/pallas_call | solution.py:501
  62.7 3.2 %all-to-all-done.1 = f32[256,1,384]{2,1,0:T(1,128)S(1)} async-done(((f32[256,1,384]{2,1,0:T(1,128)}), f32[256,1,384]{2,1,0:T(1,128)S(1)}, u32[]{:S(2)}, u32[]{:S(2)}) %all-to-all-start.1) | async-done | bytes 393248 | tf_op jit(solution)/shard_map/all_to_all | solution.py:530
  66.0 0.0 copy-done
  66.0 0.0 copy-done.1
  66.0 0.0 copy-done.2
  66.0 2.6 %gather.1 = f32[1,1024]{1,0:T(1,128)} custom-call(f32[768,128]{1,0:T(8,128)S(1)} %bitcast.7, s32[3,1024]{1,0:T(4,128)S(1)} %copy-done.2, f32[64,1024]{1,0:T(8,128)S(1)} %copy-done, bf16[2,256,256]{2,1,0:T(8,128)(2,1)S(1)} %copy-done.1, f32[1,1024]{1,0:T(1,128)S(1)} %near.1.near_ref), custom_call_target="tpu_custom_call" | custom-call | tf_op jit(solution)/shard_map/gather/pallas_call | solution.py:610
  (1 shorter events, 0.0 us)
Async XLA Ops:
  0.0 60.3 %copy-start.3 = (s32[32]{0:T(128)S(1)}, s32[32]{0:T(128)}, u32[]{:S(2)}) copy-start(s32[32]{0:T(128)} %target_ref.1) | copy-start | bytes 388
  0.0 60.3 %copy-start.4 = (s32[32]{0:T(128)S(1)}, s32[32]{0:T(128)}, u32[]{:S(2)}) copy-start(s32[32]{0:T(128)} %source_ref.1) | copy-start | bytes 388
  4.7 34.1 %all-to-all-start = ((f32[256,1,384]{2,1,0:T(1,128)}), f32[256,1,384]{2,1,0:T(1,128)S(1)}, u32[]{:S(2)}, u32[]{:S(2)}) async-start(f32[256,1,384]{2,1,0:T(1,128)} %bitcast.2), calls=%async_computation | async-start | bytes 786432 | tf_op jit(solution)/shard_map/all_to_all | solution.py:530
  20.3 4.7 %collective-permute-start = (f32[24,128]{1,0:T(8,128)S(1)}, f32[24,128]{1,0:T(8,128)S(1)}, u32[]{:S(2)}, u32[]{:S(2)}) collective-permute-start(f32[24,128]{1,0:T(8,128)S(1)} %get-tuple-element.18), channel_id=1, source_target_pairs={{0,224},{32,192},{64,160},{96,128},{128,96},{160,64},{192,32},{224... | collective-permute-start | bytes 36872 | tf_op jit(solution)/shard_map/ppermute | solution.py:525
  25.1 4.0 %collective-permute-start.1 = (f32[80,128]{1,0:T(8,128)S(1)}, f32[80,128]{1,0:T(8,128)S(1)}, u32[]{:S(2)}, u32[]{:S(2)}) collective-permute-start(f32[80,128]{1,0:T(8,128)S(1)} %get-tuple-element.23), channel_id=1, source_target_pairs={{0,32},{32,0},{64,96},{96,64},{128,160},{160,128},{192,224},{224,1... | collective-permute-start | bytes 122888 | tf_op jit(solution)/shard_map/ppermute | solution.py:525
  27.1 3.9 %collective-permute-start.2 = (f32[80,128]{1,0:T(8,128)S(1)}, f32[80,128]{1,0:T(8,128)S(1)}, u32[]{:S(2)}, u32[]{:S(2)}) collective-permute-start(f32[80,128]{1,0:T(8,128)S(1)} %get-tuple-element.24), channel_id=1, source_target_pairs={{0,64},{32,96},{64,0},{96,32},{128,192},{160,224},{192,128},{224,1... | collective-permute-start | bytes 122888 | tf_op jit(solution)/shard_map/ppermute | solution.py:525
  27.1 5.7 %collective-permute-start.3 = (f32[80,128]{1,0:T(8,128)S(1)}, f32[80,128]{1,0:T(8,128)S(1)}, u32[]{:S(2)}, u32[]{:S(2)}) collective-permute-start(f32[80,128]{1,0:T(8,128)S(1)} %get-tuple-element.25), channel_id=1, source_target_pairs={{0,96},{32,64},{64,32},{96,0},{128,224},{160,192},{192,160},{224,1... | collective-permute-start | bytes 122888 | tf_op jit(solution)/shard_map/ppermute | solution.py:525
  38.8 27.2 %copy-start = (f32[64,1024]{1,0:T(8,128)S(1)}, f32[64,1024]{1,0:T(8,128)}, u32[]{:S(2)}) copy-start(f32[64,1024]{1,0:T(8,128)} %weights_ref.1) | copy-start | bytes 786436
  38.8 27.2 %copy-start.1 = (bf16[2,256,256]{2,1,0:T(8,128)(2,1)S(1)}, bf16[2,256,256]{2,1,0:T(8,128)(2,1)}, u32[]{:S(2)}) copy-start(bf16[2,256,256]{2,1,0:T(8,128)(2,1)} %constant.5.clone.table_ref) | copy-start | bytes 786436
  38.8 27.2 %copy-start.2 = (s32[3,1024]{1,0:T(4,128)S(1)}, s32[3,1024]{1,0:T(4,128)}, u32[]{:S(2)}) copy-start(s32[3,1024]{1,0:T(4,128)} %anchors_ref.1) | copy-start | bytes 36868
  41.4 24.5 %all-to-all-start.1 = ((f32[256,1,384]{2,1,0:T(1,128)}), f32[256,1,384]{2,1,0:T(1,128)S(1)}, u32[]{:S(2)}, u32[]{:S(2)}) async-start(f32[256,1,384]{2,1,0:T(1,128)} %bitcast.4), calls=%async_computation.1 | async-start | bytes 786432 | tf_op jit(solution)/shard_map/all_to_all | solution.py:530
  47.4 12.9 %collective-permute-start.4 = (f32[24,128]{1,0:T(8,128)S(1)}, f32[24,128]{1,0:T(8,128)S(1)}, u32[]{:S(2)}, u32[]{:S(2)}) collective-permute-start(f32[24,128]{1,0:T(8,128)S(1)} %get-tuple-element.28.own_ref), channel_id=1, source_target_pairs={{0,1},{1,2},{2,3},{3,4},{4,5},{5,6},{6,7},{7,8},{8,9},{9,10},{10,1... | collective-permute-start | bytes 36872 | tf_op jit(solution)/shard_map/ppermute | solution.py:493
  49.0 11.3 %collective-permute-start.5 = (f32[24,128]{1,0:T(8,128)S(1)}, f32[24,128]{1,0:T(8,128)S(1)}, u32[]{:S(2)}, u32[]{:S(2)}) collective-permute-start(f32[24,128]{1,0:T(8,128)S(1)} %get-tuple-element.28.own_ref), channel_id=1, source_target_pairs={{0,31},{1,0},{2,1},{3,2},{4,3},{5,4},{6,5},{7,6},{8,7},{9,8},{10,9... | collective-permute-start | bytes 36872 | tf_op jit(solution)/shard_map/ppermute | solution.py:493
